TPU v7x, 32 devices: a whole 2x2x4 slice. The times are simulated.
32 devices in a mesh: sta: 8 (over z, y), day: 4 (over x, core).
Axes of the slice: x: 2, y: 2, z: 4, core: 2. Of those that a mesh axis runs over, the one named last changes fastest.
Arguments:
- solution: float32 [4, 4096, 4096], P(None, 'sta', 'day'), may hold values from -6 to 6
- residual: float32 [4, 4096, 4096], P(None, 'sta', 'day'), may hold values from -6 to 6
- direction: float32 [4, 4096, 4096], P(None, 'sta', 'day'), may hold values from -6 to 6
- observed: int32 [4096, 4096], P('sta', 'day'), may hold values 0 or 1
- coords: float32 [2, 4096], replicated, may hold values from 0 to 1
- day_features: float32 [4, 4096], replicated, may hold values from 0 to 1
- noise: float32 [4096], P('sta'), may hold values from 0.1 to 1
Outputs:
- new_solution: float32 [4, 4096, 4096], P(None, 'sta', 'day')
- new_residual: float32 [4, 4096, 4096], P(None, 'sta', 'day')
- new_direction: float32 [4, 4096, 4096], P(None, 'sta', 'day')
All inputs are finite; a program needn't handle non-finite values. No bound on the sum of `observed` on one device may be relied on, other than what follows from the above.
Results may differ from a plain program's by a relative error of at most 0.000054.
Values sent between devices are 32-bit elements; how exact they have to be, the bound alone decides.
No kernel may reach another device: no remote copies, remote signals or barrier semaphores. Data moves between devices by JAX's collectives and lax.ppermute only.
A program may use at most 192 MiB of HBM per device.

v0:
```python
import math

import jax
import jax.numpy as jnp
from jax import lax
from jax.sharding import PartitionSpec as P

STATIONS = 4096
DAYS = 4096
FEAT = 4


space_range = 0.5
time_range = 0.5


def space_apply(stacked, coords):
    nblock, slen, width = stacked.shape
    rows = math.gcd(512, STATIONS)
    scale = 2.0 / STATIONS**0.5

    def space_one_block(index):
        part = lax.dynamic_slice_in_dim(coords, index * rows, rows, 1)
        dx = part[0][:, None] - coords[0][None, :]
        dy = part[1][:, None] - coords[1][None, :]
        kern = jnp.exp(-jnp.sqrt(dx * dx + dy * dy) / space_range) * scale
        kern = kern.reshape(rows, nblock, slen)
        return jnp.einsum("ibs,bsc->ic", kern, stacked, precision=lax.Precision.HIGHEST)

    result = lax.map(space_one_block, jnp.arange(STATIONS // rows, dtype=jnp.int32))
    return result.reshape(STATIONS, width)


def time_apply(stacked, day_features):
    nblock, count, tlen = stacked.shape
    cols = math.gcd(512, DAYS)
    scale = 2.0 / DAYS**0.5

    def time_one_block(index):
        part = lax.dynamic_slice_in_dim(day_features, index * cols, cols, 1)
        total = jnp.zeros((DAYS, cols), jnp.float32)
        for feature in range(FEAT):
            diff = day_features[feature][:, None] - part[feature][None, :]
            total = total + diff * diff
        kern = (jnp.exp(-jnp.sqrt(total) / time_range) * scale).reshape(nblock, tlen, cols)
        return jnp.einsum("brt,btc->rc", stacked, kern, precision=lax.Precision.HIGHEST)

    result = lax.map(time_one_block, jnp.arange(DAYS // cols, dtype=jnp.int32))
    return jnp.transpose(result, (1, 0, 2)).reshape(count, DAYS)


def shards(solution, residual, direction, observed, coords, day_features, noise):
    n_sta = lax.axis_size("sta")
    n_day = lax.axis_size("day")
    probes, s_loc, t_loc = direction.shape
    weight = observed.astype(jnp.float32)
    masked = weight[None] * direction
    short = s_loc // n_day
    count = probes * short
    pieces = jnp.transpose(masked.reshape(probes, n_day, short, t_loc), (1, 0, 2, 3)).reshape(
        n_day, count, t_loc
    )
    day_rows = lax.all_to_all(pieces, "day", split_axis=0, concat_axis=0, tiled=True)
    inner = time_apply(day_rows, day_features)
    total = n_sta * n_day
    narrow = DAYS // total
    sending = jnp.transpose(inner.reshape(count, total, narrow), (1, 0, 2))
    columns = lax.all_to_all(sending, ("sta", "day"), split_axis=0, concat_axis=0, tiled=True)
    columns = jnp.transpose(columns.reshape(total, probes, short, narrow), (0, 2, 1, 3)).reshape(
        total, short, probes * narrow
    )
    smooth = space_apply(columns, coords).reshape(total, short, probes * narrow)
    returned = lax.all_to_all(smooth, ("sta", "day"), split_axis=0, concat_axis=0, tiled=True)
    regroup = returned.reshape(n_day, n_sta, short, probes * narrow)
    settled = lax.all_to_all(regroup, "day", split_axis=0, concat_axis=0, tiled=True)
    settled = settled.reshape(n_day, n_sta, short, probes, narrow)
    outer = jnp.transpose(settled, (3, 0, 2, 1, 4)).reshape(probes, s_loc, t_loc)
    image = weight[None] * outer + noise[None, :, None] * direction
    local_norm = jnp.sum(residual * residual, axis=(1, 2))
    local_curve = jnp.sum(direction * image, axis=(1, 2))
    norm_now, curve = lax.psum((local_norm, local_curve), ("sta", "day"))
    alpha = norm_now / curve
    new_residual = residual - alpha[:, None, None] * image
    norm_next = lax.psum(jnp.sum(new_residual * new_residual, axis=(1, 2)), ("sta", "day"))
    new_solution = solution + alpha[:, None, None] * direction
    beta = (norm_next / norm_now)[:, None, None]
    new_direction = new_residual + beta * direction
    return (new_solution, new_residual, new_direction)


def solution(mesh):
    in_specs = (
        P(None, "sta", "day"),
        P(None, "sta", "day"),
        P(None, "sta", "day"),
        P("sta", "day"),
        P(),
        P(),
        P("sta"),
    )
    out_specs = (P(None, "sta", "day"), P(None, "sta", "day"), P(None, "sta", "day"))
    return jax.shard_map(shards, mesh=mesh, in_specs=in_specs, out_specs=out_specs, check_vma=False)
```

profile of v0, /device:TPU:0, one launch (start us, length us, event | category | flops | bytes accessed | tf_op | source)
XLA Modules:
  0.0 1203.9 jit_solution(17321370272689405766)
XLA Ops:
  0.6 1.9 convert_element_type.3
  2.5 5.5 broadcast_multiply_fusion
  8.0 4.4 copy.15
  12.4 5.8 all-to-all-start
  18.2 93.8 %all-to-all-done = f32[4,512,1024]{2,1,0:T(8,128)} async-done(((f32[4,512,1024]{2,1,0:T(8,128)}), f32[4,512,1024]{2,1,0:T(8,128)}, u32[]{:S(2)}, u32[]{:S(2)}) %all-to-all-start) | async-done | bytes 8388640 | tf_op jit(solution)/shard_map/all_to_all | solution.py:63
  112.0 234.7 %while.20 = (s32[]{:T(128)}, f32[8,512,512]{1,2,0:T(8,128)}, f32[4,4096]{1,0:T(4,128)S(1)}, s32[8]{0:T(128)S(1)}, f32[4,512,1024]{2,1,0:T(8,128)}, /*index=5*/s3...) while((s32[]{:T(128)}, f32[8,512,512]{1,2,0:T(8,128)}, f32[4,4096]{1,0:T(4,128)S(1)}, ...), condition=%wide.region_3.4_spmd, body=%wide.region_2.3_spmd.sunk | while | flops 12914262016 | bytes 9790179 | solution.py:48
  112.2 0.6 dynamic_slice.15
  113.5 0.2 slice_reduce_fusion.5
  113.7 27.7 %fusion.72 = f32[8,512,512]{1,2,0:T(8,128)} fusion(f32[8,512,512]{1,2,0:T(8,128)} %get-tuple-element.215, s32[]{:T(128)} %get-tuple-element.214, f32[4,512,1024]{2,1,0:T(8,128)} %get-tuple-element.230, f32[512]{0:T(512)S(1)} %bitcast.85, f32[4,1024]{1,0:T(4,128)S(1)} %sub.292, f32[512]{0:T(512)S(1)} %bitcast.83, f32[4,1024]{1,0:T(4,128)S(1)} %sub.293, ...), kind=kOutput, calls=%fused_computation.50.clone.1 | convolution fusion | flops 12914262016 | bytes 9511424 | tf_op jit(solution)/shard_map/while/body/eval_jaxpr/brt,btc->rc/dot_general | solution.py:46
  141.5 0.6 dynamic_slice.15
  142.8 0.2 slice_reduce_fusion.5
  143.0 27.7 %fusion.72 = f32[8,512,512]{1,2,0:T(8,128)} fusion(f32[8,512,512]{1,2,0:T(8,128)} %get-tuple-element.215, s32[]{:T(128)} %get-tuple-element.214, f32[4,512,1024]{2,1,0:T(8,128)} %get-tuple-element.230, f32[512]{0:T(512)S(1)} %bitcast.85, f32[4,1024]{1,0:T(4,128)S(1)} %sub.292, f32[512]{0:T(512)S(1)} %bitcast.83, f32[4,1024]{1,0:T(4,128)S(1)} %sub.293, ...), kind=kOutput, calls=%fused_computation.50.clone.1 | convolution fusion | flops 12914262016 | bytes 9511424 | tf_op jit(solution)/shard_map/while/body/eval_jaxpr/brt,btc->rc/dot_general | solution.py:46
  170.7 0.6 dynamic_slice.15
  172.1 0.2 slice_reduce_fusion.5
  172.3 27.7 %fusion.72 = f32[8,512,512]{1,2,0:T(8,128)} fusion(f32[8,512,512]{1,2,0:T(8,128)} %get-tuple-element.215, s32[]{:T(128)} %get-tuple-element.214, f32[4,512,1024]{2,1,0:T(8,128)} %get-tuple-element.230, f32[512]{0:T(512)S(1)} %bitcast.85, f32[4,1024]{1,0:T(4,128)S(1)} %sub.292, f32[512]{0:T(512)S(1)} %bitcast.83, f32[4,1024]{1,0:T(4,128)S(1)} %sub.293, ...), kind=kOutput, calls=%fused_computation.50.clone.1 | convolution fusion | flops 12914262016 | bytes 9511424 | tf_op jit(solution)/shard_map/while/body/eval_jaxpr/brt,btc->rc/dot_general | solution.py:46
  200.0 0.6 dynamic_slice.15
  201.4 0.2 slice_reduce_fusion.5
  201.6 27.7 %fusion.72 = f32[8,512,512]{1,2,0:T(8,128)} fusion(f32[8,512,512]{1,2,0:T(8,128)} %get-tuple-element.215, s32[]{:T(128)} %get-tuple-element.214, f32[4,512,1024]{2,1,0:T(8,128)} %get-tuple-element.230, f32[512]{0:T(512)S(1)} %bitcast.85, f32[4,1024]{1,0:T(4,128)S(1)} %sub.292, f32[512]{0:T(512)S(1)} %bitcast.83, f32[4,1024]{1,0:T(4,128)S(1)} %sub.293, ...), kind=kOutput, calls=%fused_computation.50.clone.1 | convolution fusion | flops 12914262016 | bytes 9511424 | tf_op jit(solution)/shard_map/while/body/eval_jaxpr/brt,btc->rc/dot_general | solution.py:46
  229.3 0.6 dynamic_slice.15
  230.7 0.2 slice_reduce_fusion.5
  230.9 27.7 %fusion.72 = f32[8,512,512]{1,2,0:T(8,128)} fusion(f32[8,512,512]{1,2,0:T(8,128)} %get-tuple-element.215, s32[]{:T(128)} %get-tuple-element.214, f32[4,512,1024]{2,1,0:T(8,128)} %get-tuple-element.230, f32[512]{0:T(512)S(1)} %bitcast.85, f32[4,1024]{1,0:T(4,128)S(1)} %sub.292, f32[512]{0:T(512)S(1)} %bitcast.83, f32[4,1024]{1,0:T(4,128)S(1)} %sub.293, ...), kind=kOutput, calls=%fused_computation.50.clone.1 | convolution fusion | flops 12914262016 | bytes 9511424 | tf_op jit(solution)/shard_map/while/body/eval_jaxpr/brt,btc->rc/dot_general | solution.py:46
  258.6 0.6 dynamic_slice.15
  260.0 0.2 slice_reduce_fusion.5
  260.2 27.7 %fusion.72 = f32[8,512,512]{1,2,0:T(8,128)} fusion(f32[8,512,512]{1,2,0:T(8,128)} %get-tuple-element.215, s32[]{:T(128)} %get-tuple-element.214, f32[4,512,1024]{2,1,0:T(8,128)} %get-tuple-element.230, f32[512]{0:T(512)S(1)} %bitcast.85, f32[4,1024]{1,0:T(4,128)S(1)} %sub.292, f32[512]{0:T(512)S(1)} %bitcast.83, f32[4,1024]{1,0:T(4,128)S(1)} %sub.293, ...), kind=kOutput, calls=%fused_computation.50.clone.1 | convolution fusion | flops 12914262016 | bytes 9511424 | tf_op jit(solution)/shard_map/while/body/eval_jaxpr/brt,btc->rc/dot_general | solution.py:46
  287.9 0.6 dynamic_slice.15
  289.2 0.2 slice_reduce_fusion.5
  289.5 27.7 %fusion.72 = f32[8,512,512]{1,2,0:T(8,128)} fusion(f32[8,512,512]{1,2,0:T(8,128)} %get-tuple-element.215, s32[]{:T(128)} %get-tuple-element.214, f32[4,512,1024]{2,1,0:T(8,128)} %get-tuple-element.230, f32[512]{0:T(512)S(1)} %bitcast.85, f32[4,1024]{1,0:T(4,128)S(1)} %sub.292, f32[512]{0:T(512)S(1)} %bitcast.83, f32[4,1024]{1,0:T(4,128)S(1)} %sub.293, ...), kind=kOutput, calls=%fused_computation.50.clone.1 | convolution fusion | flops 12914262016 | bytes 9511424 | tf_op jit(solution)/shard_map/while/body/eval_jaxpr/brt,btc->rc/dot_general | solution.py:46
  317.2 0.6 dynamic_slice.15
  318.5 0.2 slice_reduce_fusion.5
  318.8 27.7 %fusion.72 = f32[8,512,512]{1,2,0:T(8,128)} fusion(f32[8,512,512]{1,2,0:T(8,128)} %get-tuple-element.215, s32[]{:T(128)} %get-tuple-element.214, f32[4,512,1024]{2,1,0:T(8,128)} %get-tuple-element.230, f32[512]{0:T(512)S(1)} %bitcast.85, f32[4,1024]{1,0:T(4,128)S(1)} %sub.292, f32[512]{0:T(512)S(1)} %bitcast.83, f32[4,1024]{1,0:T(4,128)S(1)} %sub.293, ...), kind=kOutput, calls=%fused_computation.50.clone.1 | convolution fusion | flops 12914262016 | bytes 9511424 | tf_op jit(solution)/shard_map/while/body/eval_jaxpr/brt,btc->rc/dot_general | solution.py:46
  346.7 5.9 all-to-all-start.1
  352.6 186.0 %all-to-all-done.1 = f32[32,512,128]{1,2,0:T(8,128)} async-done(((f32[32,512,128]{1,2,0:T(8,128)}), f32[32,512,128]{1,2,0:T(8,128)}, u32[]{:S(2)}, u32[]{:S(2)}) %all-to-all-start.1) | async-done | bytes 8388640 | tf_op jit(solution)/shard_map/all_to_all | solution.py:68
  538.7 8.9 copy.17
  547.6 9.0 copy.18
  556.6 9.0 copy.19
  565.5 207.1 %while.21 = (s32[]{:T(128)}, f32[8,512,512]{2,1,0:T(8,128)}, s32[8]{0:T(128)S(1)}, f32[2,4096]{1,0:T(2,128)S(1)}, f32[32,128,512]{2,1,0:T(8,128)}, /*index=5*/s32[]{:T(128)}, s32[1]{0:T(128)}, s32[]{:T(128)}, s32[]{:T(128)}, s32[]{}) while((s32[]{:T(128)}, f32[8,512,512]{2,1,0:T(8,128)}, s32[8]{0:T(128)S(1)}, f32[2,4096]{1,0:T(2,128)S(1)}, ...), condition=%wide.region_5.6_spmd, body=%wide.region_4.5_spmd.sunk | while | flops 12901679104 | bytes 9548467 | solution.py:30
  565.5 0.6 dynamic_slice.16
  566.9 24.5 %fusion.76 = f32[8,512,512]{2,1,0:T(8,128)} fusion(f32[8,512,512]{2,1,0:T(8,128)} %get-tuple-element.249, s32[]{:T(128)} %get-tuple-element.248, f32[32,128,512]{2,1,0:T(8,128)} %get-tuple-element.262, f32[32,128]{1,0:T(8,128)S(1)} %bitcast.81, f32[512]{0:T(512)S(1)} %bitcast.87, f32[32,128]{1,0:T(8,128)S(1)} %bitcast.80, f32[512]{0:T(512)S(1)} %bitcast.86), kind=kOutput, calls=%fused_computation.18.clone.1 | convolution fusion | flops 12901679104 | bytes 9474560 | tf_op jit(solution)/shard_map/while/body/eval_jaxpr/ibs,bsc->ic/dot_general | solution.py:28
  591.4 0.6 dynamic_slice.16
  592.8 24.5 %fusion.76 = f32[8,512,512]{2,1,0:T(8,128)} fusion(f32[8,512,512]{2,1,0:T(8,128)} %get-tuple-element.249, s32[]{:T(128)} %get-tuple-element.248, f32[32,128,512]{2,1,0:T(8,128)} %get-tuple-element.262, f32[32,128]{1,0:T(8,128)S(1)} %bitcast.81, f32[512]{0:T(512)S(1)} %bitcast.87, f32[32,128]{1,0:T(8,128)S(1)} %bitcast.80, f32[512]{0:T(512)S(1)} %bitcast.86), kind=kOutput, calls=%fused_computation.18.clone.1 | convolution fusion | flops 12901679104 | bytes 9474560 | tf_op jit(solution)/shard_map/while/body/eval_jaxpr/ibs,bsc->ic/dot_general | solution.py:28
  617.3 0.6 dynamic_slice.16
  618.6 24.5 %fusion.76 = f32[8,512,512]{2,1,0:T(8,128)} fusion(f32[8,512,512]{2,1,0:T(8,128)} %get-tuple-element.249, s32[]{:T(128)} %get-tuple-element.248, f32[32,128,512]{2,1,0:T(8,128)} %get-tuple-element.262, f32[32,128]{1,0:T(8,128)S(1)} %bitcast.81, f32[512]{0:T(512)S(1)} %bitcast.87, f32[32,128]{1,0:T(8,128)S(1)} %bitcast.80, f32[512]{0:T(512)S(1)} %bitcast.86), kind=kOutput, calls=%fused_computation.18.clone.1 | convolution fusion | flops 12901679104 | bytes 9474560 | tf_op jit(solution)/shard_map/while/body/eval_jaxpr/ibs,bsc->ic/dot_general | solution.py:28
  643.2 0.6 dynamic_slice.16
  644.5 24.5 %fusion.76 = f32[8,512,512]{2,1,0:T(8,128)} fusion(f32[8,512,512]{2,1,0:T(8,128)} %get-tuple-element.249, s32[]{:T(128)} %get-tuple-element.248, f32[32,128,512]{2,1,0:T(8,128)} %get-tuple-element.262, f32[32,128]{1,0:T(8,128)S(1)} %bitcast.81, f32[512]{0:T(512)S(1)} %bitcast.87, f32[32,128]{1,0:T(8,128)S(1)} %bitcast.80, f32[512]{0:T(512)S(1)} %bitcast.86), kind=kOutput, calls=%fused_computation.18.clone.1 | convolution fusion | flops 12901679104 | bytes 9474560 | tf_op jit(solution)/shard_map/while/body/eval_jaxpr/ibs,bsc->ic/dot_general | solution.py:28
  669.1 0.6 dynamic_slice.16
  670.4 24.5 %fusion.76 = f32[8,512,512]{2,1,0:T(8,128)} fusion(f32[8,512,512]{2,1,0:T(8,128)} %get-tuple-element.249, s32[]{:T(128)} %get-tuple-element.248, f32[32,128,512]{2,1,0:T(8,128)} %get-tuple-element.262, f32[32,128]{1,0:T(8,128)S(1)} %bitcast.81, f32[512]{0:T(512)S(1)} %bitcast.87, f32[32,128]{1,0:T(8,128)S(1)} %bitcast.80, f32[512]{0:T(512)S(1)} %bitcast.86), kind=kOutput, calls=%fused_computation.18.clone.1 | convolution fusion | flops 12901679104 | bytes 9474560 | tf_op jit(solution)/shard_map/while/body/eval_jaxpr/ibs,bsc->ic/dot_general | solution.py:28
  694.9 0.6 dynamic_slice.16
  696.3 24.5 %fusion.76 = f32[8,512,512]{2,1,0:T(8,128)} fusion(f32[8,512,512]{2,1,0:T(8,128)} %get-tuple-element.249, s32[]{:T(128)} %get-tuple-element.248, f32[32,128,512]{2,1,0:T(8,128)} %get-tuple-element.262, f32[32,128]{1,0:T(8,128)S(1)} %bitcast.81, f32[512]{0:T(512)S(1)} %bitcast.87, f32[32,128]{1,0:T(8,128)S(1)} %bitcast.80, f32[512]{0:T(512)S(1)} %bitcast.86), kind=kOutput, calls=%fused_computation.18.clone.1 | convolution fusion | flops 12901679104 | bytes 9474560 | tf_op jit(solution)/shard_map/while/body/eval_jaxpr/ibs,bsc->ic/dot_general | solution.py:28
  720.8 0.6 dynamic_slice.16
  722.2 24.5 %fusion.76 = f32[8,512,512]{2,1,0:T(8,128)} fusion(f32[8,512,512]{2,1,0:T(8,128)} %get-tuple-element.249, s32[]{:T(128)} %get-tuple-element.248, f32[32,128,512]{2,1,0:T(8,128)} %get-tuple-element.262, f32[32,128]{1,0:T(8,128)S(1)} %bitcast.81, f32[512]{0:T(512)S(1)} %bitcast.87, f32[32,128]{1,0:T(8,128)S(1)} %bitcast.80, f32[512]{0:T(512)S(1)} %bitcast.86), kind=kOutput, calls=%fused_computation.18.clone.1 | convolution fusion | flops 12901679104 | bytes 9474560 | tf_op jit(solution)/shard_map/while/body/eval_jaxpr/ibs,bsc->ic/dot_general | solution.py:28
  746.7 0.6 dynamic_slice.16
  748.1 24.5 %fusion.76 = f32[8,512,512]{2,1,0:T(8,128)} fusion(f32[8,512,512]{2,1,0:T(8,128)} %get-tuple-element.249, s32[]{:T(128)} %get-tuple-element.248, f32[32,128,512]{2,1,0:T(8,128)} %get-tuple-element.262, f32[32,128]{1,0:T(8,128)S(1)} %bitcast.81, f32[512]{0:T(512)S(1)} %bitcast.87, f32[32,128]{1,0:T(8,128)S(1)} %bitcast.80, f32[512]{0:T(512)S(1)} %bitcast.86), kind=kOutput, calls=%fused_computation.18.clone.1 | convolution fusion | flops 12901679104 | bytes 9474560 | tf_op jit(solution)/shard_map/while/body/eval_jaxpr/ibs,bsc->ic/dot_general | solution.py:28
  772.6 8.9 copy.20
  781.5 187.2 %all_to_all.20 = f32[32,128,512]{1,2,0:T(8,128)} all-to-all(f32[32,128,512]{1,2,0:T(8,128)} %copy.20), channel_id=1, replica_groups=mesh['sta'=8,'day'=4] {'sta','day'}, dimensions={0} | all-to-all | bytes 16777216 | tf_op jit(solution)/shard_map/all_to_all | solution.py:73
  968.7 5.9 all-to-all-start.3
  974.6 4.2 multiply_reduce_fusion.2
  978.8 88.9 %all-to-all-done.3 = f32[4,8,128,512]{2,3,1,0:T(8,128)} async-done(((f32[4,8,128,512]{2,3,1,0:T(8,128)}), f32[4,8,128,512]{2,3,1,0:T(8,128)}, u32[]{:S(2)}, u32[]{:S(2)}) %all-to-all-start.3) | async-done | bytes 8388640 | tf_op jit(solution)/shard_map/all_to_all | solution.py:75
  1067.8 9.9 copy.21
  1077.7 9.4 reshape.109
  1087.1 7.0 multiply_reduce_fusion.1
  1094.1 38.4 %all-reduce = (f32[4]{0:T(128)S(1)}, f32[4]{0:T(128)S(1)}) all-reduce(f32[4]{0:T(128)S(1)} %multiply_reduce_fusion.2, f32[4]{0:T(128)S(1)} %multiply_reduce_fusion.1), channel_id=1, replica_groups=mesh['sta'=8,'day'=4] {'sta','day'}, use_global_device_ids=true, to_apply=%region_1.2 | all-reduce | flops 8 | bytes 64 | tf_op jit(solution)/shard_map/psum | solution.py:81
  1132.5 18.0 %multiply_reduce_fusion = (f32[4]{0:T(128)S(1)}, f32[4,512,1024]{2,1,0:T(8,128)}, f32[4,512,1024]{2,1,0:T(8,128)}) fusion(f32[4,512,1024]{2,1,0:T(8,128)} %param.12, f32[4,512,1024]{2,1,0:T(8,128)} %param.13, f32[512]{0:T(512)S(1)} %copy-done.4, f32[4,512,1024]{2,1,0:T(8,128)} %reshape.109, f32[512,1024]{1,0:T(8,128)S(1)} %copy-done.1, f32[4]{0:T(128)S(1)} %div.12, ...), kind=kLoop, calls=%fused_computation.59 | loop fusion | flops 18874364 | bytes 52430880 | tf_op jit(solution)/shard_map/reduce_sum | solution.py:84
  1150.5 40.7 %psum.23 = f32[4]{0:T(128)S(1)} all-reduce(f32[4]{0:T(128)S(1)} %get-tuple-element.105), channel_id=1, replica_groups=mesh['sta'=8,'day'=4] {'sta','day'}, use_global_device_ids=true, to_apply=%region_9.10 | all-reduce | flops 4 | bytes 32 | tf_op jit(solution)/shard_map/psum | solution.py:84
  1191.2 12.3 %multiply_add_fusion = f32[4,512,1024]{2,1,0:T(8,128)} fusion(f32[4,512,1024]{2,1,0:T(8,128)} %get-tuple-element.106, f32[4,512,1024]{2,1,0:T(8,128)} %param.13, f32[4]{0:T(128)S(1)} %div.13), kind=kLoop, calls=%fused_computation.58 | loop fusion | flops 4194304 | bytes 25165840 | tf_op jit(solution)/shard_map/add | solution.py:87
  (72 shorter events, 2.0 us)
Async XLA Ops:
  2.5 5.5 copy-start
  12.4 99.6 %copy-start.2 = (f32[4,4096]{1,0:T(4,128)S(1)}, f32[4,4096]{1,0:T(4,128)}, u32[]{:S(2)}) copy-start(f32[4,4096]{1,0:T(4,128)} %param.16) | copy-start | bytes 196612
  12.4 99.6 %all-to-all-start = ((f32[4,512,1024]{2,1,0:T(8,128)}), f32[4,512,1024]{2,1,0:T(8,128)}, u32[]{:S(2)}, u32[]{:S(2)}) async-start(f32[4,512,1024]{2,1,0:T(8,128)} %bitcast.73), calls=%async_computation | async-start | bytes 16777216 | tf_op jit(solution)/shard_map/all_to_all | solution.py:63
  346.7 192.0 %all-to-all-start.1 = ((f32[32,512,128]{1,2,0:T(8,128)}), f32[32,512,128]{1,2,0:T(8,128)}, u32[]{:S(2)}, u32[]{:S(2)}) async-start(f32[32,512,128]{1,2,0:T(8,128)} %bitcast.79), calls=%async_computation.1 | async-start | bytes 16777216 | tf_op jit(solution)/shard_map/all_to_all | solution.py:68
  556.6 9.0 copy-start.3
  968.7 99.1 %all-to-all-start.3 = ((f32[4,8,128,512]{2,3,1,0:T(8,128)}), f32[4,8,128,512]{2,3,1,0:T(8,128)}, u32[]{:S(2)}, u32[]{:S(2)}) async-start(f32[4,8,128,512]{2,3,1,0:T(8,128)} %bitcast.74), calls=%async_computation.3 | async-start | bytes 16777216 | tf_op jit(solution)/shard_map/all_to_all | solution.py:75
  1077.7 9.4 copy-start.1
  1077.7 9.4 copy-start.4
where the time goes:
time: 1210 us; the launch traced here: 1200 us
  matrix products  418 us (35%)
  waiting for transfers between devices  369 us (30%)
  blocking collectives  266 us (22%)
  local copies, waits for them, and re-layouts  72.2 us (6%)
  other arithmetic  48.8 us (4%)
  starting transfers between devices  17.6 us (1%)
    dot_general x8, matrix products, time_one_block(): jnp.einsum('brt,btc->rc', stacked, kern, precision=lax.Precision.HIGHEST)  222 us
    dot_general x8, matrix products, space_one_block(): jnp.einsum('ibs,bsc->ic', kern, stacked, precision=lax.Precision.HIGHEST)  196 us
    all_to_all x1, blocking collectives, shards(): lax.all_to_all(smooth, ('sta', 'day'), split_axis=0, concat_axis=0, tiled...  187 us
    all_to_all x1, waiting for transfers between devices, shards(): lax.all_to_all(sending, ('sta', 'day'), split_axis=0, concat_axis=0, tile...  186 us
    all_to_all x1, waiting for transfers between devices, shards(): lax.all_to_all(pieces, 'day', split_axis=0, concat_axis=0, tiled=True)  93.8 us
    all_to_all x1, waiting for transfers between devices, shards(): lax.all_to_all(regroup, 'day', split_axis=0, concat_axis=0, tiled=True)  88.9 us
    psum x1, blocking collectives, shards(): lax.psum(jnp.sum(new_residual * new_residual, axis=(1, 2)), ('sta', 'day'))  40.7 us
    psum x1, blocking collectives, shards(): norm_now, curve = lax.psum((local_norm, local_curve), ('sta', 'day'))  38.4 us
  transfers between devices with their start and end apart: 3, of which 3 were waited for; matrix products, arithmetic and copies ran while one was open for 0% of the time, Pallas kernels for 0%

commit v1 on v0

v1 whole, which is shorter than its diff:
```python
import functools
import math

import jax
import jax.numpy as jnp
from jax import lax
from jax.experimental import pallas as pl
from jax.experimental.pallas import tpu as pltpu
from jax.sharding import PartitionSpec as P

STATIONS = 4096
DAYS = 4096
FEAT = 4

space_range = 0.5
time_range = 0.5

MIB = 1 << 20


def params(limit):
    return pltpu.CompilerParams(vmem_limit_bytes=limit * MIB)


def mask_kernel(observed, direction, out):
    out[0] = observed[...].astype(jnp.float32) * direction[0]


def mask_call(observed, direction, probe, parts):
    _, s_loc, t_loc = direction.shape
    width = t_loc // parts
    return pl.pallas_call(
        mask_kernel,
        grid=(parts,),
        in_specs=[
            pl.BlockSpec((s_loc, width), lambda j: (0, j)),
            pl.BlockSpec((1, s_loc, width), lambda j: (probe, 0, j)),
        ],
        out_specs=pl.BlockSpec((1, s_loc, width), lambda j: (j, 0, 0)),
        out_shape=jax.ShapeDtypeStruct((parts, s_loc, width), jnp.float32),
        compiler_params=params(24),
        cost_estimate=pl.CostEstimate(flops=s_loc * t_loc, bytes_accessed=12 * s_loc * t_loc, transcendentals=0),
        name="mask",
    )(observed, direction)


def entries_kernel(features, slope, shift, rows_order, cols_order, rows, cols, high, low):
    step = 32

    @pl.loop(0, rows.shape[0] // step)
    def _(index):
        at = pl.ds(pl.multiple_of(index * step, step), step)
        mine = rows[at, :]
        total = None
        for feature in range(features):
            diff = mine[:, feature : feature + 1] - cols[feature : feature + 1, :]
            total = diff * diff if total is None else total + diff * diff
        dist = total * lax.rsqrt(jnp.maximum(total, 1e-37))
        value = jnp.exp2(dist * slope + shift)
        top = value.astype(jnp.bfloat16)
        high[at, :] = top
        low[at, :] = (value - top.astype(jnp.float32)).astype(jnp.bfloat16)


def entries_call(table, rows_order, cols_order, tile, reach, order, name):
    features = table.shape[0]
    n_rows, n_cols = rows_order.shape[0], cols_order.shape[0]
    shape = (n_rows * tile, n_cols * tile)
    count = shape[0] * shape[1]
    out_spec = pl.BlockSpec((tile, tile), lambda i, j, ro, co: (i, j))
    slope = -1.0 / (reach * math.log(2.0))
    shift = math.log2(2.0 / order**0.5)
    return pl.pallas_call(
        functools.partial(entries_kernel, features, slope, shift),
        grid_spec=pltpu.PrefetchScalarGridSpec(
            num_scalar_prefetch=2,
            grid=(n_rows, n_cols),
            in_specs=[
                pl.BlockSpec((tile, features), lambda i, j, ro, co: (ro[i], 0)),
                pl.BlockSpec((features, tile), lambda i, j, ro, co: (0, co[j])),
            ],
            out_specs=[out_spec, out_spec],
        ),
        out_shape=[jax.ShapeDtypeStruct(shape, jnp.bfloat16)] * 2,
        compiler_params=params(24),
        cost_estimate=pl.CostEstimate(flops=16 * count, bytes_accessed=4 * count, transcendentals=2 * count),
        name=name,
    )(rows_order, cols_order, table.T, table)


def split(value):
    top = value.astype(jnp.bfloat16)
    return top, (value - top.astype(jnp.float32)).astype(jnp.bfloat16)


def dot(a, b):
    return jnp.dot(a, b, preferred_element_type=jnp.float32)


def space_kernel(count, *refs):
    cells = refs[:count]
    high, low, out, cells_high, cells_low = refs[count:]
    blocks, s_loc, _ = cells[0].shape

    @pl.when(pl.program_id(0) == 0)
    def _():
        for k in range(count):
            for b in range(blocks):
                at = pl.ds((k * blocks + b) * s_loc, s_loc)
                cells_high[at, :], cells_low[at, :] = split(cells[k][b])

    total = dot(high[...], cells_high[...])
    total += dot(high[...], cells_low[...])
    total += dot(low[...], cells_high[...])
    out[0] = total


def space_call(cells, high, low):
    blocks, s_loc, width = cells[0].shape
    stations = high.shape[1]
    whole = pl.BlockSpec((blocks, s_loc, width), lambda i: (0, 0, 0))
    matrix = pl.BlockSpec((s_loc, stations), lambda i: (i, 0))
    return pl.pallas_call(
        functools.partial(space_kernel, len(cells)),
        grid=(blocks,),
        in_specs=[whole] * len(cells) + [matrix, matrix],
        out_specs=pl.BlockSpec((1, s_loc, width), lambda i: (i, 0, 0)),
        out_shape=jax.ShapeDtypeStruct((blocks, s_loc, width), jnp.float32),
        scratch_shapes=[pltpu.VMEM((stations, width), jnp.bfloat16)] * 2,
        compiler_params=params(48),
        cost_estimate=pl.CostEstimate(
            flops=6 * blocks * s_loc * stations * width,
            bytes_accessed=4 * blocks * s_loc * stations + 8 * stations * width,
            transcendentals=0,
        ),
        name="space",
    )(*cells, high, low)


def time_kernel(count, *refs):
    cells = refs[:count]
    high, low, out, cells_high, cells_low = refs[count:]
    blocks, _, width = cells[0].shape

    @pl.when(pl.program_id(0) == 0)
    def _():
        for k in range(count):
            for b in range(blocks):
                at = pl.ds((k * blocks + b) * width, width)
                cells_high[:, at], cells_low[:, at] = split(cells[k][b])

    total = dot(cells_high[...], high[...])
    total += dot(cells_low[...], high[...])
    total += dot(cells_high[...], low[...])
    out[0] = total


def time_call(cells, high, low):
    blocks, s_loc, width = cells[0].shape
    days = high.shape[0]
    whole = pl.BlockSpec((blocks, s_loc, width), lambda i: (0, 0, 0))
    matrix = pl.BlockSpec((days, width), lambda i: (0, i))
    return pl.pallas_call(
        functools.partial(time_kernel, len(cells)),
        grid=(blocks,),
        in_specs=[whole] * len(cells) + [matrix, matrix],
        out_specs=pl.BlockSpec((1, s_loc, width), lambda i: (i, 0, 0)),
        out_shape=jax.ShapeDtypeStruct((blocks, s_loc, width), jnp.float32),
        scratch_shapes=[pltpu.VMEM((s_loc, days), jnp.bfloat16)] * 2,
        compiler_params=params(48),
        cost_estimate=pl.CostEstimate(
            flops=6 * blocks * s_loc * days * width,
            bytes_accessed=4 * blocks * width * days + 8 * days * s_loc,
            transcendentals=0,
        ),
        name="time",
    )(*cells, high, low)


def sums_kernel(observed, noise, residual, direction, outer, out, total):
    step = pl.program_id(0)

    @pl.when(step == 0)
    def _():
        total[...] = jnp.zeros_like(total)

    res = residual[0]
    way = direction[0]
    image = observed[...].astype(jnp.float32) * outer[0] + noise[...] * way
    for row, product in enumerate((res * res, way * image, res * image, image * image)):
        total[row : row + 1, :] += jnp.sum(product, axis=0, keepdims=True)

    @pl.when(step == pl.num_programs(0) - 1)
    def _():
        out[...] = jnp.broadcast_to(jnp.sum(total[...], axis=1, keepdims=True), out.shape)


def sums_call(observed, noise, residual, direction, outer, probe):
    parts, s_loc, width = outer.shape
    column = pl.BlockSpec((1, s_loc, width), lambda j: (probe, 0, j))
    return pl.pallas_call(
        sums_kernel,
        grid=(parts,),
        in_specs=[
            pl.BlockSpec((s_loc, width), lambda j: (0, j)),
            pl.BlockSpec((s_loc, 1), lambda j: (0, 0)),
            column,
            column,
            pl.BlockSpec((1, s_loc, width), lambda j: (j, 0, 0)),
        ],
        out_specs=pl.BlockSpec((8, 128), lambda j: (0, 0)),
        out_shape=jax.ShapeDtypeStruct((8, 128), jnp.float32),
        scratch_shapes=[pltpu.VMEM((8, width), jnp.float32)],
        compiler_params=params(32),
        cost_estimate=pl.CostEstimate(
            flops=12 * parts * s_loc * width, bytes_accessed=16 * parts * s_loc * width, transcendentals=0
        ),
        name="sums",
    )(observed, noise, residual, direction, outer)


def update_kernel(row, parts, observed, noise, solution, residual, direction, outer, *refs):
    new_solution, new_residual, new_direction = refs[-3:]
    totals = jnp.sum(parts[:, row * 8 : row * 8 + 8, :], axis=0)
    rr, pap, cross, square = (totals[k : k + 1, :1] for k in range(4))
    alpha = rr / pap
    rr_next = rr + alpha * (alpha * square - 2.0 * cross)
    beta = rr_next / rr
    way = direction[0]
    image = observed[...].astype(jnp.float32) * outer[0] + noise[...] * way
    fresh = residual[0] - alpha * image
    new_solution[0] = solution[0] + alpha * way
    new_residual[0] = fresh
    new_direction[0] = fresh + beta * way


def update_call(stats, row, observed, noise, solution, residual, direction, outer, probe, earlier):
    parts, s_loc, width = outer.shape
    column = pl.BlockSpec((1, s_loc, width), lambda j: (probe, 0, j))
    shape = jax.ShapeDtypeStruct(direction.shape, jnp.float32)
    return pl.pallas_call(
        functools.partial(update_kernel, row),
        grid=(parts,),
        in_specs=[
            pl.BlockSpec(stats.shape, lambda j: (0, 0, 0)),
            pl.BlockSpec((s_loc, width), lambda j: (0, j)),
            pl.BlockSpec((s_loc, 1), lambda j: (0, 0)),
            column,
            column,
            column,
            pl.BlockSpec((1, s_loc, width), lambda j: (j, 0, 0)),
        ]
        + [pl.BlockSpec(memory_space=pl.ANY)] * len(earlier),
        out_specs=[column] * 3,
        out_shape=[shape] * 3,
        input_output_aliases={7 + k: k for k in range(len(earlier))},
        compiler_params=params(40),
        cost_estimate=pl.CostEstimate(
            flops=12 * parts * s_loc * width, bytes_accessed=32 * parts * s_loc * width, transcendentals=0
        ),
        name="update",
    )(stats, observed, noise, solution, residual, direction, outer, *earlier)


def shards(solution, residual, direction, observed, coords, day_features, noise):
    n_sta = lax.axis_size("sta")
    n_day = lax.axis_size("day")
    probes, s_loc, t_loc = direction.shape
    n_z = math.gcd(n_sta, 4)
    n_y = n_sta // n_z
    n_core = math.gcd(n_day, 2)
    n_x = n_day // n_core
    sta = lax.axis_index("sta")
    day = lax.axis_index("day")
    z_groups = [[z * n_y + y for z in range(n_z)] for y in range(n_y)]

    def over_z(pieces):
        return lax.all_to_all(pieces, "sta", 0, 0, axis_index_groups=z_groups, tiled=True)

    def over_y(cells):
        found = [cells]
        for k in range(1, n_y):
            pairs = [(z * n_y + y, z * n_y + (y + k) % n_y) for z in range(n_z) for y in range(n_y)]
            found.append(lax.ppermute(cells, "sta", pairs))
        return found

    def over_day(cells):
        found = []
        swap = [(j, j - j % n_core + (j + 1) % n_core) for j in range(n_day)]
        for k in range(n_x):
            pairs = [(x * n_core + c, (x + k) % n_x * n_core + c) for x in range(n_x) for c in range(n_core)]
            here = lax.ppermute(cells, "day", pairs) if k else cells
            found.append(here)
            if n_core > 1:
                found.append(lax.ppermute(here, "day", swap))
        return found

    def over_all(block):
        many = jnp.broadcast_to(block[None], (n_sta * n_day, *block.shape))
        return lax.all_to_all(many, ("sta", "day"), 0, 0, tiled=True)

    tile_s = math.gcd(512, s_loc)
    tile_t = math.gcd(512, t_loc)

    def tiles(blocks, size, tile):
        each = size // tile
        return (blocks[:, None] * each + jnp.arange(each, dtype=jnp.int32)[None, :]).reshape(-1)

    z_index = jnp.arange(n_z, dtype=jnp.int32)
    y_index = jnp.arange(n_y, dtype=jnp.int32)
    y_here = sta % n_y
    mine_s = z_index * n_y + y_here
    all_s = (z_index[None, :] * n_y + (y_here - y_index[:, None]) % n_y).reshape(-1)
    x_index = jnp.arange(n_x, dtype=jnp.int32)
    c_index = jnp.arange(n_core, dtype=jnp.int32)
    x_here, c_here = day // n_core, day % n_core
    all_t = ((x_here - x_index[:, None]) % n_x * n_core + (c_here + c_index[None, :]) % n_core).reshape(-1)
    mine_t = day[None].astype(jnp.int32)

    pieces = [mask_call(observed, direction, p, n_z) for p in range(probes)]

    space = entries_call(
        coords, tiles(mine_s, s_loc, tile_s), tiles(all_s, s_loc, tile_s), tile_s, space_range, STATIONS, "space_entries"
    )
    time = entries_call(
        day_features, tiles(all_t, t_loc, tile_t), tiles(mine_t, t_loc, tile_t), tile_t, time_range, DAYS, "time_entries"
    )

    def smooth_space(cells):
        return over_z(space_call(over_y(over_z(cells)), *space))

    def smooth_time(cells):
        return time_call(over_day(cells), *time)

    early = probes // 2
    outer = [smooth_time(smooth_space(pieces[p])) for p in range(early)]
    outer += [smooth_space(smooth_time(pieces[p])) for p in range(early, probes)]

    noise = noise[:, None]
    sums = [sums_call(observed, noise, residual, direction, outer[p], p) for p in range(probes)]
    first = over_all(jnp.concatenate(sums[:-1], axis=0))
    last = over_all(sums[-1])
    new = ()
    for p in range(probes):
        stats, row = (first, p) if p < probes - 1 else (last, 0)
        new = update_call(stats, row, observed, noise, solution, residual, direction, outer[p], p, new)
    return tuple(new)


def solution(mesh):
    in_specs = (
        P(None, "sta", "day"),
        P(None, "sta", "day"),
        P(None, "sta", "day"),
        P("sta", "day"),
        P(),
        P(),
        P("sta"),
    )
    out_specs = (P(None, "sta", "day"), P(None, "sta", "day"), P(None, "sta", "day"))
    return jax.shard_map(shards, mesh=mesh, in_specs=in_specs, out_specs=out_specs, check_vma=False)
```

time: 1210 us -> 607 us (0.50)
  matrix products: 418 us -> 0 us
  Pallas kernels: 0 us -> 289 us
  blocking collectives: 266 us -> 0 us
  waiting for transfers between devices: 369 us -> 170 us
  starting transfers between devices: 17.6 us -> 66.8 us
  other arithmetic: 48.8 us -> 0.26 us
    dot_general x16 -> x0, matrix products: 418 us -> none  [the longest x8 222 us: time_one_block(): jnp.einsum('brt,btc->rc', stacked, kern, precision=lax.Precision.HIGHEST)]
    pallas_call x0 -> x22, Pallas kernels: none -> 289 us  [the longest x2 91.4 us: entries_call(): pl.pallas_call(functools.partial(entries_kernel, features, slope, shift),...]
    all_to_all x3 -> x10, waiting for transfers between devices: 369 us -> 85.9 us  [the longest x8 82.9 us: over_z(): lax.all_to_all(pieces, 'sta', 0, 0, axis_index_groups=z_groups, tiled=True)]
    all_to_all x1 -> x0, blocking collectives: 187 us -> none  [shards(): lax.all_to_all(smooth, ('sta', 'day'), split_axis=0, concat_axis=0, tiled...]
    ppermute x0 -> x16, waiting for transfers between devices: none -> 83.9 us  [the longest x4 64.2 us: over_day(): here = lax.ppermute(cells, 'day', pairs) if k else cells]
    psum x2 -> x0, blocking collectives: 79.1 us -> none  [the longest x1 40.7 us: shards(): lax.psum(jnp.sum(new_residual * new_residual, axis=(1, 2)), ('sta', 'day'))]
    unnamed x10 -> x70, local copies, waits for them, and re-layouts: 0.02 us -> 68 us
    all_to_all x3 -> x10, starting transfers between devices: 17.6 us -> 55.6 us  [the longest x8 48.9 us: over_z(): lax.all_to_all(pieces, 'sta', 0, 0, axis_index_groups=z_groups, tiled=True)]
  transfers between devices with their start and end apart: 3 -> 26, of which waited for: 3 -> 8; matrix products, arithmetic and copies ran while one was open for 0% -> 1% of each run, Pallas kernels for 0% -> 47%
where the time goes in v1:
time: 607 us; the launch traced here: 597 us
  Pallas kernels  289 us (48%)
  waiting for transfers between devices  170 us (28%)
  local copies, waits for them, and re-layouts  69.8 us (11%)
  starting transfers between devices  66.8 us (11%)
    pallas_call x2, Pallas kernels, entries_call(): pl.pallas_call(functools.partial(entries_kernel, features, slope, shift),...  91.4 us
    all_to_all x8, waiting for transfers between devices, over_z(): lax.all_to_all(pieces, 'sta', 0, 0, axis_index_groups=z_groups, tiled=True)  82.9 us
    pallas_call x4, Pallas kernels, time_call(): pl.pallas_call(functools.partial(time_kernel, len(cells)), grid=(blocks,)...  80.7 us
    pallas_call x4, Pallas kernels, space_call(): pl.pallas_call(functools.partial(space_kernel, len(cells)), grid=(blocks,...  77.3 us
    unnamed x70, local copies, waits for them, and re-layouts  68 us
    ppermute x4, waiting for transfers between devices, over_day(): here = lax.ppermute(cells, 'day', pairs) if k else cells  64.2 us
    all_to_all x8, starting transfers between devices, over_z(): lax.all_to_all(pieces, 'sta', 0, 0, axis_index_groups=z_groups, tiled=True)  48.9 us
    pallas_call x4, Pallas kernels, update_call(): pl.pallas_call(functools.partial(update_kernel, row), grid=(parts,), in_s...  23.7 us
  transfers between devices with their start and end apart: 26, of which 8 were waited for; matrix products, arithmetic and copies ran while one was open for 1% of the time, Pallas kernels for 47%

profile of v1, /device:TPU:0, one launch (start us, length us, event | category | flops | bytes accessed | tf_op | source)
XLA Modules:
  0.0 596.5 jit_solution(12938174407581083053)
XLA Ops:
  0.6 3.4 copy-done
  4.0 1.6 copy-done.7
  7.5 6.4 %all-to-all-start.5 = ((f32[4,512,256]{2,1,0:T(8,128)}), f32[4,512,256]{2,1,0:T(8,128)}, u32[]{:S(2)}, u32[]{:S(2)}) async-start(f32[4,512,256]{2,1,0:T(8,128)} %copy-done.14), calls=%async_computation.5 | async-start | bytes 4194304 | tf_op jit(solution)/shard_map/all_to_all | solution.py:278
  14.0 3.4 copy-done.1
  17.4 2.1 mask.4.refs_0_
  19.5 1.5 collective-permute-start.1
  21.0 2.1 mask.7.refs_0_
  23.7 44.7 %collective-permute-done.1.refs_2_ = f32[4,512,256]{2,1,0:T(8,128)} collective-permute-done((f32[4,512,256]{2,1,0:T(8,128)}, f32[4,512,256]{2,1,0:T(8,128)}, u32[]{:S(2)}, u32[]{:S(2)}) %collective-permute-start.1) | collective-permute-done | bytes 2097184 | tf_op jit(solution)/shard_map/ppermute | solution.py:292
  70.3 5.2 all-to-all-start.3
  76.1 2.0 copy.21
  78.1 1.6 copy-done.24
  79.6 34.2 %time_entries.1 = (bf16[4096,1024]{1,0:T(8,128)(2,1)S(1)}, bf16[4096,1024]{1,0:T(8,128)(2,1)S(1)}) custom-call(s32[8]{0:T(128)S(1)} %add.131.rows_order, s32[2]{0:T(128)S(1)} %iota_add_fusion.1.cols_order, f32[4096,4]{1,0:T(8,128)S(1)} %bitcast.5, f32[4,4096]{1,0:T(4,128)S(1)} %copy-done.26), custom_call_target="tpu_custom_call" | custom-call | flops 67108864 | bytes 16777216 | tf_op jit(solution)/shard_map/time_entries/pallas_call | solution.py:73
  113.9 3.4 copy-done.29
  117.3 3.4 copy-done.30
  121.0 20.1 %time.4 = f32[4,512,256]{2,1,0:T(8,128)S(1)} custom-call(f32[4,512,256]{2,1,0:T(8,128)} %mask.4.refs_0_, f32[4,512,256]{2,1,0:T(8,128)} %collective-permute-done.refs_1_, f32[4,512,256]{2,1,0:T(8,128)} %collective-permute-done.1.refs_2_, f32[4,512,256]{2,1,0:T(8,128)} %collective-permute-done.2.refs_3_, bf16[4096,1024]{1,0:T(8,128)(2,1)} %copy-done.29, ...), custom_call_target="tpu_custom_call" | custom-call | flops 12884901888 | bytes 33554432 | tf_op jit(solution)/shard_map/time/pallas_call | solution.py:163
  142.4 5.1 all-to-all-start
  147.5 1.5 collective-permute-start.8
  149.0 20.1 %time.7 = f32[4,512,256]{2,1,0:T(8,128)S(1)} custom-call(f32[4,512,256]{2,1,0:T(8,128)} %mask.7.refs_0_, f32[4,512,256]{2,1,0:T(8,128)} %collective-permute-done.12.refs_1_, f32[4,512,256]{2,1,0:T(8,128)} %collective-permute-done.13.refs_2_, f32[4,512,256]{2,1,0:T(8,128)} %collective-permute-done.14.refs_3_, bf16[4096,1024]{1,0:T(8,128)(2,1)} %copy-done.29, ...), custom_call_target="tpu_custom_call" | custom-call | flops 12884901888 | bytes 33554432 | tf_op jit(solution)/shard_map/time/pallas_call | solution.py:163
  170.5 25.5 %all-to-all-done.refs_0_ = f32[4,512,256]{2,1,0:T(8,128)} async-done(((f32[4,512,256]{2,1,0:T(8,128)}), f32[4,512,256]{2,1,0:T(8,128)}, u32[]{:S(2)}, u32[]{:S(2)}) %all-to-all-start) | async-done | bytes 2097184 | tf_op jit(solution)/shard_map/all_to_all | solution.py:278
  196.0 4.7 all-to-all-start.7
  200.9 2.0 copy.22
  202.9 1.6 copy-done.25
  204.5 57.2 %space_entries.1 = (bf16[2048,4096]{1,0:T(8,128)(2,1)S(1)}, bf16[2048,4096]{1,0:T(8,128)(2,1)}) custom-call(s32[4]{0:T(128)S(1)} %broadcast_add_fusion.1.rows_order, s32[8]{0:T(128)S(1)} %add.141.cols_order, f32[4096,2]{1,0:T(8,128)S(1)} %bitcast.6, f32[2,4096]{1,0:T(2,128)S(1)} %copy-done.27), custom_call_target="tpu_custom_call" | custom-call | flops 134217728 | bytes 33554432 | tf_op jit(solution)/shard_map/space_entries/pallas_call | solution.py:73
  261.8 5.8 copy-done.28
  267.5 1.5 collective-permute-start.4
  269.0 19.3 %space.6 = f32[4,512,256]{2,1,0:T(8,128)S(1)} custom-call(f32[4,512,256]{2,1,0:T(8,128)} %all-to-all-done.5.refs_0_, f32[4,512,256]{2,1,0:T(8,128)} %collective-permute-done.8.refs_1_, bf16[2048,4096]{1,0:T(8,128)(2,1)} %copy-done.28, bf16[2048,4096]{1,0:T(8,128)(2,1)} %get-tuple-element.19.refs_3_), custom_call_target="tpu_custom_call" | custom-call | flops 12884901888 | bytes 41943040 | tf_op jit(solution)/shard_map/space/pallas_call | solution.py:123
  289.7 5.1 all-to-all-start.6
  294.8 19.7 %collective-permute-done.4.refs_1_ = f32[4,512,256]{2,1,0:T(8,128)} collective-permute-done((f32[4,512,256]{2,1,0:T(8,128)}, f32[4,512,256]{2,1,0:T(8,128)}, u32[]{:S(2)}, u32[]{:S(2)}) %collective-permute-start.4) | collective-permute-done | bytes 2097184 | tf_op jit(solution)/shard_map/ppermute | solution.py:284
  314.5 19.3 %space.5 = f32[4,512,256]{2,1,0:T(8,128)S(1)} custom-call(f32[4,512,256]{2,1,0:T(8,128)} %all-to-all-done.3.refs_0_, f32[4,512,256]{2,1,0:T(8,128)} %collective-permute-done.4.refs_1_, bf16[2048,4096]{1,0:T(8,128)(2,1)} %copy-done.28, bf16[2048,4096]{1,0:T(8,128)(2,1)} %get-tuple-element.19.refs_3_), custom_call_target="tpu_custom_call" | custom-call | flops 12884901888 | bytes 41943040 | tf_op jit(solution)/shard_map/space/pallas_call | solution.py:123
  335.1 6.7 %all-to-all-done.6.refs_0_ = f32[4,512,256]{2,1,0:T(8,128)} async-done(((f32[4,512,256]{2,1,0:T(8,128)}), f32[4,512,256]{2,1,0:T(8,128)}, u32[]{:S(2)}, u32[]{:S(2)}) %all-to-all-start.6) | async-done | bytes 2097184 | tf_op jit(solution)/shard_map/all_to_all | solution.py:278
  341.8 4.5 all-to-all-start.4
  346.9 1.5 collective-permute-start.3
  348.4 1.5 collective-permute-start.10
  349.9 44.2 %all-to-all-done.4.refs_0_ = f32[4,512,256]{2,1,0:T(8,128)} async-done(((f32[4,512,256]{2,1,0:T(8,128)}), f32[4,512,256]{2,1,0:T(8,128)}, u32[]{:S(2)}, u32[]{:S(2)}) %all-to-all-start.4) | async-done | bytes 2097184 | tf_op jit(solution)/shard_map/all_to_all | solution.py:278
  394.0 1.5 collective-permute-start.6
  395.5 19.3 %space.7 = f32[4,512,256]{2,1,0:T(8,128)S(1)} custom-call(f32[4,512,256]{2,1,0:T(8,128)} %all-to-all-done.7.refs_0_, f32[4,512,256]{2,1,0:T(8,128)} %collective-permute-done.15.refs_1_, bf16[2048,4096]{1,0:T(8,128)(2,1)} %copy-done.28, bf16[2048,4096]{1,0:T(8,128)(2,1)} %get-tuple-element.19.refs_3_), custom_call_target="tpu_custom_call" | custom-call | flops 12884901888 | bytes 41943040 | tf_op jit(solution)/shard_map/space/pallas_call | solution.py:123
  414.8 1.3 copy-done.20
  416.2 4.7 all-to-all-start.8
  421.4 19.5 %collective-permute-done.6.refs_2_ = f32[4,512,256]{2,1,0:T(8,128)} collective-permute-done((f32[4,512,256]{2,1,0:T(8,128)}, f32[4,512,256]{2,1,0:T(8,128)}, u32[]{:S(2)}, u32[]{:S(2)}) %collective-permute-start.6) | collective-permute-done | bytes 2097184 | tf_op jit(solution)/shard_map/ppermute | solution.py:292
  440.9 19.4 %space.4 = f32[4,512,256]{2,1,0:T(8,128)S(1)} custom-call(f32[4,512,256]{2,1,0:T(8,128)} %all-to-all-done.refs_0_, f32[4,512,256]{2,1,0:T(8,128)} %collective-permute-done.3.refs_1_, bf16[2048,4096]{1,0:T(8,128)(2,1)} %copy-done.28, bf16[2048,4096]{1,0:T(8,128)(2,1)} %get-tuple-element.19.refs_3_), custom_call_target="tpu_custom_call" | custom-call | flops 12884901888 | bytes 41943040 | tf_op jit(solution)/shard_map/space/pallas_call | solution.py:123
  461.6 6.5 %all-to-all-done.8.outer = f32[4,512,256]{2,1,0:T(8,128)} async-done(((f32[4,512,256]{2,1,0:T(8,128)}), f32[4,512,256]{2,1,0:T(8,128)}, u32[]{:S(2)}, u32[]{:S(2)}) %all-to-all-start.8) | async-done | bytes 2097184 | tf_op jit(solution)/shard_map/all_to_all | solution.py:278
  468.1 13.2 %all-to-all-start.1 = ((f32[4,512,256]{2,1,0:T(8,128)}), f32[4,512,256]{2,1,0:T(8,128)}, u32[]{:S(2)}, u32[]{:S(2)}) async-start(f32[4,512,256]{2,1,0:T(8,128)} %copy-done.19), calls=%async_computation.1 | async-start | bytes 4194304 | tf_op jit(solution)/shard_map/all_to_all | solution.py:278
  481.5 20.1 %time.6.outer = f32[4,512,256]{2,1,0:T(8,128)S(1)} custom-call(f32[4,512,256]{2,1,0:T(8,128)} %all-to-all-done.6.refs_0_, f32[4,512,256]{2,1,0:T(8,128)} %collective-permute-done.9.refs_1_, f32[4,512,256]{2,1,0:T(8,128)} %collective-permute-done.10.refs_2_, f32[4,512,256]{2,1,0:T(8,128)} %collective-permute-done.11.refs_3_, bf16[4096,1024]{1,0:T(8,128)(2,1)} %copy-done.29, ...), custom_call_target="tpu_custom_call" | custom-call | flops 12884901888 | bytes 33554432 | tf_op jit(solution)/shard_map/time/pallas_call | solution.py:163
  502.9 3.4 copy-done.2
  506.3 3.4 copy-done.4
  509.7 1.6 copy-done.16
  511.3 1.6 sums.6
  512.9 20.3 %time.5.outer = f32[4,512,256]{2,1,0:T(8,128)S(1)} custom-call(f32[4,512,256]{2,1,0:T(8,128)} %all-to-all-done.4.refs_0_, f32[4,512,256]{2,1,0:T(8,128)} %collective-permute-done.5.refs_1_, f32[4,512,256]{2,1,0:T(8,128)} %collective-permute-done.6.refs_2_, f32[4,512,256]{2,1,0:T(8,128)} %collective-permute-done.7.refs_3_, bf16[4096,1024]{1,0:T(8,128)(2,1)} %copy-done.29, ...), custom_call_target="tpu_custom_call" | custom-call | flops 12884901888 | bytes 33554432 | tf_op jit(solution)/shard_map/time/pallas_call | solution.py:163
  533.2 3.4 copy-done.5
  536.6 1.6 sums.5
  539.6 3.3 sums.7
  543.7 3.9 all-to-all-start.9
  547.6 3.4 copy-done.3
  551.0 3.4 copy-done.6
  554.4 3.3 sums.4
  557.7 3.1 all-to-all-done.9.parts
  561.5 2.8 all-to-all-start.2
  564.2 3.4 copy-done.9
  567.6 1.6 copy-done.12
  569.2 5.8 update.4
  575.0 5.7 update.5
  580.7 6.1 %update.6 = (f32[4,512,1024]{2,1,0:T(8,128)}, f32[4,512,1024]{2,1,0:T(8,128)}, f32[4,512,1024]{2,1,0:T(8,128)}) custom-call(f32[32,24,128]{2,1,0:T(8,128)S(1)} %all-to-all-done.9.parts, s32[512,1024]{1,0:T(8,128)S(1)} %copy-done.8, f32[512,1]{1,0:T(8,128)S(1)} %copy.23.noise, ...), custom_call_target="tpu_custom_call", output_to_operand_aliasing={{0}: (7, {}), {1}: (8, {}), {2}: (9, {})} | custom-call | flops 6291456 | bytes 16777216 | tf_op jit(solution)/shard_map/update/pallas_call | solution.py:241
  586.8 3.4 copy-done.10
  590.2 6.1 %update.7 = (f32[4,512,1024]{2,1,0:T(8,128)}, f32[4,512,1024]{2,1,0:T(8,128)}, f32[4,512,1024]{2,1,0:T(8,128)}) custom-call(f32[32,8,128]{2,1,0:T(8,128)S(1)} %all-to-all-done.2.parts, s32[512,1024]{1,0:T(8,128)S(1)} %copy-done.8, f32[512,1]{1,0:T(8,128)S(1)} %copy.23.noise, ...), custom_call_target="tpu_custom_call", output_to_operand_aliasing={{0}: (7, {}), {1}: (8, {}), {2}: (9, {})} | custom-call | flops 6291456 | bytes 16777216 | tf_op jit(solution)/shard_map/update/pallas_call | solution.py:241
  (96 shorter events, 17.4 us)
Async XLA Ops:
  0.6 3.4 copy-start
  4.0 1.6 copy-start.7
  6.2 1.3 copy-start.14
  7.5 6.5 %copy-start.8 = (s32[512,1024]{1,0:T(8,128)S(1)}, s32[512,1024]{1,0:T(8,128)}, u32[]{:S(2)}) copy-start(s32[512,1024]{1,0:T(8,128)} %observed.23) | copy-start | bytes 6291460
  7.5 62.7 %all-to-all-start.5 = ((f32[4,512,256]{2,1,0:T(8,128)}), f32[4,512,256]{2,1,0:T(8,128)}, u32[]{:S(2)}, u32[]{:S(2)}) async-start(f32[4,512,256]{2,1,0:T(8,128)} %copy-done.14), calls=%async_computation.5 | async-start | bytes 4194304 | tf_op jit(solution)/shard_map/all_to_all | solution.py:278
  14.0 3.4 copy-start.1
  19.5 48.9 %collective-permute-start.1 = (f32[4,512,256]{2,1,0:T(8,128)}, f32[4,512,256]{2,1,0:T(8,128)}, u32[]{:S(2)}, u32[]{:S(2)}) collective-permute-start(f32[4,512,256]{2,1,0:T(8,128)} %mask.4.refs_0_), channel_id=1, source_target_pairs={{0,2},{1,3},{2,0},{3,1},{4,6},{5,7},{6,4},{7,5},{8,10},{9,11},{10,... | collective-permute-start | bytes 6291464 | tf_op jit(solution)/shard_map/ppermute | solution.py:292
  23.1 97.5 %collective-permute-start.13 = (f32[4,512,256]{2,1,0:T(8,128)}, f32[4,512,256]{2,1,0:T(8,128)}, u32[]{:S(2)}, u32[]{:S(2)}) collective-permute-start(f32[4,512,256]{2,1,0:T(8,128)} %mask.7.refs_0_), channel_id=1, source_target_pairs={{0,2},{1,3},{2,0},{3,1},{4,6},{5,7},{6,4},{7,5},{8,10},{9,11},{10,... | collective-permute-start | bytes 6291464 | tf_op jit(solution)/shard_map/ppermute | solution.py:292
  23.7 97.3 %collective-permute-start = (f32[4,512,256]{2,1,0:T(8,128)}, f32[4,512,256]{2,1,0:T(8,128)}, u32[]{:S(2)}, u32[]{:S(2)}) collective-permute-start(f32[4,512,256]{2,1,0:T(8,128)} %mask.4.refs_0_), channel_id=1, source_target_pairs={{0,1},{1,0},{2,3},{3,2},{4,5},{5,4},{6,7},{7,6},{8,9},{9,8},{10,11... | collective-permute-start | bytes 6291464 | tf_op jit(solution)/shard_map/ppermute | solution.py:295
  68.4 52.6 %collective-permute-start.2 = (f32[4,512,256]{2,1,0:T(8,128)}, f32[4,512,256]{2,1,0:T(8,128)}, u32[]{:S(2)}, u32[]{:S(2)}) collective-permute-start(f32[4,512,256]{2,1,0:T(8,128)} %collective-permute-done.1.refs_2_), channel_id=1, source_target_pairs={{0,1},{1,0},{2,3},{3,2},{4,5},{5,4},{6,7},{7,6},{8,9},{9,8},{10,11... | collective-permute-start | bytes 6291464 | tf_op jit(solution)/shard_map/ppermute | solution.py:295
  69.0 1.3 copy-start.13
  70.3 5.8 copy-start.26
  70.3 72.2 %all-to-all-start.3 = ((f32[4,512,256]{2,1,0:T(8,128)}), f32[4,512,256]{2,1,0:T(8,128)}, u32[]{:S(2)}, u32[]{:S(2)}) async-start(f32[4,512,256]{2,1,0:T(8,128)} %copy-done.13), calls=%async_computation.3 | async-start | bytes 4194304 | tf_op jit(solution)/shard_map/all_to_all | solution.py:278
  75.5 73.5 %collective-permute-start.12 = (f32[4,512,256]{2,1,0:T(8,128)}, f32[4,512,256]{2,1,0:T(8,128)}, u32[]{:S(2)}, u32[]{:S(2)}) collective-permute-start(f32[4,512,256]{2,1,0:T(8,128)} %mask.7.refs_0_), channel_id=1, source_target_pairs={{0,1},{1,0},{2,3},{3,2},{4,5},{5,4},{6,7},{7,6},{8,9},{9,8},{10,11... | collective-permute-start | bytes 6291464 | tf_op jit(solution)/shard_map/ppermute | solution.py:295
  78.1 1.6 copy-start.24
  113.9 3.4 copy-start.29
  117.3 3.4 copy-start.30
  120.7 28.4 %collective-permute-start.14 = (f32[4,512,256]{2,1,0:T(8,128)}, f32[4,512,256]{2,1,0:T(8,128)}, u32[]{:S(2)}, u32[]{:S(2)}) collective-permute-start(f32[4,512,256]{2,1,0:T(8,128)} %collective-permute-done.13.refs_2_), channel_id=1, source_target_pairs={{0,1},{1,0},{2,3},{3,2},{4,5},{5,4},{6,7},{7,6},{8,9},{9,8},{10,11... | collective-permute-start | bytes 6291464 | tf_op jit(solution)/shard_map/ppermute | solution.py:295
  141.1 1.3 copy-start.21
  142.4 53.6 %all-to-all-start = ((f32[4,512,256]{2,1,0:T(8,128)}), f32[4,512,256]{2,1,0:T(8,128)}, u32[]{:S(2)}, u32[]{:S(2)}) async-start(f32[4,512,256]{2,1,0:T(8,128)} %copy-done.21), calls=%async_computation | async-start | bytes 4194304 | tf_op jit(solution)/shard_map/all_to_all | solution.py:278
  147.5 121.5 %collective-permute-start.8 = (f32[4,512,256]{2,1,0:T(8,128)}, f32[4,512,256]{2,1,0:T(8,128)}, u32[]{:S(2)}, u32[]{:S(2)}) collective-permute-start(f32[4,512,256]{2,1,0:T(8,128)} %all-to-all-done.5.refs_0_), channel_id=1, source_target_pairs={{0,4},{4,0},{8,12},{12,8},{16,20},{20,16},{24,28},{28,24},{1,5},{5... | collective-permute-start | bytes 6291464 | tf_op jit(solution)/shard_map/ppermute | solution.py:284
  169.2 1.3 copy-start.18
  170.5 30.4 %copy-start.27 = (f32[2,4096]{1,0:T(2,128)S(1)}, f32[2,4096]{1,0:T(2,128)}, u32[]{:S(2)}) copy-start(f32[2,4096]{1,0:T(2,128)} %cols.3) | copy-start | bytes 98308
  196.0 93.7 %all-to-all-start.7 = ((f32[4,512,256]{2,1,0:T(8,128)}), f32[4,512,256]{2,1,0:T(8,128)}, u32[]{:S(2)}, u32[]{:S(2)}) async-start(f32[4,512,256]{2,1,0:T(8,128)} %copy-done.18), calls=%async_computation.7 | async-start | bytes 4194304 | tf_op jit(solution)/shard_map/all_to_all | solution.py:278
  202.9 1.6 copy-start.25
  261.8 5.8 copy-start.28
  267.5 46.9 %collective-permute-start.4 = (f32[4,512,256]{2,1,0:T(8,128)}, f32[4,512,256]{2,1,0:T(8,128)}, u32[]{:S(2)}, u32[]{:S(2)}) collective-permute-start(f32[4,512,256]{2,1,0:T(8,128)} %all-to-all-done.3.refs_0_), channel_id=1, source_target_pairs={{0,4},{4,0},{8,12},{12,8},{16,20},{20,16},{24,28},{28,24},{1,5},{5... | collective-permute-start | bytes 6291464 | tf_op jit(solution)/shard_map/ppermute | solution.py:284
  288.4 1.3 copy-start.23
  289.7 52.1 %all-to-all-start.6 = ((f32[4,512,256]{2,1,0:T(8,128)}), f32[4,512,256]{2,1,0:T(8,128)}, u32[]{:S(2)}, u32[]{:S(2)}) async-start(f32[4,512,256]{2,1,0:T(8,128)} %copy-done.23), calls=%async_computation.6 | async-start | bytes 4194304 | tf_op jit(solution)/shard_map/all_to_all | solution.py:278
  333.8 1.3 copy-start.22
  341.8 52.2 %all-to-all-start.4 = ((f32[4,512,256]{2,1,0:T(8,128)}), f32[4,512,256]{2,1,0:T(8,128)}, u32[]{:S(2)}, u32[]{:S(2)}) async-start(f32[4,512,256]{2,1,0:T(8,128)} %copy-done.22), calls=%async_computation.4 | async-start | bytes 4194304 | tf_op jit(solution)/shard_map/all_to_all | solution.py:278
  346.3 49.2 %collective-permute-start.15 = (f32[4,512,256]{2,1,0:T(8,128)}, f32[4,512,256]{2,1,0:T(8,128)}, u32[]{:S(2)}, u32[]{:S(2)}) collective-permute-start(f32[4,512,256]{2,1,0:T(8,128)} %all-to-all-done.7.refs_0_), channel_id=1, source_target_pairs={{0,4},{4,0},{8,12},{12,8},{16,20},{20,16},{24,28},{28,24},{1,5},{5... | collective-permute-start | bytes 6291464 | tf_op jit(solution)/shard_map/ppermute | solution.py:284
  346.9 94.1 %collective-permute-start.3 = (f32[4,512,256]{2,1,0:T(8,128)}, f32[4,512,256]{2,1,0:T(8,128)}, u32[]{:S(2)}, u32[]{:S(2)}) collective-permute-start(f32[4,512,256]{2,1,0:T(8,128)} %all-to-all-done.refs_0_), channel_id=1, source_target_pairs={{0,4},{4,0},{8,12},{12,8},{16,20},{20,16},{24,28},{28,24},{1,5},{5... | collective-permute-start | bytes 6291464 | tf_op jit(solution)/shard_map/ppermute | solution.py:284
  348.4 72.5 %collective-permute-start.10 = (f32[4,512,256]{2,1,0:T(8,128)}, f32[4,512,256]{2,1,0:T(8,128)}, u32[]{:S(2)}, u32[]{:S(2)}) collective-permute-start(f32[4,512,256]{2,1,0:T(8,128)} %all-to-all-done.6.refs_0_), channel_id=1, source_target_pairs={{0,2},{1,3},{2,0},{3,1},{4,6},{5,7},{6,4},{7,5},{8,10},{9,11},{10,... | collective-permute-start | bytes 6291464 | tf_op jit(solution)/shard_map/ppermute | solution.py:292
  394.0 46.9 %collective-permute-start.6 = (f32[4,512,256]{2,1,0:T(8,128)}, f32[4,512,256]{2,1,0:T(8,128)}, u32[]{:S(2)}, u32[]{:S(2)}) collective-permute-start(f32[4,512,256]{2,1,0:T(8,128)} %all-to-all-done.4.refs_0_), channel_id=1, source_target_pairs={{0,2},{1,3},{2,0},{3,1},{4,6},{5,7},{6,4},{7,5},{8,10},{9,11},{10,... | collective-permute-start | bytes 6291464 | tf_op jit(solution)/shard_map/ppermute | solution.py:292
  414.8 1.3 copy-start.20
  416.2 51.9 %all-to-all-start.8 = ((f32[4,512,256]{2,1,0:T(8,128)}), f32[4,512,256]{2,1,0:T(8,128)}, u32[]{:S(2)}, u32[]{:S(2)}) async-start(f32[4,512,256]{2,1,0:T(8,128)} %copy-done.20), calls=%async_computation.8 | async-start | bytes 4194304 | tf_op jit(solution)/shard_map/all_to_all | solution.py:278
  420.9 60.6 %collective-permute-start.9 = (f32[4,512,256]{2,1,0:T(8,128)}, f32[4,512,256]{2,1,0:T(8,128)}, u32[]{:S(2)}, u32[]{:S(2)}) collective-permute-start(f32[4,512,256]{2,1,0:T(8,128)} %all-to-all-done.6.refs_0_), channel_id=1, source_target_pairs={{0,1},{1,0},{2,3},{3,2},{4,5},{5,4},{6,7},{7,6},{8,9},{9,8},{10,11... | collective-permute-start | bytes 6291464 | tf_op jit(solution)/shard_map/ppermute | solution.py:295
  420.9 60.6 %collective-permute-start.11 = (f32[4,512,256]{2,1,0:T(8,128)}, f32[4,512,256]{2,1,0:T(8,128)}, u32[]{:S(2)}, u32[]{:S(2)}) collective-permute-start(f32[4,512,256]{2,1,0:T(8,128)} %collective-permute-done.10.refs_2_), channel_id=1, source_target_pairs={{0,1},{1,0},{2,3},{3,2},{4,5},{5,4},{6,7},{7,6},{8,9},{9,8},{10,11... | collective-permute-start | bytes 6291464 | tf_op jit(solution)/shard_map/ppermute | solution.py:295
  421.4 91.5 %collective-permute-start.5 = (f32[4,512,256]{2,1,0:T(8,128)}, f32[4,512,256]{2,1,0:T(8,128)}, u32[]{:S(2)}, u32[]{:S(2)}) collective-permute-start(f32[4,512,256]{2,1,0:T(8,128)} %all-to-all-done.4.refs_0_), channel_id=1, source_target_pairs={{0,1},{1,0},{2,3},{3,2},{4,5},{5,4},{6,7},{7,6},{8,9},{9,8},{10,11... | collective-permute-start | bytes 6291464 | tf_op jit(solution)/shard_map/ppermute | solution.py:295
  440.9 72.0 %collective-permute-start.7 = (f32[4,512,256]{2,1,0:T(8,128)}, f32[4,512,256]{2,1,0:T(8,128)}, u32[]{:S(2)}, u32[]{:S(2)}) collective-permute-start(f32[4,512,256]{2,1,0:T(8,128)} %collective-permute-done.6.refs_2_), channel_id=1, source_target_pairs={{0,1},{1,0},{2,3},{3,2},{4,5},{5,4},{6,7},{7,6},{8,9},{9,8},{10,11... | collective-permute-start | bytes 6291464 | tf_op jit(solution)/shard_map/ppermute | solution.py:295
  460.3 1.3 copy-start.19
  461.6 19.7 %copy-start.31 = (f32[512]{0:T(512)S(1)}, f32[512]{0:T(512)}, u32[]{:S(2)}) copy-start(f32[512]{0:T(512)} %param.13) | copy-start | bytes 6148
  468.1 74.8 %all-to-all-start.1 = ((f32[4,512,256]{2,1,0:T(8,128)}), f32[4,512,256]{2,1,0:T(8,128)}, u32[]{:S(2)}, u32[]{:S(2)}) async-start(f32[4,512,256]{2,1,0:T(8,128)} %copy-done.19), calls=%async_computation.1 | async-start | bytes 4194304 | tf_op jit(solution)/shard_map/all_to_all | solution.py:278
  501.6 1.3 copy-start.15
  502.9 3.4 copy-start.2
  506.3 3.4 copy-start.4
  509.7 1.6 copy-start.16
  511.3 21.9 %slice-start = ((s8[8388608]{0:T(1024)(128)(4,1)}), s8[4194304]{0:T(1024)(128)(4,1)S(1)}, s32[]{:S(2)}) async-start(s8[8388608]{0:T(1024)(128)(4,1)} %bitcast.3), calls=%async_computation.10 | async-start | bytes 8388608
  512.9 20.3 %slice-start.1 = ((s8[8388608]{0:T(1024)(128)(4,1)}), s8[4194304]{0:T(1024)(128)(4,1)S(1)}, s32[]{:S(2)}) async-start(s8[8388608]{0:T(1024)(128)(4,1)} %bitcast.3), calls=%async_computation.11 | async-start | bytes 8388608
  533.2 3.4 copy-start.5
  538.2 1.3 copy-start.11
  543.7 17.1 %all-to-all-start.9 = ((f32[32,24,128]{2,1,0:T(8,128)}), f32[32,24,128]{2,1,0:T(8,128)S(1)}, u32[]{:S(2)}, u32[]{:S(2)}) async-start(f32[32,24,128]{2,1,0:T(8,128)} %broadcast_in_dim.8), calls=%async_computation.9 | async-start | bytes 786432 | tf_op jit(solution)/shard_map/all_to_all | solution.py:300
  547.6 3.4 copy-start.3
  551.0 3.4 copy-start.6
  561.5 25.4 %all-to-all-start.2 = ((f32[32,8,128]{2,1,0:T(8,128)}), f32[32,8,128]{2,1,0:T(8,128)S(1)}, u32[]{:S(2)}, u32[]{:S(2)}) async-start(f32[32,8,128]{2,1,0:T(8,128)} %broadcast_in_dim.7), calls=%async_computation.2 | async-start | bytes 262144 | tf_op jit(solution)/shard_map/all_to_all | solution.py:300
  564.2 3.4 copy-start.9
  567.6 1.6 copy-start.12
  569.2 5.8 copy-start.17
  586.8 3.4 copy-start.10

commit v2 on v0

v2 whole, which is shorter than its diff:
```python
import functools
import math

import jax
import jax.numpy as jnp
from jax import lax
from jax.experimental import pallas as pl
from jax.experimental.pallas import tpu as pltpu
from jax.sharding import PartitionSpec as P

STATIONS = 4096
DAYS = 4096
FEAT = 4

space_range = 0.5
time_range = 0.5

HBM = pltpu.MemorySpace.HBM
F32 = jnp.float32
BF16 = jnp.bfloat16


class Chain:
    def __init__(self, place):
        self.place = place
        self.token = None

    def __call__(self, body, name, grid, operands, in_specs, outs, out_specs, scratch=(), aliases=()):
        operands, in_specs = list(operands), list(in_specs)
        n_in, n_tok = len(operands), 0 if self.token is None else 1
        if n_tok:
            operands.append(self.token)
            in_specs.append(pl.BlockSpec(memory_space=HBM))
        n_out = len(outs)

        def kernel(place, *refs):
            rest = refs[n_in + n_tok :]
            body(place, *refs[:n_in], *rest[:n_out], *rest[n_out + 1 :])

        found = pl.pallas_call(
            kernel,
            grid_spec=pltpu.PrefetchScalarGridSpec(
                num_scalar_prefetch=1,
                grid=grid,
                in_specs=in_specs,
                out_specs=list(out_specs) + [pl.BlockSpec(memory_space=HBM)],
                scratch_shapes=list(scratch),
            ),
            out_shape=[jax.ShapeDtypeStruct(*out) for out in outs] + [jax.ShapeDtypeStruct((8, 128), F32)],
            input_output_aliases={1 + k: v for k, v in aliases},
            compiler_params=pltpu.CompilerParams(vmem_limit_bytes=60 << 20),
            cost_estimate=pl.CostEstimate(flops=0, bytes_accessed=0, transcendentals=0),
            name=name,
        )(self.place, *operands)
        self.token = found[-1]
        return list(found[:-1])


def rows_spec(*shape):
    lead = len(shape) - 2
    return pl.BlockSpec(shape, lambda i, place: (0,) * lead + (i, 0))


def columns_of(place, k, sign, parts, width):
    block = lax.rem(place[0] + (k if sign > 0 else parts - k), parts)
    return pl.ds(pl.multiple_of(block * width, width), width)


CHUNKS = 4


def mask_call(chain, observed, direction, probe, parts, together):
    _, s_loc, t_loc = direction.shape
    width, rows = t_loc // parts, s_loc // CHUNKS

    def body(place, seen, way, *out):
        for k in range(parts):
            if together:
                at = pl.ds(k * width, width)
                out[0][k] = seen[:, at].astype(F32) * way[0, :, at]
            else:
                at = columns_of(place, k, 1, parts, width)
                out[k][...] = seen[:, at].astype(F32) * way[0, :, at]

    if together:
        outs, specs = [((parts, s_loc, width), F32)], [rows_spec(parts, rows, width)]
    else:
        outs, specs = [((s_loc, width), F32)] * parts, [rows_spec(rows, width)] * parts
    found = chain(
        body,
        "mask",
        (CHUNKS,),
        (observed, direction),
        [rows_spec(rows, t_loc), pl.BlockSpec((1, rows, t_loc), lambda i, place: (probe, i, 0))],
        outs,
        specs,
    )
    return found[0] if together else found


def stack_call(chain, pieces):
    s_loc, width = pieces[0].shape
    parts, rows = len(pieces), s_loc // CHUNKS

    def body(place, *refs):
        for k in range(parts):
            refs[parts][lax.rem(place[0] + parts - k, parts)] = refs[k][...]

    return chain(
        body,
        "stack",
        (CHUNKS,),
        pieces,
        [rows_spec(rows, width)] * parts,
        [((parts, s_loc, width), F32)],
        [rows_spec(parts, rows, width)],
    )[0]


def add_call(chain, terms):
    parts, s_loc, width = terms[0].shape
    rows = s_loc // CHUNKS

    def body(place, *refs):
        for k in range(parts):
            block = lax.rem(place[0] + k, parts)
            total = refs[0][block]
            for term in refs[1 : len(terms)]:
                total = total + term[block]
            refs[len(terms) + k][...] = total

    return chain(
        body,
        "add",
        (CHUNKS,),
        terms,
        [rows_spec(parts, rows, width)] * len(terms),
        [((s_loc, width), F32)] * parts,
        [rows_spec(rows, width)] * parts,
    )


def gate_call(chain, array):
    hbm = pl.BlockSpec(memory_space=HBM)
    return chain(lambda place, a, b: None, "gate", (), [array], [hbm], [(array.shape, array.dtype)], [hbm], aliases=[(0, 0)])[0]


def entries_call(chain, table, unit, n_rows, n_cols, row_block, col_block, reach, order, name, halves=(0, 1), earlier=()):
    features = table.shape[0]
    shape = (n_rows * unit, n_cols * unit)
    half, of = halves
    row_units = max(1, math.gcd(n_rows // of, 1024 // unit))
    col_units = max(1, math.gcd(n_cols, 1024 // unit))
    tile = (row_units * unit, col_units * unit)
    count = n_rows // of // row_units
    first = half * count
    shift = math.log(2.0 / order**0.5)
    step = 16

    def body(place, *refs):
        rows, cols = refs[:row_units], refs[row_units : row_units + col_units]
        high, low, across, down = refs[-4:]
        for u in range(col_units):
            for feature in range(features):
                line = cols[u][feature : feature + 1, :] * (1.0 / reach)
                across[feature, :, u * unit : (u + 1) * unit] = jnp.broadcast_to(line, (8, unit))
        for u in range(row_units):
            turned = jnp.concatenate([rows[u][...], jnp.zeros((8 - features, unit), F32)], axis=0).T * (1.0 / reach)
            for feature in range(features):
                down[feature, u * unit : (u + 1) * unit, :] = jnp.broadcast_to(turned[:, feature : feature + 1], (unit, 128))

        @pl.loop(0, tile[0] // step)
        def _(index):
            at = pl.ds(pl.multiple_of(index * step, step), step)
            total = None
            for feature in range(features):
                mine = jnp.concatenate([down[feature, at, :]] * (tile[1] // 128), axis=1)
                other = jnp.concatenate([across[feature]] * (step // 8), axis=0)
                diff = mine - other
                total = diff * diff if total is None else total + diff * diff
            dist = total * lax.rsqrt(jnp.maximum(total, 1e-37))
            high[at, :], low[at, :] = split(jnp.exp(shift - dist))

    def row_spec(u):
        return pl.BlockSpec((features, unit), lambda i, j, place: (0, row_block(place, (i + first) * row_units + u)))

    def col_spec(u):
        return pl.BlockSpec((features, unit), lambda i, j, place: (0, col_block(place, j * col_units + u)))

    out = pl.BlockSpec(tile, lambda i, j, place: (i + first, j))
    operands = [table] * (row_units + col_units)
    return chain(
        body,
        name,
        (count, n_cols // col_units),
        operands + list(earlier),
        [row_spec(u) for u in range(row_units)]
        + [col_spec(u) for u in range(col_units)]
        + [pl.BlockSpec(memory_space=HBM)] * len(earlier),
        [(shape, BF16)] * 2,
        [out, out],
        scratch=[pltpu.VMEM((features, 8, tile[1]), F32), pltpu.VMEM((features, tile[0], 128), F32)],
        aliases=[(len(operands) + k, k) for k in range(len(earlier))],
    )


def split(value):
    top = value.astype(BF16)
    return top, (value - top.astype(F32)).astype(BF16)


def dot(a, b):
    return jnp.dot(a, b, preferred_element_type=F32)


def space_call(chain, cells, matrices, together):
    parts, s_loc, width = cells[0].shape
    count = len(cells)
    span = parts * s_loc

    def body(place, *refs):
        mine, kern = refs[:count], refs[count : 3 * count]
        out, (cells_high, cells_low) = refs[3 * count : -2], refs[-2:]
        step = pl.program_id(0)

        @pl.when(step == 0)
        def _():
            for n in range(count):
                for b in range(parts):
                    at = pl.ds((n * parts + b) * s_loc, s_loc)
                    cells_high[at, :], cells_low[at, :] = split(mine[n][b])

        total = None
        for n in range(count):
            at = pl.ds(n * span, span)
            high, low = kern[2 * n], kern[2 * n + 1]
            term = dot(high[...], cells_high[at, :]) + dot(high[...], cells_low[at, :]) + dot(low[...], cells_high[at, :])
            total = term if total is None else total + term
        if together:
            out[0][0] = total
        else:
            for k in range(parts):

                @pl.when(step == k)
                def _():
                    out[k][...] = total

    whole = pl.BlockSpec((parts, s_loc, width), lambda i, place: (0, 0, 0))
    if together:
        matrix = pl.BlockSpec((s_loc, span), lambda i, place: (i, 0))
        outs, specs = [((parts, s_loc, width), F32)], [pl.BlockSpec((1, s_loc, width), lambda i, place: (i, 0, 0))]
    else:
        matrix = pl.BlockSpec((s_loc, span), lambda i, place: (lax.rem(place[0] + i, parts), 0))
        outs, specs = [((s_loc, width), F32)] * parts, [pl.BlockSpec((s_loc, width), lambda i, place: (0, 0))] * parts
    found = chain(
        body,
        "space",
        (parts,),
        list(cells) + [m for pair in matrices for m in pair],
        [whole] * count + [matrix] * (2 * count),
        outs,
        specs,
        scratch=[pltpu.VMEM((count * span, width), BF16)] * 2,
    )
    return found[0] if together else found


def time_call(chain, cells, matrix, cores):
    parts, s_loc, width = cells[0].shape
    count = len(cells)
    days = count * parts * width
    each = math.gcd(parts, 2)
    steps = parts // each

    def body(place, *refs):
        mine, (high, low) = refs[:count], refs[count : count + 2]
        out, (cells_high, cells_low) = refs[count + 2 : -2], refs[-2:]
        step = pl.program_id(0)

        @pl.when(step == 0)
        def _():
            for n in range(count):
                for b in range(parts):
                    at = pl.ds((n * parts + b) * width, width)
                    cells_high[:, at], cells_low[:, at] = split(mine[n][b])

        total = dot(cells_high[...], high[...]) + dot(cells_low[...], high[...]) + dot(cells_high[...], low[...])
        for c in range(cores):

            @pl.when(step // steps == c)
            def _():
                for e in range(each):
                    out[c][e] = total[:, e * width : (e + 1) * width]

    def out_spec(c):
        return pl.BlockSpec(
            (each, s_loc, width), lambda i, place: (jnp.clip(i - c * steps, 0, steps - 1), 0, 0)
        )

    whole = pl.BlockSpec((parts, s_loc, width), lambda i, place: (0, 0, 0))
    columns = pl.BlockSpec((days, each * width), lambda i, place: (0, i))
    return chain(
        body,
        "time",
        (steps * cores,),
        list(cells) + list(matrix),
        [whole] * count + [columns] * 2,
        [((parts, s_loc, width), F32)] * cores,
        [out_spec(c) for c in range(cores)],
        scratch=[pltpu.VMEM((s_loc, days), BF16)] * 2,
    )


class Outer:
    def __init__(self, refs):
        self.operands = list(refs)
        self.whole = refs[0].ndim == 3
        self.parts = refs[0].shape[0] if self.whole else len(refs)
        self.width = refs[0].shape[-1]

    def specs(self, rows):
        one = rows_spec(self.parts, rows, self.width) if self.whole else rows_spec(rows, self.width)
        return [one] * len(self.operands)

    def each(self, place, refs):
        for k in range(self.parts):
            if self.whole:
                value = refs[0][k]
                for other in refs[1:]:
                    value = value + other[k]
                yield pl.ds(k * self.width, self.width), value
            else:
                yield columns_of(place, k, -1, self.parts, self.width), refs[k][...]


def sums_call(chain, observed, noise, residual, direction, outer, probe):
    _, s_loc, t_loc = direction.shape
    rows = s_loc // CHUNKS
    n = len(outer.operands)

    def body(place, seen, var, res_ref, way_ref, *refs):
        out, total = refs[n:]
        step = pl.program_id(0)

        @pl.when(step == 0)
        def _():
            total[...] = jnp.zeros_like(total)

        for at, value in outer.each(place, refs[:n]):
            res, way = res_ref[0, :, at], way_ref[0, :, at]
            image = seen[:, at].astype(F32) * value + var[...] * way
            for row, product in enumerate((res * res, way * image, res * image, image * image)):
                total[row : row + 1, :] += jnp.sum(product, axis=0, keepdims=True)

        @pl.when(step == pl.num_programs(0) - 1)
        def _():
            out[...] = jnp.broadcast_to(jnp.sum(total[...], axis=1, keepdims=True), out.shape)

    probe_rows = pl.BlockSpec((1, rows, t_loc), lambda i, place: (probe, i, 0))
    return chain(
        body,
        "sums",
        (CHUNKS,),
        [observed, noise, residual, direction, *outer.operands],
        [rows_spec(rows, t_loc), rows_spec(rows, 1), probe_rows, probe_rows] + outer.specs(rows),
        [((8, 128), F32)],
        [pl.BlockSpec((8, 128), lambda i, place: (0, 0))],
        scratch=[pltpu.VMEM((8, outer.width), F32)],
    )[0]


def update_call(chain, stats, row, observed, noise, solution, residual, direction, outer, probe, earlier):
    _, s_loc, t_loc = direction.shape
    rows = s_loc // CHUNKS
    n = len(outer.operands)

    def body(place, given, seen, var, sol_ref, res_ref, way_ref, *refs):
        new_solution, new_residual, new_direction = refs[-3:]
        totals = jnp.sum(given[:, row * 8 : row * 8 + 8, :], axis=0)
        rr, pap, cross, square = (totals[k : k + 1, :1] for k in range(4))
        alpha = rr / pap
        rr_next = rr + alpha * (alpha * square - 2.0 * cross)
        beta = rr_next / rr
        for at, value in outer.each(place, refs[:n]):
            way = way_ref[0, :, at]
            image = seen[:, at].astype(F32) * value + var[...] * way
            fresh = res_ref[0, :, at] - alpha * image
            new_solution[0, :, at] = sol_ref[0, :, at] + alpha * way
            new_residual[0, :, at] = fresh
            new_direction[0, :, at] = fresh + beta * way

    probe_rows = pl.BlockSpec((1, rows, t_loc), lambda i, place: (probe, i, 0))
    operands = [stats, observed, noise, solution, residual, direction, *outer.operands]
    return chain(
        body,
        "update",
        (CHUNKS,),
        operands + list(earlier),
        [
            pl.BlockSpec(stats.shape, lambda i, place: (0, 0, 0)),
            rows_spec(rows, t_loc),
            rows_spec(rows, 1),
            probe_rows,
            probe_rows,
            probe_rows,
        ]
        + outer.specs(rows)
        + [pl.BlockSpec(memory_space=HBM)] * len(earlier),
        [(direction.shape, F32)] * 3,
        [probe_rows] * 3,
        aliases=[(len(operands) + k, k) for k in range(len(earlier))],
    )


def shards(solution, residual, direction, observed, coords, day_features, noise):
    n_sta = lax.axis_size("sta")
    n_day = lax.axis_size("day")
    _, s_loc, t_loc = direction.shape
    n_z = math.gcd(n_sta, 4)
    n_y = n_sta // n_z
    n_c = math.gcd(n_day, 2)
    n_x = n_day // n_c
    sta = lax.axis_index("sta")
    day = lax.axis_index("day")
    place = jnp.stack([sta // n_y, sta % n_y, day // n_c, day % n_c]).astype(jnp.int32)
    chain = Chain(place)

    def over_z(pieces):
        found = [pieces[0]]
        for k in range(1, n_z):
            pairs = [(z * n_y + y, (z + k) % n_z * n_y + y) for z in range(n_z) for y in range(n_y)]
            found.append(lax.ppermute(pieces[k], "sta", pairs))
        return found

    def over_z_at_once(pieces):
        groups = [[z * n_y + y for z in range(n_z)] for y in range(n_y)]
        return lax.all_to_all(pieces, "sta", 0, 0, axis_index_groups=groups, tiled=True)

    def over_y(cells):
        found = [cells]
        for k in range(1, n_y):
            pairs = [(z * n_y + y, z * n_y + (y + k) % n_y) for z in range(n_z) for y in range(n_y)]
            found.append(lax.ppermute(cells, "sta", pairs))
        return found

    def over_x(cells):
        found = [cells]
        for k in range(1, n_x):
            pairs = [(x * n_c + c, (x + k) % n_x * n_c + c) for x in range(n_x) for c in range(n_c)]
            found.append(lax.ppermute(cells, "day", pairs))
        return found

    def over_core(terms):
        pairs = [(j, j - j % n_c + (j + 1) % n_c) for j in range(n_day)]
        return terms[:1] + [lax.ppermute(term, "day", pairs) for term in terms[1:]]

    def over_all(*blocks):
        many = jnp.concatenate(blocks, axis=0) if len(blocks) > 1 else blocks[0]
        many = jnp.broadcast_to(many[None], (n_sta * n_day, *many.shape))
        return lax.all_to_all(many, ("sta", "day"), 0, 0, tiled=True)

    def back(value, k, size):
        return lax.rem(value + size - k, size)

    def space_row(place, i):
        return i * n_y + place[1]

    def space_col(shift):
        return lambda place, j: j * n_y + lax.rem(place[1] + n_y - shift, n_y)

    def time_row(place, i):
        return back(place[2], i, n_x) * n_c + place[3]

    def time_col(place, j):
        return place[2] * n_c + lax.rem(place[3] + j, n_c)

    def space_entries(shift, halves, earlier):
        col = space_col(shift)
        return entries_call(
            chain, coords, s_loc, n_z, n_z, space_row, col, space_range, STATIONS, "space_entries", halves, earlier
        )

    def space(cells, together):
        return space_call(chain, cells, matrices, together)

    def days(arrived):
        return over_core(time_call(chain, arrived, time, n_c))

    noise = noise[:, None]

    def sums(outer, p):
        return sums_call(chain, observed, noise, residual, direction, outer, p)

    def update(stats, row, outer, p, earlier):
        return update_call(chain, stats, row, observed, noise, solution, residual, direction, outer, p, earlier)

    def mask(p, together):
        return mask_call(chain, observed, direction, p, n_z, together)

    out0 = over_z(mask(0, False))
    x2 = over_x(mask(2, True))
    out1 = over_z_at_once(mask(1, True))
    time = entries_call(chain, day_features, t_loc, n_x, n_c, time_row, time_col, time_range, DAYS, "time_entries")
    x3 = over_x(mask(3, True))
    out2 = over_z(add_call(chain, days(x2)))
    cells0 = over_y(stack_call(chain, out0))
    matrices = [space_entries(0, (0, 2), ())]
    cells1 = over_y(gate_call(chain, out1))
    out3 = days(x3)
    matrices[0] = space_entries(0, (1, 2), matrices[0])
    out3 = over_z(add_call(chain, out3))
    for k in range(1, n_y):
        matrices.append(space_entries(k, (0, 1), ()))
    cells2 = over_y(stack_call(chain, out2))
    home0 = over_z_at_once(space(cells0, True))
    cells3 = over_y(stack_call(chain, out3))
    home1 = over_z(space(cells1, False))
    x0 = over_x(gate_call(chain, home0))
    home2 = over_z_at_once(space(cells2, True))
    home3 = over_z(space(cells3, False))
    outer0 = days(x0)
    x1 = over_x(stack_call(chain, home1))
    outer0 = Outer(outer0)
    sums0 = sums(outer0, 0)
    outer2 = Outer([home2])
    stats02 = over_all(sums0, sums(outer2, 2))
    outer1 = days(x1)
    new = update(stats02, 0, outer0, 0, ())
    outer1 = Outer(outer1)
    stats1 = over_all(sums(outer1, 1))
    new = update(stats02, 1, outer2, 2, new)
    outer3 = Outer(home3)
    stats3 = over_all(sums(outer3, 3))
    new = update(stats1, 0, outer1, 1, new)
    new = update(stats3, 0, outer3, 3, new)
    return tuple(new)


def solution(mesh):
    in_specs = (
        P(None, "sta", "day"),
        P(None, "sta", "day"),
        P(None, "sta", "day"),
        P("sta", "day"),
        P(),
        P(),
        P("sta"),
    )
    out_specs = (P(None, "sta", "day"), P(None, "sta", "day"), P(None, "sta", "day"))
    return jax.shard_map(shards, mesh=mesh, in_specs=in_specs, out_specs=out_specs, check_vma=False)
```

time: 1210 us -> 660 us (0.55)
  matrix products: 418 us -> 0 us
  Pallas kernels: 0 us -> 335 us
  blocking collectives: 266 us -> 0 us
  waiting for transfers between devices: 369 us -> 203 us
  starting transfers between devices: 17.6 us -> 102 us
  local copies, waits for them, and re-layouts: 72.2 us -> 17.2 us
  other arithmetic: 48.8 us -> 0.61 us
    dot_general x16 -> x0, matrix products: 418 us -> none  [the longest x8 222 us: time_one_block(): jnp.einsum('brt,btc->rc', stacked, kern, precision=lax.Precision.HIGHEST)]
    all_to_all x3 -> x6, waiting for transfers between devices: 369 us -> 27.2 us  [the longest x3 27.2 us: over_all(): return lax.all_to_all(many, ('sta', 'day'), 0, 0, tiled=True)]
    pallas_call x0 -> x32, Pallas kernels: none -> 335 us  [__call__(): pl.pallas_call(kernel, grid_spec=pltpu.PrefetchScalarGridSpec(num_scalar_...]
    all_to_all x1 -> x0, blocking collectives: 187 us -> none  [shards(): lax.all_to_all(smooth, ('sta', 'day'), split_axis=0, concat_axis=0, tiled...]
    ppermute x0 -> x27, waiting for transfers between devices: none -> 176 us  [the longest x15 136 us: over_z(): found.append(lax.ppermute(pieces[k], 'sta', pairs))]
    psum x2 -> x0, blocking collectives: 79.1 us -> none  [the longest x1 40.7 us: shards(): lax.psum(jnp.sum(new_residual * new_residual, axis=(1, 2)), ('sta', 'day'))]
    ppermute x0 -> x27, starting transfers between devices: none -> 47.7 us  [the longest x15 36.7 us: over_z(): found.append(lax.ppermute(pieces[k], 'sta', pairs))]
    all_to_all x3 -> x6, starting transfers between devices: 17.6 us -> 54 us  [the longest x3 31.6 us: over_z_at_once(): lax.all_to_all(pieces, 'sta', 0, 0, axis_index_groups=groups, tiled=True)]
  transfers between devices with their start and end apart: 3 -> 33, of which waited for: 3 -> 9; matrix products, arithmetic and copies ran while one was open for 0% -> 0% of each run, Pallas kernels for 0% -> 39%
where the time goes in v2:
time: 660 us; the launch traced here: 658 us
  Pallas kernels  335 us (51%)
  waiting for transfers between devices  203 us (31%)
  starting transfers between devices  102 us (15%)
  local copies, waits for them, and re-layouts  17.2 us (3%)
    pallas_call x32, Pallas kernels, __call__(): pl.pallas_call(kernel, grid_spec=pltpu.PrefetchScalarGridSpec(num_scalar_...  335 us
    ppermute x15, waiting for transfers between devices, over_z(): found.append(lax.ppermute(pieces[k], 'sta', pairs))  136 us
    ppermute x4, waiting for transfers between devices, over_x(): found.append(lax.ppermute(cells, 'day', pairs))  39 us
    ppermute x15, starting transfers between devices, over_z(): found.append(lax.ppermute(pieces[k], 'sta', pairs))  36.7 us
    all_to_all x3, starting transfers between devices, over_z_at_once(): lax.all_to_all(pieces, 'sta', 0, 0, axis_index_groups=groups, tiled=True)  31.6 us
    all_to_all x3, waiting for transfers between devices, over_all(): return lax.all_to_all(many, ('sta', 'day'), 0, 0, tiled=True)  27.2 us
    all_to_all x3, starting transfers between devices, over_all(): return lax.all_to_all(many, ('sta', 'day'), 0, 0, tiled=True)  22.4 us
  transfers between devices with their start and end apart: 33, of which 9 were waited for; matrix products, arithmetic and copies ran while one was open for 0% of the time, Pallas kernels for 39%

profile of v2, /device:TPU:0, one launch (start us, length us, event | category | flops | bytes accessed | tf_op | source)
XLA Modules:
  0.0 658.3 jit_solution(13523996487651685557)
XLA Ops:
  1.3 4.9 mask.4
  6.2 4.9 mask.5
  11.0 2.9 collective-permute-start.4
  13.9 4.9 mask.6
  18.8 4.9 all-to-all-start
  23.7 22.3 %time_entries.1 = (bf16[2048,2048]{1,0:T(8,128)(2,1)}, bf16[2048,2048]{1,0:T(8,128)(2,1)}, f32[8,128]{1,0:T(8,128)}) custom-call(s32[4]{0:T(128)} %pad_add_fusion.place, f32[4,4096]{1,0:T(4,128)} %refs_1_.15, f32[4,4096]{1,0:T(4,128)} %refs_1_.15, f32[8,128]{1,0:T(8,128)} %get-tuple-element.99.refs_2_), custom_call_target="tpu_custom_call" | custom-call | tf_op jit(solution)/shard_map/time_entries/pallas_call | solution.py:40
  46.0 4.8 mask.7
  50.8 9.1 %collective-permute-done.4.refs_1_ = f32[4,512,256]{2,1,0:T(8,128)} collective-permute-done((f32[4,512,256]{2,1,0:T(8,128)}, f32[4,512,256]{2,1,0:T(8,128)}, u32[]{:S(2)}, u32[]{:S(2)}) %collective-permute-start.4) | collective-permute-done | bytes 2097184 | tf_op jit(solution)/shard_map/ppermute | solution.py:450
  59.9 20.4 %time.4 = (f32[4,512,256]{2,1,0:T(8,128)}, f32[4,512,256]{2,1,0:T(8,128)}, f32[8,128]{1,0:T(8,128)}) custom-call(s32[4]{0:T(128)} %pad_add_fusion.place, f32[4,512,256]{2,1,0:T(8,128)} %get-tuple-element.109.refs_0_, f32[4,512,256]{2,1,0:T(8,128)} %collective-permute-done.4.refs_1_, bf16[2048,2048]{1,0:T(8,128)(2,1)} %get-tuple-element.102.refs_2_, ...), custom_call_target="tpu_custom_call" | custom-call | tf_op jit(solution)/shard_map/time/pallas_call | solution.py:40
  80.3 1.8 collective-permute-start
  82.1 1.6 collective-permute-start.1
  83.7 2.6 collective-permute-start.2
  87.7 4.8 add.19
  92.5 6.6 collective-permute-done.1.refs_1_
  99.1 21.8 %collective-permute-done.2.refs_2_ = f32[512,256]{1,0:T(8,128)S(1)} collective-permute-done((f32[512,256]{1,0:T(8,128)}, f32[512,256]{1,0:T(8,128)S(1)}, u32[]{:S(2)}, u32[]{:S(2)}) %collective-permute-start.2) | collective-permute-done | bytes 524320 | tf_op jit(solution)/shard_map/ppermute | solution.py:432
  121.9 4.5 stack.24
  126.3 10.5 %space_entries.3 = (bf16[2048,2048]{1,0:T(8,128)(2,1)}, bf16[2048,2048]{1,0:T(8,128)(2,1)}, f32[8,128]{1,0:T(8,128)}) custom-call(s32[4]{0:T(128)} %pad_add_fusion.place, f32[2,4096]{1,0:T(2,128)} %refs_3_.13, f32[2,4096]{1,0:T(2,128)} %refs_3_.13, f32[2,4096]{1,0:T(2,128)} %refs_3_.13, f32[2,4096]{1,0:T(2,128)} %refs_3_.13, f32[8,128]{1,0:T(8,128)} %get-tuple-element.115.refs_4_), custom_call_target="tpu_custom_call" | custom-call | tf_op jit(solution)/shard_map/space_entries/pallas_call | solution.py:40
  138.8 20.5 %time.5 = (f32[4,512,256]{2,1,0:T(8,128)}, f32[4,512,256]{2,1,0:T(8,128)}, f32[8,128]{1,0:T(8,128)}) custom-call(s32[4]{0:T(128)} %pad_add_fusion.place, f32[4,512,256]{2,1,0:T(8,128)} %get-tuple-element.101.refs_0_, f32[4,512,256]{2,1,0:T(8,128)} %collective-permute-done.refs_1_, bf16[2048,2048]{1,0:T(8,128)(2,1)} %get-tuple-element.102.refs_2_, ...), custom_call_target="tpu_custom_call" | custom-call | tf_op jit(solution)/shard_map/time/pallas_call | solution.py:40
  159.3 1.6 collective-permute-start.10
  160.9 11.5 %collective-permute-start.11 = (f32[512,256]{1,0:T(8,128)}, f32[512,256]{1,0:T(8,128)S(1)}, u32[]{:S(2)}, u32[]{:S(2)}) collective-permute-start(f32[512,256]{1,0:T(8,128)} %get-tuple-element.135), channel_id=1, source_target_pairs={{0,8},{4,12},{8,16},{12,20},{16,24},{20,28},{24,0},{28,4},{1,9},{5... | collective-permute-start | bytes 1572872 | tf_op jit(solution)/shard_map/ppermute | solution.py:432
  172.3 1.8 collective-permute-start.12
  174.7 10.4 %space_entries.4 = (bf16[2048,2048]{1,0:T(8,128)(2,1)}, bf16[2048,2048]{1,0:T(8,128)(2,1)}, f32[8,128]{1,0:T(8,128)}) custom-call(s32[4]{0:T(128)} %pad_add_fusion.place, f32[2,4096]{1,0:T(2,128)} %refs_3_.13, f32[2,4096]{1,0:T(2,128)} %refs_3_.13, f32[2,4096]{1,0:T(2,128)} %refs_3_.13, ...), custom_call_target="tpu_custom_call", output_to_operand_aliasing={{0}: (5, {}), {1}: (6, {})} | custom-call | tf_op jit(solution)/shard_map/space_entries/pallas_call | solution.py:40
  186.4 4.9 add.20
  191.3 17.3 %space_entries.5 = (bf16[2048,2048]{1,0:T(8,128)(2,1)}, bf16[2048,2048]{1,0:T(8,128)(2,1)}, f32[8,128]{1,0:T(8,128)}) custom-call(s32[4]{0:T(128)} %pad_add_fusion.place, f32[2,4096]{1,0:T(2,128)} %refs_3_.13, f32[2,4096]{1,0:T(2,128)} %refs_3_.13, f32[2,4096]{1,0:T(2,128)} %refs_3_.13, f32[2,4096]{1,0:T(2,128)} %refs_3_.13, f32[8,128]{1,0:T(8,128)} %get-tuple-element.131.refs_4_), custom_call_target="tpu_custom_call" | custom-call | tf_op jit(solution)/shard_map/space_entries/pallas_call | solution.py:40
  209.8 4.5 stack.25
  214.3 21.4 %space.4 = (f32[4,512,256]{2,1,0:T(8,128)}, f32[8,128]{1,0:T(8,128)}) custom-call(s32[4]{0:T(128)} %pad_add_fusion.place, f32[4,512,256]{2,1,0:T(8,128)} %get-tuple-element.128.refs_0_, f32[4,512,256]{2,1,0:T(8,128)} %collective-permute-done.10.refs_1_, bf16[2048,2048]{1,0:T(8,128)(2,1)} %get-tuple-element.129.refs_2_, ...), custom_call_target="tpu_custom_call" | custom-call | tf_op jit(solution)/shard_map/space/pallas_call | solution.py:40
  235.7 13.4 %all-to-all-start.1 = ((f32[4,512,256]{2,1,0:T(8,128)}), f32[4,512,256]{2,1,0:T(8,128)S(1)}, u32[]{:S(2)}, u32[]{:S(2)}) async-start(f32[4,512,256]{2,1,0:T(8,128)} %get-tuple-element.143), calls=%async_computation.1 | async-start | bytes 4194304 | tf_op jit(solution)/shard_map/all_to_all | solution.py:437
  249.6 1.5 collective-permute-start.15
  251.1 2.0 collective-permute-start.7
  253.1 2.4 collective-permute-start.8
  255.5 1.5 collective-permute-start.9
  257.0 42.8 %collective-permute-done.7.refs_1_ = f32[512,256]{1,0:T(8,128)S(1)} collective-permute-done((f32[512,256]{1,0:T(8,128)}, f32[512,256]{1,0:T(8,128)S(1)}, u32[]{:S(2)}, u32[]{:S(2)}) %collective-permute-start.7) | collective-permute-done | bytes 524320 | tf_op jit(solution)/shard_map/ppermute | solution.py:432
  299.8 32.1 %collective-permute-done.8.refs_2_ = f32[512,256]{1,0:T(8,128)S(1)} collective-permute-done((f32[512,256]{1,0:T(8,128)}, f32[512,256]{1,0:T(8,128)S(1)}, u32[]{:S(2)}, u32[]{:S(2)}) %collective-permute-start.8) | collective-permute-done | bytes 524320 | tf_op jit(solution)/shard_map/ppermute | solution.py:432
  332.8 4.5 stack.26
  337.8 22.1 %space.5 = (f32[512,256]{1,0:T(8,128)}, f32[512,256]{1,0:T(8,128)}, f32[512,256]{1,0:T(8,128)}, f32[512,256]{1,0:T(8,128)}, f32[8,128]{1,0:T(8,128)}) custom-call(s32[4]{0:T(128)} %pad_add_fusion.place, f32[4,512,256]{2,1,0:T(8,128)} %get-tuple-element.144.refs_0_, f32[4,512,256]{2,1,0:T(8,128)} %collective-permute-done.16.refs_1_, ...), custom_call_target="tpu_custom_call" | custom-call | tf_op jit(solution)/shard_map/space/pallas_call | solution.py:40
  362.5 21.4 %space.6 = (f32[4,512,256]{2,1,0:T(8,128)}, f32[8,128]{1,0:T(8,128)}) custom-call(s32[4]{0:T(128)} %pad_add_fusion.place, f32[4,512,256]{2,1,0:T(8,128)} %get-tuple-element.142.refs_0_, f32[4,512,256]{2,1,0:T(8,128)} %collective-permute-done.15.refs_1_, bf16[2048,2048]{1,0:T(8,128)(2,1)} %get-tuple-element.129.refs_2_, ...), custom_call_target="tpu_custom_call" | custom-call | tf_op jit(solution)/shard_map/space/pallas_call | solution.py:40
  383.9 13.4 %all-to-all-start.2 = ((f32[4,512,256]{2,1,0:T(8,128)}), f32[4,512,256]{2,1,0:T(8,128)S(1)}, u32[]{:S(2)}, u32[]{:S(2)}) async-start(f32[4,512,256]{2,1,0:T(8,128)} %get-tuple-element.164), calls=%async_computation.2 | async-start | bytes 4194304 | tf_op jit(solution)/shard_map/all_to_all | solution.py:437
  397.3 2.0 collective-permute-start.22
  399.4 2.4 collective-permute-start.23
  401.7 1.5 collective-permute-start.24
  403.2 22.1 %space.7 = (f32[512,256]{1,0:T(8,128)}, f32[512,256]{1,0:T(8,128)}, f32[512,256]{1,0:T(8,128)}, f32[512,256]{1,0:T(8,128)}, f32[8,128]{1,0:T(8,128)}) custom-call(s32[4]{0:T(128)} %pad_add_fusion.place, f32[4,512,256]{2,1,0:T(8,128)} %get-tuple-element.141.refs_0_, f32[4,512,256]{2,1,0:T(8,128)} %collective-permute-done.14.refs_1_, ...), custom_call_target="tpu_custom_call" | custom-call | tf_op jit(solution)/shard_map/space/pallas_call | solution.py:40
  425.3 20.4 %time.6 = (f32[4,512,256]{2,1,0:T(8,128)}, f32[4,512,256]{2,1,0:T(8,128)}, f32[8,128]{1,0:T(8,128)}) custom-call(s32[4]{0:T(128)} %pad_add_fusion.place, f32[4,512,256]{2,1,0:T(8,128)} %get-tuple-element.153.refs_0_, f32[4,512,256]{2,1,0:T(8,128)} %collective-permute-done.20.refs_1_, bf16[2048,2048]{1,0:T(8,128)(2,1)} %get-tuple-element.102.refs_2_, ...), custom_call_target="tpu_custom_call" | custom-call | tf_op jit(solution)/shard_map/time/pallas_call | solution.py:40
  445.7 2.3 collective-permute-done.22.refs_1_
  448.0 30.9 %collective-permute-done.23.refs_2_ = f32[512,256]{1,0:T(8,128)S(1)} collective-permute-done((f32[512,256]{1,0:T(8,128)}, f32[512,256]{1,0:T(8,128)S(1)}, u32[]{:S(2)}, u32[]{:S(2)}) %collective-permute-start.23) | collective-permute-done | bytes 524320 | tf_op jit(solution)/shard_map/ppermute | solution.py:432
  479.9 4.5 stack.27
  484.4 1.5 collective-permute-start.25
  486.7 6.3 sums.4
  493.1 1.4 copy-done
  494.5 5.8 sums.5
  500.2 30.0 %collective-permute-done.25.refs_1_ = f32[4,512,256]{2,1,0:T(8,128)} collective-permute-done((f32[4,512,256]{2,1,0:T(8,128)}, f32[4,512,256]{2,1,0:T(8,128)}, u32[]{:S(2)}, u32[]{:S(2)}) %collective-permute-start.25) | collective-permute-done | bytes 2097184 | tf_op jit(solution)/shard_map/ppermute | solution.py:450
  530.2 20.6 %time.7 = (f32[4,512,256]{2,1,0:T(8,128)}, f32[4,512,256]{2,1,0:T(8,128)}, f32[8,128]{1,0:T(8,128)}) custom-call(s32[4]{0:T(128)} %pad_add_fusion.place, f32[4,512,256]{2,1,0:T(8,128)} %get-tuple-element.167.refs_0_, f32[4,512,256]{2,1,0:T(8,128)} %collective-permute-done.25.refs_1_, bf16[2048,2048]{1,0:T(8,128)(2,1)} %get-tuple-element.102.refs_2_, ...), custom_call_target="tpu_custom_call" | custom-call | tf_op jit(solution)/shard_map/time/pallas_call | solution.py:40
  551.6 14.0 %all-to-all-start.3 = ((f32[32,16,128]{2,1,0:T(8,128)}), f32[32,16,128]{2,1,0:T(8,128)S(1)}, u32[]{:S(2)}, u32[]{:S(2)}) async-start(f32[32,16,128]{2,1,0:T(8,128)} %broadcast_in_dim.9), calls=%async_computation.3 | async-start | bytes 524288 | tf_op jit(solution)/shard_map/all_to_all | solution.py:460
  565.6 1.8 collective-permute-start.17
  567.4 2.4 collective-permute-start.18
  569.8 1.4 collective-permute-start.19
  571.2 27.2 %all-to-all-done.3.refs_0_ = f32[32,16,128]{2,1,0:T(8,128)S(1)} async-done(((f32[32,16,128]{2,1,0:T(8,128)}), f32[32,16,128]{2,1,0:T(8,128)S(1)}, u32[]{:S(2)}, u32[]{:S(2)}) %all-to-all-start.3) | async-done | bytes 262176 | tf_op jit(solution)/shard_map/all_to_all | solution.py:460
  599.1 8.4 %update.4 = (f32[4,512,1024]{2,1,0:T(8,128)}, f32[4,512,1024]{2,1,0:T(8,128)}, f32[4,512,1024]{2,1,0:T(8,128)}, f32[8,128]{1,0:T(8,128)}) custom-call(s32[4]{0:T(128)} %pad_add_fusion.place, f32[32,16,128]{2,1,0:T(8,128)} %copy-done.4, s32[512,1024]{1,0:T(8,128)} %refs_1_.23, f32[512,1]{1,0:T(8,128)} %copy.28.refs_1_.refs_2_, f32[4,512,1024]{2,1,0:T(8,128)} %refs_3_.21, ...), custom_call_target="tpu_custom_call" | custom-call | tf_op jit(solution)/shard_map/update/pallas_call | solution.py:40
  608.8 6.3 sums.6
  616.5 2.6 all-to-all-start.5
  619.0 7.9 %update.5 = (f32[4,512,1024]{2,1,0:T(8,128)}, f32[4,512,1024]{2,1,0:T(8,128)}, f32[4,512,1024]{2,1,0:T(8,128)}, f32[8,128]{1,0:T(8,128)}) custom-call(s32[4]{0:T(128)} %pad_add_fusion.place, f32[32,16,128]{2,1,0:T(8,128)} %copy-done.4, s32[512,1024]{1,0:T(8,128)} %refs_1_.23, ...), custom_call_target="tpu_custom_call", output_to_operand_aliasing={{0}: (8, {}), {1}: (9, {}), {2}: (10, {})} | custom-call | tf_op jit(solution)/shard_map/update/pallas_call | solution.py:40
  627.9 5.8 sums.7
  635.0 5.8 all-to-all-start.4
  640.9 8.3 %update.6 = (f32[4,512,1024]{2,1,0:T(8,128)}, f32[4,512,1024]{2,1,0:T(8,128)}, f32[4,512,1024]{2,1,0:T(8,128)}, f32[8,128]{1,0:T(8,128)}) custom-call(s32[4]{0:T(128)} %pad_add_fusion.place, f32[32,8,128]{2,1,0:T(8,128)} %copy-done.8, s32[512,1024]{1,0:T(8,128)} %refs_1_.23, ...), custom_call_target="tpu_custom_call", output_to_operand_aliasing={{0}: (9, {}), {1}: (10, {}), {2}: (11, {})} | custom-call | tf_op jit(solution)/shard_map/update/pallas_call | solution.py:40
  649.8 8.4 %update.7 = (f32[4,512,1024]{2,1,0:T(8,128)}, f32[4,512,1024]{2,1,0:T(8,128)}, f32[4,512,1024]{2,1,0:T(8,128)}, f32[8,128]{1,0:T(8,128)}) custom-call(s32[4]{0:T(128)} %pad_add_fusion.place, f32[32,8,128]{2,1,0:T(8,128)} %copy-done.9, s32[512,1024]{1,0:T(8,128)} %refs_1_.23, ...), custom_call_target="tpu_custom_call", output_to_operand_aliasing={{0}: (11, {}), {1}: (12, {}), {2}: (13, {})} | custom-call | tf_op jit(solution)/shard_map/update/pallas_call | solution.py:40
  (90 shorter events, 21.4 us)
Async XLA Ops:
  11.0 48.9 %collective-permute-start.4 = (f32[4,512,256]{2,1,0:T(8,128)}, f32[4,512,256]{2,1,0:T(8,128)}, u32[]{:S(2)}, u32[]{:S(2)}) collective-permute-start(f32[4,512,256]{2,1,0:T(8,128)} %get-tuple-element.109.refs_0_), channel_id=1, source_target_pairs={{0,2},{1,3},{2,0},{3,1},{4,6},{5,7},{6,4},{7,5},{8,10},{9,11},{10,... | collective-permute-start | bytes 6291464 | tf_op jit(solution)/shard_map/ppermute | solution.py:450
  18.8 118.0 %all-to-all-start = ((f32[4,512,256]{2,1,0:T(8,128)}), f32[4,512,256]{2,1,0:T(8,128)S(1)}, u32[]{:S(2)}, u32[]{:S(2)}) async-start(f32[4,512,256]{2,1,0:T(8,128)} %get-tuple-element.104), calls=%async_computation | async-start | bytes 4194304 | tf_op jit(solution)/shard_map/all_to_all | solution.py:437
  80.3 7.3 %collective-permute-start.5 = (f32[4,512,256]{2,1,0:T(8,128)}, f32[4,512,256]{2,1,0:T(8,128)}, u32[]{:S(2)}, u32[]{:S(2)}) collective-permute-start(f32[4,512,256]{2,1,0:T(8,128)} %get-tuple-element.112), channel_id=1, source_target_pairs={{0,1},{1,0},{2,3},{3,2},{4,5},{5,4},{6,7},{7,6},{8,9},{9,8},{10,11... | collective-permute-start | bytes 6291464 | tf_op jit(solution)/shard_map/ppermute | solution.py:455
  80.3 58.5 %collective-permute-start = (f32[4,512,256]{2,1,0:T(8,128)}, f32[4,512,256]{2,1,0:T(8,128)}, u32[]{:S(2)}, u32[]{:S(2)}) collective-permute-start(f32[4,512,256]{2,1,0:T(8,128)} %get-tuple-element.101.refs_0_), channel_id=1, source_target_pairs={{0,2},{1,3},{2,0},{3,1},{4,6},{5,7},{6,4},{7,5},{8,10},{9,11},{10,... | collective-permute-start | bytes 6291464 | tf_op jit(solution)/shard_map/ppermute | solution.py:450
  82.1 16.9 %collective-permute-start.1 = (f32[512,256]{1,0:T(8,128)}, f32[512,256]{1,0:T(8,128)S(1)}, u32[]{:S(2)}, u32[]{:S(2)}) collective-permute-start(f32[512,256]{1,0:T(8,128)} %get-tuple-element.106), channel_id=1, source_target_pairs={{0,8},{4,12},{8,16},{12,20},{16,24},{20,28},{24,0},{28,4},{1,9},{5... | collective-permute-start | bytes 1572872 | tf_op jit(solution)/shard_map/ppermute | solution.py:432
  83.7 37.1 %collective-permute-start.2 = (f32[512,256]{1,0:T(8,128)}, f32[512,256]{1,0:T(8,128)S(1)}, u32[]{:S(2)}, u32[]{:S(2)}) collective-permute-start(f32[512,256]{1,0:T(8,128)} %get-tuple-element.107), channel_id=1, source_target_pairs={{0,16},{4,20},{8,24},{12,28},{16,0},{20,4},{24,8},{28,12},{1,17},{... | collective-permute-start | bytes 1572872 | tf_op jit(solution)/shard_map/ppermute | solution.py:432
  86.3 34.5 %collective-permute-start.3 = (f32[512,256]{1,0:T(8,128)}, f32[512,256]{1,0:T(8,128)S(1)}, u32[]{:S(2)}, u32[]{:S(2)}) collective-permute-start(f32[512,256]{1,0:T(8,128)} %get-tuple-element.108), channel_id=1, source_target_pairs={{0,24},{4,28},{8,0},{12,4},{16,8},{20,12},{24,16},{28,20},{1,25},{... | collective-permute-start | bytes 1572872 | tf_op jit(solution)/shard_map/ppermute | solution.py:432
  99.0 21.8 %copy-start.16 = (f32[512,256]{1,0:T(8,128)}, f32[512,256]{1,0:T(8,128)S(1)}, u32[]{:S(2)}) copy-start(f32[512,256]{1,0:T(8,128)S(1)} %collective-permute-done.1.refs_1_) | copy-start | bytes 1572868
  120.8 0.8 copy-start.17
  120.8 1.0 copy-start.18
  136.8 1.3 copy-start.2
  159.3 25.8 %collective-permute-start.6 = (f32[4,512,256]{2,1,0:T(8,128)}, f32[4,512,256]{2,1,0:T(8,128)S(1)}, u32[]{:S(2)}, u32[]{:S(2)}) collective-permute-start(f32[4,512,256]{2,1,0:T(8,128)} %get-tuple-element.119), channel_id=1, source_target_pairs={{0,1},{1,0},{2,3},{3,2},{4,5},{5,4},{6,7},{7,6},{8,9},{9,8},{10,11... | collective-permute-start | bytes 6291464 | tf_op jit(solution)/shard_map/ppermute | solution.py:455
  159.3 55.0 %collective-permute-start.10 = (f32[4,512,256]{2,1,0:T(8,128)}, f32[4,512,256]{2,1,0:T(8,128)}, u32[]{:S(2)}, u32[]{:S(2)}) collective-permute-start(f32[4,512,256]{2,1,0:T(8,128)} %get-tuple-element.128.refs_0_), channel_id=1, source_target_pairs={{0,4},{4,0},{8,12},{12,8},{16,20},{20,16},{24,28},{28,24},{1,5},{5... | collective-permute-start | bytes 6291464 | tf_op jit(solution)/shard_map/ppermute | solution.py:443
  160.9 47.8 %collective-permute-start.11 = (f32[512,256]{1,0:T(8,128)}, f32[512,256]{1,0:T(8,128)S(1)}, u32[]{:S(2)}, u32[]{:S(2)}) collective-permute-start(f32[512,256]{1,0:T(8,128)} %get-tuple-element.135), channel_id=1, source_target_pairs={{0,8},{4,12},{8,16},{12,20},{16,24},{20,28},{24,0},{28,4},{1,9},{5... | collective-permute-start | bytes 1572872 | tf_op jit(solution)/shard_map/ppermute | solution.py:432
  172.3 36.3 %collective-permute-start.12 = (f32[512,256]{1,0:T(8,128)}, f32[512,256]{1,0:T(8,128)S(1)}, u32[]{:S(2)}, u32[]{:S(2)}) collective-permute-start(f32[512,256]{1,0:T(8,128)} %get-tuple-element.136), channel_id=1, source_target_pairs={{0,16},{4,20},{8,24},{12,28},{16,0},{20,4},{24,8},{28,12},{1,17},{... | collective-permute-start | bytes 1572872 | tf_op jit(solution)/shard_map/ppermute | solution.py:432
  174.1 34.5 %collective-permute-start.13 = (f32[512,256]{1,0:T(8,128)}, f32[512,256]{1,0:T(8,128)S(1)}, u32[]{:S(2)}, u32[]{:S(2)}) collective-permute-start(f32[512,256]{1,0:T(8,128)} %get-tuple-element.137), channel_id=1, source_target_pairs={{0,24},{4,28},{8,0},{12,4},{16,8},{20,12},{24,16},{28,20},{1,25},{... | collective-permute-start | bytes 1572872 | tf_op jit(solution)/shard_map/ppermute | solution.py:432
  185.1 1.3 copy-start.7
  208.6 0.8 copy-start.12
  208.7 0.9 copy-start.14
  208.7 1.1 copy-start.15
  235.7 124.2 %all-to-all-start.1 = ((f32[4,512,256]{2,1,0:T(8,128)}), f32[4,512,256]{2,1,0:T(8,128)S(1)}, u32[]{:S(2)}, u32[]{:S(2)}) async-start(f32[4,512,256]{2,1,0:T(8,128)} %get-tuple-element.143), calls=%async_computation.1 | async-start | bytes 4194304 | tf_op jit(solution)/shard_map/all_to_all | solution.py:437
  249.1 88.8 %collective-permute-start.16 = (f32[4,512,256]{2,1,0:T(8,128)}, f32[4,512,256]{2,1,0:T(8,128)}, u32[]{:S(2)}, u32[]{:S(2)}) collective-permute-start(f32[4,512,256]{2,1,0:T(8,128)} %get-tuple-element.144.refs_0_), channel_id=1, source_target_pairs={{0,4},{4,0},{8,12},{12,8},{16,20},{20,16},{24,28},{28,24},{1,5},{5... | collective-permute-start | bytes 6291464 | tf_op jit(solution)/shard_map/ppermute | solution.py:443
  249.6 112.9 %collective-permute-start.15 = (f32[4,512,256]{2,1,0:T(8,128)}, f32[4,512,256]{2,1,0:T(8,128)}, u32[]{:S(2)}, u32[]{:S(2)}) collective-permute-start(f32[4,512,256]{2,1,0:T(8,128)} %get-tuple-element.142.refs_0_), channel_id=1, source_target_pairs={{0,4},{4,0},{8,12},{12,8},{16,20},{20,16},{24,28},{28,24},{1,5},{5... | collective-permute-start | bytes 6291464 | tf_op jit(solution)/shard_map/ppermute | solution.py:443
  251.1 48.6 %collective-permute-start.7 = (f32[512,256]{1,0:T(8,128)}, f32[512,256]{1,0:T(8,128)S(1)}, u32[]{:S(2)}, u32[]{:S(2)}) collective-permute-start(f32[512,256]{1,0:T(8,128)} %get-tuple-element.125), channel_id=1, source_target_pairs={{0,8},{4,12},{8,16},{12,20},{16,24},{20,28},{24,0},{28,4},{1,9},{5... | collective-permute-start | bytes 1572872 | tf_op jit(solution)/shard_map/ppermute | solution.py:432
  253.1 78.7 %collective-permute-start.8 = (f32[512,256]{1,0:T(8,128)}, f32[512,256]{1,0:T(8,128)S(1)}, u32[]{:S(2)}, u32[]{:S(2)}) collective-permute-start(f32[512,256]{1,0:T(8,128)} %get-tuple-element.126), channel_id=1, source_target_pairs={{0,16},{4,20},{8,24},{12,28},{16,0},{20,4},{24,8},{28,12},{1,17},{... | collective-permute-start | bytes 1572872 | tf_op jit(solution)/shard_map/ppermute | solution.py:432
  255.5 76.4 %collective-permute-start.9 = (f32[512,256]{1,0:T(8,128)}, f32[512,256]{1,0:T(8,128)S(1)}, u32[]{:S(2)}, u32[]{:S(2)}) collective-permute-start(f32[512,256]{1,0:T(8,128)} %get-tuple-element.127), channel_id=1, source_target_pairs={{0,24},{4,28},{8,0},{12,4},{16,8},{20,12},{24,16},{28,20},{1,25},{... | collective-permute-start | bytes 1572872 | tf_op jit(solution)/shard_map/ppermute | solution.py:432
  299.7 32.1 %copy-start.19 = (f32[512,256]{1,0:T(8,128)}, f32[512,256]{1,0:T(8,128)S(1)}, u32[]{:S(2)}) copy-start(f32[512,256]{1,0:T(8,128)S(1)} %collective-permute-done.7.refs_1_) | copy-start | bytes 1572868
  331.9 0.8 copy-start.20
  331.9 1.0 copy-start.21
  337.3 65.9 %collective-permute-start.14 = (f32[4,512,256]{2,1,0:T(8,128)}, f32[4,512,256]{2,1,0:T(8,128)}, u32[]{:S(2)}, u32[]{:S(2)}) collective-permute-start(f32[4,512,256]{2,1,0:T(8,128)} %get-tuple-element.141.refs_0_), channel_id=1, source_target_pairs={{0,4},{4,0},{8,12},{12,8},{16,20},{20,16},{24,28},{28,24},{1,5},{5... | collective-permute-start | bytes 6291464 | tf_op jit(solution)/shard_map/ppermute | solution.py:443
  359.9 1.3 copy-start.1
  361.9 63.4 %collective-permute-start.20 = (f32[4,512,256]{2,1,0:T(8,128)}, f32[4,512,256]{2,1,0:T(8,128)}, u32[]{:S(2)}, u32[]{:S(2)}) collective-permute-start(f32[4,512,256]{2,1,0:T(8,128)} %get-tuple-element.153.refs_0_), channel_id=1, source_target_pairs={{0,2},{1,3},{2,0},{3,1},{4,6},{5,7},{6,4},{7,5},{8,10},{9,11},{10,... | collective-permute-start | bytes 6291464 | tf_op jit(solution)/shard_map/ppermute | solution.py:450
  383.9 109.1 %all-to-all-start.2 = ((f32[4,512,256]{2,1,0:T(8,128)}), f32[4,512,256]{2,1,0:T(8,128)S(1)}, u32[]{:S(2)}, u32[]{:S(2)}) async-start(f32[4,512,256]{2,1,0:T(8,128)} %get-tuple-element.164), calls=%async_computation.2 | async-start | bytes 4194304 | tf_op jit(solution)/shard_map/all_to_all | solution.py:437
  397.3 50.7 %collective-permute-start.22 = (f32[512,256]{1,0:T(8,128)}, f32[512,256]{1,0:T(8,128)S(1)}, u32[]{:S(2)}, u32[]{:S(2)}) collective-permute-start(f32[512,256]{1,0:T(8,128)} %get-tuple-element.158), channel_id=1, source_target_pairs={{0,8},{4,12},{8,16},{12,20},{16,24},{20,28},{24,0},{28,4},{1,9},{5... | collective-permute-start | bytes 1572872 | tf_op jit(solution)/shard_map/ppermute | solution.py:432
  399.4 79.6 %collective-permute-start.23 = (f32[512,256]{1,0:T(8,128)}, f32[512,256]{1,0:T(8,128)S(1)}, u32[]{:S(2)}, u32[]{:S(2)}) collective-permute-start(f32[512,256]{1,0:T(8,128)} %get-tuple-element.159), channel_id=1, source_target_pairs={{0,16},{4,20},{8,24},{12,28},{16,0},{20,4},{24,8},{28,12},{1,17},{... | collective-permute-start | bytes 1572872 | tf_op jit(solution)/shard_map/ppermute | solution.py:432
  401.7 77.2 %collective-permute-start.24 = (f32[512,256]{1,0:T(8,128)}, f32[512,256]{1,0:T(8,128)S(1)}, u32[]{:S(2)}, u32[]{:S(2)}) collective-permute-start(f32[512,256]{1,0:T(8,128)} %get-tuple-element.160), channel_id=1, source_target_pairs={{0,24},{4,28},{8,0},{12,4},{16,8},{20,12},{24,16},{28,20},{1,25},{... | collective-permute-start | bytes 1572872 | tf_op jit(solution)/shard_map/ppermute | solution.py:432
  445.7 40.1 %copy-start.24 = (f32[512]{0:T(512)S(1)}, f32[512]{0:T(512)}, u32[]{:S(2)}) copy-start(f32[512]{0:T(512)} %param.13) | copy-start | bytes 6148
  445.7 41.0 %collective-permute-start.21 = (f32[4,512,256]{2,1,0:T(8,128)}, f32[4,512,256]{2,1,0:T(8,128)}, u32[]{:S(2)}, u32[]{:S(2)}) collective-permute-start(f32[4,512,256]{2,1,0:T(8,128)} %get-tuple-element.156), channel_id=1, source_target_pairs={{0,1},{1,0},{2,3},{3,2},{4,5},{5,4},{6,7},{7,6},{8,9},{9,8},{10,11... | collective-permute-start | bytes 6291464 | tf_op jit(solution)/shard_map/ppermute | solution.py:455
  448.0 30.9 %copy-start.10 = (f32[512,256]{1,0:T(8,128)}, f32[512,256]{1,0:T(8,128)S(1)}, u32[]{:S(2)}) copy-start(f32[512,256]{1,0:T(8,128)S(1)} %collective-permute-done.22.refs_1_) | copy-start | bytes 1572868
  478.9 0.8 copy-start.11
  478.9 1.0 copy-start.13
  484.4 45.8 %collective-permute-start.25 = (f32[4,512,256]{2,1,0:T(8,128)}, f32[4,512,256]{2,1,0:T(8,128)}, u32[]{:S(2)}, u32[]{:S(2)}) collective-permute-start(f32[4,512,256]{2,1,0:T(8,128)} %get-tuple-element.167.refs_0_), channel_id=1, source_target_pairs={{0,2},{1,3},{2,0},{3,1},{4,6},{5,7},{6,4},{7,5},{8,10},{9,11},{10,... | collective-permute-start | bytes 6291464 | tf_op jit(solution)/shard_map/ppermute | solution.py:450
  493.1 1.4 copy-start
  530.2 20.6 %copy-start.22 = (f32[8,128]{1,0:T(8,128)S(1)}, f32[8,128]{1,0:T(8,128)}, u32[]{:S(2)}) copy-start(f32[8,128]{1,0:T(8,128)} %get-tuple-element.163) | copy-start | bytes 12292
  530.2 20.6 %copy-start.23 = (f32[8,128]{1,0:T(8,128)S(1)}, f32[8,128]{1,0:T(8,128)}, u32[]{:S(2)}) copy-start(f32[8,128]{1,0:T(8,128)} %get-tuple-element.166) | copy-start | bytes 12292
  550.9 56.6 %collective-permute-start.26 = (f32[4,512,256]{2,1,0:T(8,128)}, f32[4,512,256]{2,1,0:T(8,128)S(1)}, u32[]{:S(2)}, u32[]{:S(2)}) collective-permute-start(f32[4,512,256]{2,1,0:T(8,128)} %get-tuple-element.174), channel_id=1, source_target_pairs={{0,1},{1,0},{2,3},{3,2},{4,5},{5,4},{6,7},{7,6},{8,9},{9,8},{10,11... | collective-permute-start | bytes 6291464 | tf_op jit(solution)/shard_map/ppermute | solution.py:455
  551.6 46.8 %all-to-all-start.3 = ((f32[32,16,128]{2,1,0:T(8,128)}), f32[32,16,128]{2,1,0:T(8,128)S(1)}, u32[]{:S(2)}, u32[]{:S(2)}) async-start(f32[32,16,128]{2,1,0:T(8,128)} %broadcast_in_dim.9), calls=%async_computation.3 | async-start | bytes 524288 | tf_op jit(solution)/shard_map/all_to_all | solution.py:460
  565.6 61.3 %collective-permute-start.17 = (f32[512,256]{1,0:T(8,128)}, f32[512,256]{1,0:T(8,128)S(1)}, u32[]{:S(2)}, u32[]{:S(2)}) collective-permute-start(f32[512,256]{1,0:T(8,128)} %get-tuple-element.150), channel_id=1, source_target_pairs={{0,8},{4,12},{8,16},{12,20},{16,24},{20,28},{24,0},{28,4},{1,9},{5... | collective-permute-start | bytes 1572872 | tf_op jit(solution)/shard_map/ppermute | solution.py:432
  567.4 59.5 %collective-permute-start.18 = (f32[512,256]{1,0:T(8,128)}, f32[512,256]{1,0:T(8,128)S(1)}, u32[]{:S(2)}, u32[]{:S(2)}) collective-permute-start(f32[512,256]{1,0:T(8,128)} %get-tuple-element.151), channel_id=1, source_target_pairs={{0,16},{4,20},{8,24},{12,28},{16,0},{20,4},{24,8},{28,12},{1,17},{... | collective-permute-start | bytes 1572872 | tf_op jit(solution)/shard_map/ppermute | solution.py:432
  569.8 57.1 %collective-permute-start.19 = (f32[512,256]{1,0:T(8,128)}, f32[512,256]{1,0:T(8,128)}, u32[]{:S(2)}, u32[]{:S(2)}) collective-permute-start(f32[512,256]{1,0:T(8,128)} %get-tuple-element.152), channel_id=1, source_target_pairs={{0,24},{4,28},{8,0},{12,4},{16,8},{20,12},{24,16},{28,20},{1,25},{... | collective-permute-start | bytes 1572872 | tf_op jit(solution)/shard_map/ppermute | solution.py:432
  598.4 0.7 copy-start.4
  607.5 1.3 copy-start.3
  616.5 17.2 %all-to-all-start.5 = ((f32[32,8,128]{2,1,0:T(8,128)}), f32[32,8,128]{2,1,0:T(8,128)S(1)}, u32[]{:S(2)}, u32[]{:S(2)}) async-start(f32[32,8,128]{2,1,0:T(8,128)} %broadcast_in_dim.11), calls=%async_computation.5 | async-start | bytes 262144 | tf_op jit(solution)/shard_map/all_to_all | solution.py:460
  626.9 0.8 copy-start.5
  626.9 1.0 copy-start.6
  633.7 7.2 %copy-start.8 = (f32[32,8,128]{2,1,0:T(8,128)}, f32[32,8,128]{2,1,0:T(8,128)S(1)}, u32[]{:S(2)}) copy-start(f32[32,8,128]{2,1,0:T(8,128)S(1)} %all-to-all-done.5.refs_0_) | copy-start | bytes 393220
  635.0 14.2 %all-to-all-start.4 = ((f32[32,8,128]{2,1,0:T(8,128)}), f32[32,8,128]{2,1,0:T(8,128)S(1)}, u32[]{:S(2)}, u32[]{:S(2)}) async-start(f32[32,8,128]{2,1,0:T(8,128)} %broadcast_in_dim.10), calls=%async_computation.4 | async-start | bytes 262144 | tf_op jit(solution)/shard_map/all_to_all | solution.py:460
  649.2 0.6 copy-start.9

commit v3 on v2

--- a/solution.py
+++ b/solution.py
@@ -25,7 +25,7 @@
         self.place = place
         self.token = None
 
-    def __call__(self, body, name, grid, operands, in_specs, outs, out_specs, scratch=(), aliases=()):
+    def __call__(self, body, name, grid, operands, in_specs, outs, out_specs, scratch=(), aliases=(), bytes_hint=0):
         operands, in_specs = list(operands), list(in_specs)
         n_in, n_tok = len(operands), 0 if self.token is None else 1
         if n_tok:
@@ -49,7 +49,7 @@
             out_shape=[jax.ShapeDtypeStruct(*out) for out in outs] + [jax.ShapeDtypeStruct((8, 128), F32)],
             input_output_aliases={1 + k: v for k, v in aliases},
             compiler_params=pltpu.CompilerParams(vmem_limit_bytes=60 << 20),
-            cost_estimate=pl.CostEstimate(flops=0, bytes_accessed=0, transcendentals=0),
+            cost_estimate=pl.CostEstimate(flops=1150*bytes_hint, bytes_accessed=bytes_hint, transcendentals=0),
             name=name,
         )(self.place, *operands)
         self.token = found[-1]
@@ -117,32 +117,36 @@
     )[0]
 
 
-def add_call(chain, terms):
+def add_call(chain, terms, together):
     parts, s_loc, width = terms[0].shape
     rows = s_loc // CHUNKS
 
     def body(place, *refs):
         for k in range(parts):
-            block = lax.rem(place[0] + k, parts)
+            block = k if together else lax.rem(place[0] + k, parts)
             total = refs[0][block]
             for term in refs[1 : len(terms)]:
                 total = total + term[block]
-            refs[len(terms) + k][...] = total
-
+            if together:
+                refs[len(terms)][k] = total
+            else:
+                refs[len(terms) + k][...] = total
+
+    if together:
+        outs, specs = [((parts, s_loc, width), F32)], [rows_spec(parts, rows, width)]
+    else:
+        outs, specs = [((s_loc, width), F32)] * parts, [rows_spec(rows, width)] * parts
+    found = chain(body, "add", (CHUNKS,), terms, [rows_spec(parts, rows, width)] * len(terms), outs, specs)
+    return found[0] if together else found
+
+
+def gate_call(chain, *arrays):
+    anywhere = [pl.BlockSpec(memory_space=pl.ANY)] * len(arrays)
+    outs = [(array.shape, array.dtype) for array in arrays]
+    same = [(k, k) for k in range(len(arrays))]
     return chain(
-        body,
-        "add",
-        (CHUNKS,),
-        terms,
-        [rows_spec(parts, rows, width)] * len(terms),
-        [((s_loc, width), F32)] * parts,
-        [rows_spec(rows, width)] * parts,
-    )
-
-
-def gate_call(chain, array):
-    hbm = pl.BlockSpec(memory_space=HBM)
-    return chain(lambda place, a, b: None, "gate", (), [array], [hbm], [(array.shape, array.dtype)], [hbm], aliases=[(0, 0)])[0]
+        lambda place, *refs: None, "gate", (), arrays, anywhere, outs, anywhere, aliases=same, bytes_hint=20 << 20
+    )
 
 
 def entries_call(chain, table, unit, n_rows, n_cols, row_block, col_block, reach, order, name, halves=(0, 1), earlier=()):
@@ -333,7 +337,7 @@
                 yield columns_of(place, k, -1, self.parts, self.width), refs[k][...]
 
 
-def sums_call(chain, observed, noise, residual, direction, outer, probe):
+def sums_call(chain, observed, noise, residual, direction, outer, probe, bytes_hint=0):
     _, s_loc, t_loc = direction.shape
     rows = s_loc // CHUNKS
     n = len(outer.operands)
@@ -366,6 +370,7 @@
         [((8, 128), F32)],
         [pl.BlockSpec((8, 128), lambda i, place: (0, 0))],
         scratch=[pltpu.VMEM((8, outer.width), F32)],
+        bytes_hint=bytes_hint,
     )[0]
 
 
@@ -488,8 +493,8 @@
 
     noise = noise[:, None]
 
-    def sums(outer, p):
-        return sums_call(chain, observed, noise, residual, direction, outer, p)
+    def sums(outer, p, hint=0):
+        return sums_call(chain, observed, noise, residual, direction, outer, p, hint)
 
     def update(stats, row, outer, p, earlier):
         return update_call(chain, stats, row, observed, noise, solution, residual, direction, outer, p, earlier)
@@ -497,42 +502,76 @@
     def mask(p, together):
         return mask_call(chain, observed, direction, p, n_z, together)
 
-    out0 = over_z(mask(0, False))
-    x2 = over_x(mask(2, True))
-    out1 = over_z_at_once(mask(1, True))
+    def pass_on(*groups):
+        flat = iter(gate_call(chain, *[array for group in groups for array in group]))
+        return [[next(flat) for _ in group] for group in groups]
+
+    mask0 = mask(0, False)
+    mask2 = mask(2, True)
+    out0 = over_z(mask0)
+    x2 = over_x(mask2)
+    mask1 = mask(1, True)
+    mask3 = mask(3, True)
     time = entries_call(chain, day_features, t_loc, n_x, n_c, time_row, time_col, time_range, DAYS, "time_entries")
-    x3 = over_x(mask(3, True))
-    out2 = over_z(add_call(chain, days(x2)))
-    cells0 = over_y(stack_call(chain, out0))
-    matrices = [space_entries(0, (0, 2), ())]
-    cells1 = over_y(gate_call(chain, out1))
-    out3 = days(x3)
-    matrices[0] = space_entries(0, (1, 2), matrices[0])
-    out3 = over_z(add_call(chain, out3))
+    matrices = [space_entries(0, (0, 1), ())]
+    cells0 = stack_call(chain, out0)
+    (mask1,), (mask3,), x2 = pass_on([mask1], [mask3], x2[1:])
+
+    out1 = over_z_at_once(mask1)
+    x3 = over_x(mask3)
+    y0 = over_y(cells0)
+    terms2 = time_call(chain, [mask2] + x2, time, n_c)
     for k in range(1, n_y):
         matrices.append(space_entries(k, (0, 1), ()))
-    cells2 = over_y(stack_call(chain, out2))
-    home0 = over_z_at_once(space(cells0, True))
-    cells3 = over_y(stack_call(chain, out3))
-    home1 = over_z(space(cells1, False))
-    x0 = over_x(gate_call(chain, home0))
-    home2 = over_z_at_once(space(cells2, True))
-    home3 = over_z(space(cells3, False))
-    outer0 = days(x0)
-    x1 = over_x(stack_call(chain, home1))
-    outer0 = Outer(outer0)
+    x3, y0 = pass_on(x3[1:], y0[1:])
+    inner2 = add_call(chain, over_core(terms2), True)
+    (cells1,), (inner2,) = pass_on([out1], [inner2])
+
+    out2 = over_z_at_once(inner2)
+    y1 = over_y(cells1)
+    terms3 = time_call(chain, [mask3] + x3, time, n_c)
+    smooth0 = space([cells0] + y0, False)
+    (y1,) = pass_on(y1[1:])
+    inner3 = add_call(chain, over_core(terms3), False)
+    (cells2,), inner3, smooth0 = pass_on([out2], inner3, smooth0)
+
+    out3 = over_z(inner3)
+    y2 = over_y(cells2)
+    smooth1 = space([cells1] + y1, False)
+    cells3 = stack_call(chain, out3)
+    y2, smooth0, smooth1 = pass_on(y2[1:], smooth0, smooth1)
+
+    home0 = over_z(smooth0)
+    y3 = over_y(cells3)
+    smooth2 = space([cells2] + y2, False)
+    home0 = stack_call(chain, home0)
+    y3, smooth1, smooth2 = pass_on(y3[1:], smooth1, smooth2)
+
+    home1 = over_z(smooth1)
+    x0 = over_x(home0)
+    smooth3 = space([cells3] + y3, False)
+    home1 = stack_call(chain, home1)
+    x0, smooth2, smooth3 = pass_on(x0[1:], smooth2, smooth3)
+
+    home2 = over_z(smooth2)
+    x1 = over_x(home1)
+    terms0 = time_call(chain, [home0] + x0, time, n_c)
+    home2, x1, terms0, smooth3 = pass_on(home2, x1[1:], terms0, smooth3)
+
+    home3 = over_z(smooth3)
+    outer0 = Outer(over_core(terms0))
+    outer2 = Outer(home2)
+    sums2 = sums(outer2, 2)
     sums0 = sums(outer0, 0)
-    outer2 = Outer([home2])
-    stats02 = over_all(sums0, sums(outer2, 2))
-    outer1 = days(x1)
-    new = update(stats02, 0, outer0, 0, ())
-    outer1 = Outer(outer1)
-    stats1 = over_all(sums(outer1, 1))
-    new = update(stats02, 1, outer2, 2, new)
+    terms1 = time_call(chain, [home1] + x1, time, n_c)
+    outer1 = Outer(over_core(terms1))
     outer3 = Outer(home3)
-    stats3 = over_all(sums(outer3, 3))
-    new = update(stats1, 0, outer1, 1, new)
-    new = update(stats3, 0, outer3, 3, new)
+    sums3 = sums(outer3, 3, 200 << 20)
+    sums1 = sums(outer1, 1)
+    stats = over_all(sums0, sums1, sums2, sums3)
+    new = ()
+    for p, outer in enumerate((outer0, outer1, outer2, outer3)):
+        new = update(stats, p, outer, p, new)
     return tuple(new)
 
 

time: 660 us -> 522 us (0.79)
  waiting for transfers between devices: 203 us -> 51.2 us
  blocking collectives: 0 us -> 29.1 us
  starting transfers between devices: 102 us -> 83.5 us
    ppermute x15 -> x18, waiting for transfers between devices: 136 us -> 45 us  [over_z(): found.append(lax.ppermute(pieces[k], 'sta', pairs))]
    ppermute x4, waiting for transfers between devices: 39 us -> 3.38 us  [over_x(): found.append(lax.ppermute(cells, 'day', pairs))]
    all_to_all x0 -> x1, blocking collectives: none -> 29.1 us  [over_all(): return lax.all_to_all(many, ('sta', 'day'), 0, 0, tiled=True)]
    ppermute x15 -> x18, starting transfers between devices: 36.7 us -> 65.5 us  [over_z(): found.append(lax.ppermute(pieces[k], 'sta', pairs))]
    all_to_all x3 -> x0, waiting for transfers between devices: 27.2 us -> none  [over_all(): return lax.all_to_all(many, ('sta', 'day'), 0, 0, tiled=True)]
    all_to_all x3 -> x2, starting transfers between devices: 31.6 us -> 8.24 us  [over_z_at_once(): lax.all_to_all(pieces, 'sta', 0, 0, axis_index_groups=groups, tiled=True)]
    all_to_all x3 -> x0, starting transfers between devices: 22.4 us -> none  [over_all(): return lax.all_to_all(many, ('sta', 'day'), 0, 0, tiled=True)]
    pallas_call x32 -> x38, Pallas kernels: 335 us -> 339 us  [__call__(): pl.pallas_call(kernel, grid_spec=pltpu.PrefetchScalarGridSpec(num_scalar_...]
  transfers between devices with their start and end apart: 33 -> 32, of which waited for: 9 -> 8; matrix products, arithmetic and copies ran while one was open for 0% -> 0% of each run, Pallas kernels for 39% -> 55%
where the time goes in v3:
time: 522 us; the launch traced here: 520 us
  Pallas kernels  339 us (65%)
  starting transfers between devices  83.5 us (16%)
  waiting for transfers between devices  51.2 us (10%)
  blocking collectives  29.1 us (6%)
  local copies, waits for them, and re-layouts  15.1 us (3%)
    pallas_call x38, Pallas kernels, __call__(): pl.pallas_call(kernel, grid_spec=pltpu.PrefetchScalarGridSpec(num_scalar_...  339 us
    ppermute x18, starting transfers between devices, over_z(): found.append(lax.ppermute(pieces[k], 'sta', pairs))  65.5 us
    ppermute x18, waiting for transfers between devices, over_z(): found.append(lax.ppermute(pieces[k], 'sta', pairs))  45 us
    all_to_all x1, blocking collectives, over_all(): return lax.all_to_all(many, ('sta', 'day'), 0, 0, tiled=True)  29.1 us
    unnamed x54, local copies, waits for them, and re-layouts  14.2 us
  transfers between devices with their start and end apart: 32, of which 8 were waited for; matrix products, arithmetic and copies ran while one was open for 0% of the time, Pallas kernels for 55%

profile of v3, /device:TPU:0, one launch (start us, length us, event | category | flops | bytes accessed | tf_op | source)
XLA Modules:
  0.0 520.0 jit_solution(10114621917565454235)
XLA Ops:
  1.2 4.9 mask.4
  6.2 4.9 mask.5
  11.1 2.9 collective-permute-start
  14.0 1.6 collective-permute-start.1
  15.6 2.6 collective-permute-start.2
  18.2 1.3 collective-permute-start.3
  19.5 4.9 mask.6
  24.4 4.9 mask.7
  29.3 22.3 %time_entries.1 = (bf16[2048,2048]{1,0:T(8,128)(2,1)}, bf16[2048,2048]{1,0:T(8,128)(2,1)}, f32[8,128]{1,0:T(8,128)}) custom-call(s32[4]{0:T(128)} %pad_add_fusion.place, f32[4,4096]{1,0:T(4,128)} %refs_1_.15, f32[4,4096]{1,0:T(4,128)} %refs_1_.15, f32[8,128]{1,0:T(8,128)} %get-tuple-element.167.refs_2_), custom_call_target="tpu_custom_call" | custom-call | tf_op jit(solution)/shard_map/time_entries/pallas_call | solution.py:40
  51.6 17.4 %space_entries.2 = (bf16[2048,2048]{1,0:T(8,128)(2,1)}, bf16[2048,2048]{1,0:T(8,128)(2,1)}, f32[8,128]{1,0:T(8,128)}) custom-call(s32[4]{0:T(128)} %pad_add_fusion.place, f32[2,4096]{1,0:T(2,128)} %refs_3_.11, f32[2,4096]{1,0:T(2,128)} %refs_3_.11, f32[2,4096]{1,0:T(2,128)} %refs_3_.11, f32[2,4096]{1,0:T(2,128)} %refs_3_.11, f32[8,128]{1,0:T(8,128)} %get-tuple-element.168.refs_4_), custom_call_target="tpu_custom_call" | custom-call | tf_op jit(solution)/shard_map/space_entries/pallas_call | solution.py:40
  70.3 4.5 stack.24
  74.8 1.5 collective-permute-start.6
  76.3 1.4 copy-done.7
  79.0 3.6 all-to-all-start
  82.6 20.4 %time.4 = (f32[4,512,256]{2,1,0:T(8,128)}, f32[4,512,256]{2,1,0:T(8,128)}, f32[8,128]{1,0:T(8,128)}) custom-call(s32[4]{0:T(128)} %pad_add_fusion.place, f32[4,512,256]{2,1,0:T(8,128)} %get-tuple-element.162.refs_0_, f32[4,512,256]{2,1,0:T(8,128)} %get-tuple-element.172.refs_1_, bf16[2048,2048]{1,0:T(8,128)(2,1)} %get-tuple-element.173.refs_2_, ...), custom_call_target="tpu_custom_call" | custom-call | tf_op jit(solution)/shard_map/time/pallas_call | solution.py:40
  103.0 17.5 %space_entries.3 = (bf16[2048,2048]{1,0:T(8,128)(2,1)}, bf16[2048,2048]{1,0:T(8,128)(2,1)}, f32[8,128]{1,0:T(8,128)}) custom-call(s32[4]{0:T(128)} %pad_add_fusion.place, f32[2,4096]{1,0:T(2,128)} %refs_3_.11, f32[2,4096]{1,0:T(2,128)} %refs_3_.11, f32[2,4096]{1,0:T(2,128)} %refs_3_.11, f32[2,4096]{1,0:T(2,128)} %refs_3_.11, f32[8,128]{1,0:T(8,128)} %get-tuple-element.180.refs_4_), custom_call_target="tpu_custom_call" | custom-call | tf_op jit(solution)/shard_map/space_entries/pallas_call | solution.py:40
  120.5 0.9 collective-permute-done.6.refs_1_
  121.4 3.4 collective-permute-done.5.refs_0_
  125.4 4.9 add.19
  130.3 1.3 copy-done.2
  132.8 4.6 all-to-all-start.1
  137.5 20.5 %time.5 = (f32[4,512,256]{2,1,0:T(8,128)}, f32[4,512,256]{2,1,0:T(8,128)}, f32[8,128]{1,0:T(8,128)}) custom-call(s32[4]{0:T(128)} %pad_add_fusion.place, f32[4,512,256]{2,1,0:T(8,128)} %get-tuple-element.178.refs_0_, f32[4,512,256]{2,1,0:T(8,128)} %get-tuple-element.186.refs_1_, bf16[2048,2048]{1,0:T(8,128)(2,1)} %get-tuple-element.173.refs_2_, ...), custom_call_target="tpu_custom_call" | custom-call | tf_op jit(solution)/shard_map/time/pallas_call | solution.py:40
  157.9 22.0 %space.4 = (f32[512,256]{1,0:T(8,128)}, f32[512,256]{1,0:T(8,128)}, f32[512,256]{1,0:T(8,128)}, f32[512,256]{1,0:T(8,128)}, f32[8,128]{1,0:T(8,128)}) custom-call(s32[4]{0:T(128)} %pad_add_fusion.place, f32[4,512,256]{2,1,0:T(8,128)} %get-tuple-element.179.refs_0_, f32[4,512,256]{2,1,0:T(8,128)} %get-tuple-element.191.refs_1_, ...), custom_call_target="tpu_custom_call" | custom-call | tf_op jit(solution)/shard_map/space/pallas_call | solution.py:40
  180.6 4.9 add.20
  185.7 1.4 copy-done.1
  187.8 1.6 collective-permute-start.9
  189.3 1.8 collective-permute-start.10
  191.2 2.4 collective-permute-start.11
  193.6 1.5 collective-permute-start.12
  195.0 22.0 %space.5 = (f32[512,256]{1,0:T(8,128)}, f32[512,256]{1,0:T(8,128)}, f32[512,256]{1,0:T(8,128)}, f32[512,256]{1,0:T(8,128)}, f32[8,128]{1,0:T(8,128)}) custom-call(s32[4]{0:T(128)} %pad_add_fusion.place, f32[4,512,256]{2,1,0:T(8,128)} %get-tuple-element.190.refs_0_, f32[4,512,256]{2,1,0:T(8,128)} %get-tuple-element.213.refs_1_, ...), custom_call_target="tpu_custom_call" | custom-call | tf_op jit(solution)/shard_map/space/pallas_call | solution.py:40
  217.0 11.1 %collective-permute-done.11.refs_2_ = f32[512,256]{1,0:T(8,128)S(1)} collective-permute-done((f32[512,256]{1,0:T(8,128)}, f32[512,256]{1,0:T(8,128)S(1)}, u32[]{:S(2)}, u32[]{:S(2)}) %collective-permute-start.11) | collective-permute-done | bytes 524320 | tf_op jit(solution)/shard_map/ppermute | solution.py:437
  229.1 4.5 stack.25
  234.1 1.8 collective-permute-done.9.refs_0_
  235.9 1.3 copy-done.8
  237.9 9.8 %collective-permute-start.13 = (f32[512,256]{1,0:T(8,128)}, f32[512,256]{1,0:T(8,128)S(1)}, u32[]{:S(2)}, u32[]{:S(2)}) collective-permute-start(f32[512,256]{1,0:T(8,128)} %get-tuple-element.226), channel_id=1, source_target_pairs={{0,8},{4,12},{8,16},{12,20},{16,24},{20,28},{24,0},{28,4},{1,9},{5... | collective-permute-start | bytes 1572872 | tf_op jit(solution)/shard_map/ppermute | solution.py:437
  247.7 1.9 collective-permute-start.14
  250.1 22.0 %space.6 = (f32[512,256]{1,0:T(8,128)}, f32[512,256]{1,0:T(8,128)}, f32[512,256]{1,0:T(8,128)}, f32[512,256]{1,0:T(8,128)}, f32[8,128]{1,0:T(8,128)}) custom-call(s32[4]{0:T(128)} %pad_add_fusion.place, f32[4,512,256]{2,1,0:T(8,128)} %get-tuple-element.208.refs_0_, f32[4,512,256]{2,1,0:T(8,128)} %get-tuple-element.229.refs_1_, ...), custom_call_target="tpu_custom_call" | custom-call | tf_op jit(solution)/shard_map/space/pallas_call | solution.py:40
  272.2 10.9 %collective-permute-done.14.refs_2_ = f32[512,256]{1,0:T(8,128)S(1)} collective-permute-done((f32[512,256]{1,0:T(8,128)}, f32[512,256]{1,0:T(8,128)S(1)}, u32[]{:S(2)}, u32[]{:S(2)}) %collective-permute-start.14) | collective-permute-done | bytes 524320 | tf_op jit(solution)/shard_map/ppermute | solution.py:437
  284.0 4.5 stack.26
  288.6 1.5 collective-permute-start.16
  290.7 11.6 %collective-permute-start.18 = (f32[512,256]{1,0:T(8,128)}, f32[512,256]{1,0:T(8,128)S(1)}, u32[]{:S(2)}, u32[]{:S(2)}) collective-permute-start(f32[512,256]{1,0:T(8,128)} %get-tuple-element.254), channel_id=1, source_target_pairs={{0,8},{4,12},{8,16},{12,20},{16,24},{20,28},{24,0},{28,4},{1,9},{5... | collective-permute-start | bytes 1572872 | tf_op jit(solution)/shard_map/ppermute | solution.py:437
  302.3 1.8 collective-permute-start.19
  304.7 22.0 %space.7 = (f32[512,256]{1,0:T(8,128)}, f32[512,256]{1,0:T(8,128)}, f32[512,256]{1,0:T(8,128)}, f32[512,256]{1,0:T(8,128)}, f32[8,128]{1,0:T(8,128)}) custom-call(s32[4]{0:T(128)} %pad_add_fusion.place, f32[4,512,256]{2,1,0:T(8,128)} %get-tuple-element.233.refs_0_, f32[4,512,256]{2,1,0:T(8,128)} %get-tuple-element.247.refs_1_, ...), custom_call_target="tpu_custom_call" | custom-call | tf_op jit(solution)/shard_map/space/pallas_call | solution.py:40
  326.8 10.6 %collective-permute-done.19.refs_2_ = f32[512,256]{1,0:T(8,128)S(1)} collective-permute-done((f32[512,256]{1,0:T(8,128)}, f32[512,256]{1,0:T(8,128)S(1)}, u32[]{:S(2)}, u32[]{:S(2)}) %collective-permute-start.19) | collective-permute-done | bytes 524320 | tf_op jit(solution)/shard_map/ppermute | solution.py:437
  338.3 4.5 stack.27
  343.4 1.3 copy-done.6
  345.4 11.6 %collective-permute-start.21 = (f32[512,256]{1,0:T(8,128)}, f32[512,256]{1,0:T(8,128)S(1)}, u32[]{:S(2)}, u32[]{:S(2)}) collective-permute-start(f32[512,256]{1,0:T(8,128)} %get-tuple-element.260), channel_id=1, source_target_pairs={{0,8},{4,12},{8,16},{12,20},{16,24},{20,28},{24,0},{28,4},{1,9},{5... | collective-permute-start | bytes 1572872 | tf_op jit(solution)/shard_map/ppermute | solution.py:437
  356.9 2.1 collective-permute-start.22
  359.4 20.5 %time.6 = (f32[4,512,256]{2,1,0:T(8,128)}, f32[4,512,256]{2,1,0:T(8,128)}, f32[8,128]{1,0:T(8,128)}) custom-call(s32[4]{0:T(128)} %pad_add_fusion.place, f32[4,512,256]{2,1,0:T(8,128)} %get-tuple-element.232.refs_0_, f32[4,512,256]{2,1,0:T(8,128)} %get-tuple-element.264.refs_1_, bf16[2048,2048]{1,0:T(8,128)(2,1)} %get-tuple-element.173.refs_2_, ...), custom_call_target="tpu_custom_call" | custom-call | tf_op jit(solution)/shard_map/time/pallas_call | solution.py:40
  379.8 12.5 %collective-permute-done.22.refs_2_ = f32[512,256]{1,0:T(8,128)S(1)} collective-permute-done((f32[512,256]{1,0:T(8,128)}, f32[512,256]{1,0:T(8,128)S(1)}, u32[]{:S(2)}, u32[]{:S(2)}) %collective-permute-start.22) | collective-permute-done | bytes 524320 | tf_op jit(solution)/shard_map/ppermute | solution.py:437
  394.2 11.6 %collective-permute-start.27 = (f32[512,256]{1,0:T(8,128)}, f32[512,256]{1,0:T(8,128)S(1)}, u32[]{:S(2)}, u32[]{:S(2)}) collective-permute-start(f32[512,256]{1,0:T(8,128)} %get-tuple-element.287), channel_id=1, source_target_pairs={{0,8},{4,12},{8,16},{12,20},{16,24},{20,28},{24,0},{28,4},{1,9},{5... | collective-permute-start | bytes 1572872 | tf_op jit(solution)/shard_map/ppermute | solution.py:437
  405.7 1.8 collective-permute-start.28
  408.2 0.9 copy.75.refs_1_.refs_2_
  409.1 5.8 %sums.4 = (f32[8,128]{1,0:T(8,128)}, f32[8,128]{1,0:T(8,128)}) custom-call(s32[4]{0:T(128)} %pad_add_fusion.place, s32[512,1024]{1,0:T(8,128)} %refs_1_.21, f32[512,1]{1,0:T(8,128)} %copy.75.refs_1_.refs_2_, f32[4,512,1024]{2,1,0:T(8,128)} %refs_4_.7, f32[4,512,1024]{2,1,0:T(8,128)} %refs_5_.7, f32[512,256]{1,0:T(8,128)} %get-tuple-element.275.refs_4_.refs_6_, ...), custom_call_target="tpu_custom_call" | custom-call | tf_op jit(solution)/shard_map/sums/pallas_call | solution.py:40
  414.8 1.4 copy-done
  416.2 6.3 %sums.5 = (f32[8,128]{1,0:T(8,128)}, f32[8,128]{1,0:T(8,128)}) custom-call(s32[4]{0:T(128)} %pad_add_fusion.place, s32[512,1024]{1,0:T(8,128)} %refs_1_.21, f32[512,1]{1,0:T(8,128)} %copy.75.refs_1_.refs_2_, f32[4,512,1024]{2,1,0:T(8,128)} %refs_4_.7, f32[4,512,1024]{2,1,0:T(8,128)} %refs_5_.7, f32[4,512,256]{2,1,0:T(8,128)} %get-tuple-element.273.refs_4_.refs_6_, ...), custom_call_target="tpu_custom_call" | custom-call | tf_op jit(solution)/shard_map/sums/pallas_call | solution.py:40
  422.6 20.4 %time.7 = (f32[4,512,256]{2,1,0:T(8,128)}, f32[4,512,256]{2,1,0:T(8,128)}, f32[8,128]{1,0:T(8,128)}) custom-call(s32[4]{0:T(128)} %pad_add_fusion.place, f32[4,512,256]{2,1,0:T(8,128)} %get-tuple-element.263.refs_0_, f32[4,512,256]{2,1,0:T(8,128)} %get-tuple-element.282.refs_1_, bf16[2048,2048]{1,0:T(8,128)(2,1)} %get-tuple-element.173.refs_2_, ...), custom_call_target="tpu_custom_call" | custom-call | tf_op jit(solution)/shard_map/time/pallas_call | solution.py:40
  444.0 5.8 %sums.6 = (f32[8,128]{1,0:T(8,128)}, f32[8,128]{1,0:T(8,128)}) custom-call(s32[4]{0:T(128)} %pad_add_fusion.place, s32[512,1024]{1,0:T(8,128)} %refs_1_.21, f32[512,1]{1,0:T(8,128)} %copy.75.refs_1_.refs_2_, f32[4,512,1024]{2,1,0:T(8,128)} %refs_4_.7, f32[4,512,1024]{2,1,0:T(8,128)} %refs_5_.7, f32[512,256]{1,0:T(8,128)} %get-tuple-element.286.refs_4_.refs_6_, ...), custom_call_target="tpu_custom_call" | custom-call | flops 241172480000 | bytes 209715200 | tf_op jit(solution)/shard_map/sums/pallas_call | solution.py:40
  449.8 6.3 %sums.7 = (f32[8,128]{1,0:T(8,128)}, f32[8,128]{1,0:T(8,128)}) custom-call(s32[4]{0:T(128)} %pad_add_fusion.place, s32[512,1024]{1,0:T(8,128)} %refs_1_.21, f32[512,1]{1,0:T(8,128)} %copy.75.refs_1_.refs_2_, f32[4,512,1024]{2,1,0:T(8,128)} %refs_4_.7, f32[4,512,1024]{2,1,0:T(8,128)} %refs_5_.7, f32[4,512,256]{2,1,0:T(8,128)} %get-tuple-element.284.refs_4_.refs_6_, ...), custom_call_target="tpu_custom_call" | custom-call | tf_op jit(solution)/shard_map/sums/pallas_call | solution.py:40
  456.9 29.1 %all_to_all.15.refs_0_ = f32[32,32,128]{2,1,0:T(8,128)} all-to-all(f32[32,32,128]{2,1,0:T(8,128)S(1)} %broadcast_in_dim.10), channel_id=1, replica_groups=mesh['sta'=8,'day'=4] {'sta','day'}, dimensions={0} | all-to-all | bytes 1048576 | tf_op jit(solution)/shard_map/all_to_all | solution.py:465
  486.0 8.5 %update.4 = (f32[4,512,1024]{2,1,0:T(8,128)}, f32[4,512,1024]{2,1,0:T(8,128)}, f32[4,512,1024]{2,1,0:T(8,128)}, f32[8,128]{1,0:T(8,128)}) custom-call(s32[4]{0:T(128)} %pad_add_fusion.place, f32[32,32,128]{2,1,0:T(8,128)} %all_to_all.15.refs_0_, s32[512,1024]{1,0:T(8,128)} %refs_1_.21, f32[512,1]{1,0:T(8,128)} %copy.75.refs_1_.refs_2_, ...), custom_call_target="tpu_custom_call" | custom-call | tf_op jit(solution)/shard_map/update/pallas_call | solution.py:40
  494.4 8.5 %update.5 = (f32[4,512,1024]{2,1,0:T(8,128)}, f32[4,512,1024]{2,1,0:T(8,128)}, f32[4,512,1024]{2,1,0:T(8,128)}, f32[8,128]{1,0:T(8,128)}) custom-call(s32[4]{0:T(128)} %pad_add_fusion.place, f32[32,32,128]{2,1,0:T(8,128)} %all_to_all.15.refs_0_, s32[512,1024]{1,0:T(8,128)} %refs_1_.21, ...), custom_call_target="tpu_custom_call", output_to_operand_aliasing={{0}: (9, {}), {1}: (10, {}), {2}: (11, {})} | custom-call | tf_op jit(solution)/shard_map/update/pallas_call | solution.py:40
  502.9 8.5 %update.6 = (f32[4,512,1024]{2,1,0:T(8,128)}, f32[4,512,1024]{2,1,0:T(8,128)}, f32[4,512,1024]{2,1,0:T(8,128)}, f32[8,128]{1,0:T(8,128)}) custom-call(s32[4]{0:T(128)} %pad_add_fusion.place, f32[32,32,128]{2,1,0:T(8,128)} %all_to_all.15.refs_0_, s32[512,1024]{1,0:T(8,128)} %refs_1_.21, ...), custom_call_target="tpu_custom_call", output_to_operand_aliasing={{0}: (11, {}), {1}: (12, {}), {2}: (13, {})} | custom-call | tf_op jit(solution)/shard_map/update/pallas_call | solution.py:40
  511.4 8.5 %update.7 = (f32[4,512,1024]{2,1,0:T(8,128)}, f32[4,512,1024]{2,1,0:T(8,128)}, f32[4,512,1024]{2,1,0:T(8,128)}, f32[8,128]{1,0:T(8,128)}) custom-call(s32[4]{0:T(128)} %pad_add_fusion.place, f32[32,32,128]{2,1,0:T(8,128)} %all_to_all.15.refs_0_, s32[512,1024]{1,0:T(8,128)} %refs_1_.21, ...), custom_call_target="tpu_custom_call", output_to_operand_aliasing={{0}: (11, {}), {1}: (12, {}), {2}: (13, {})} | custom-call | tf_op jit(solution)/shard_map/update/pallas_call | solution.py:40
  (97 shorter events, 18.2 us)
Async XLA Ops:
  11.1 65.2 %collective-permute-start = (f32[4,512,256]{2,1,0:T(8,128)}, f32[4,512,256]{2,1,0:T(8,128)S(1)}, u32[]{:S(2)}, u32[]{:S(2)}) collective-permute-start(f32[4,512,256]{2,1,0:T(8,128)} %get-tuple-element.162.refs_0_), channel_id=1, source_target_pairs={{0,2},{1,3},{2,0},{3,1},{4,6},{5,7},{6,4},{7,5},{8,10},{9,11},{10,... | collective-permute-start | bytes 6291464 | tf_op jit(solution)/shard_map/ppermute | solution.py:455
  14.0 55.0 %collective-permute-start.1 = (f32[512,256]{1,0:T(8,128)}, f32[512,256]{1,0:T(8,128)S(1)}, u32[]{:S(2)}, u32[]{:S(2)}) collective-permute-start(f32[512,256]{1,0:T(8,128)} %get-tuple-element.164), channel_id=1, source_target_pairs={{0,8},{4,12},{8,16},{12,20},{16,24},{20,28},{24,0},{28,4},{1,9},{5... | collective-permute-start | bytes 1572872 | tf_op jit(solution)/shard_map/ppermute | solution.py:437
  15.6 53.5 %collective-permute-start.2 = (f32[512,256]{1,0:T(8,128)}, f32[512,256]{1,0:T(8,128)S(1)}, u32[]{:S(2)}, u32[]{:S(2)}) collective-permute-start(f32[512,256]{1,0:T(8,128)} %get-tuple-element.165), channel_id=1, source_target_pairs={{0,16},{4,20},{8,24},{12,28},{16,0},{20,4},{24,8},{28,12},{1,17},{... | collective-permute-start | bytes 1572872 | tf_op jit(solution)/shard_map/ppermute | solution.py:437
  18.2 50.9 %collective-permute-start.3 = (f32[512,256]{1,0:T(8,128)}, f32[512,256]{1,0:T(8,128)S(1)}, u32[]{:S(2)}, u32[]{:S(2)}) collective-permute-start(f32[512,256]{1,0:T(8,128)} %get-tuple-element.166), channel_id=1, source_target_pairs={{0,24},{4,28},{8,0},{12,4},{16,8},{20,12},{24,16},{28,20},{1,25},{... | collective-permute-start | bytes 1572872 | tf_op jit(solution)/shard_map/ppermute | solution.py:437
  69.0 0.8 copy-start.11
  69.1 1.0 copy-start.12
  69.1 1.2 copy-start.13
  74.8 46.6 %collective-permute-start.6 = (f32[4,512,256]{2,1,0:T(8,128)}, f32[4,512,256]{2,1,0:T(8,128)}, u32[]{:S(2)}, u32[]{:S(2)}) collective-permute-start(f32[4,512,256]{2,1,0:T(8,128)} %get-tuple-element.179.refs_0_), channel_id=1, source_target_pairs={{0,4},{4,0},{8,12},{12,8},{16,20},{20,16},{24,28},{28,24},{1,5},{5... | collective-permute-start | bytes 6291464 | tf_op jit(solution)/shard_map/ppermute | solution.py:448
  76.3 1.4 copy-start.7
  78.4 46.4 %collective-permute-start.5 = (f32[4,512,256]{2,1,0:T(8,128)}, f32[4,512,256]{2,1,0:T(8,128)}, u32[]{:S(2)}, u32[]{:S(2)}) collective-permute-start(f32[4,512,256]{2,1,0:T(8,128)} %get-tuple-element.178.refs_0_), channel_id=1, source_target_pairs={{0,2},{1,3},{2,0},{3,1},{4,6},{5,7},{6,4},{7,5},{8,10},{9,11},{10,... | collective-permute-start | bytes 6291464 | tf_op jit(solution)/shard_map/ppermute | solution.py:455
  79.0 51.3 %all-to-all-start = ((f32[4,512,256]{2,1,0:T(8,128)}), f32[4,512,256]{2,1,0:T(8,128)S(1)}, u32[]{:S(2)}, u32[]{:S(2)}) async-start(f32[4,512,256]{2,1,0:T(8,128)} %get-tuple-element.171), calls=%async_computation | async-start | bytes 4194304 | tf_op jit(solution)/shard_map/all_to_all | solution.py:442
  120.5 4.9 collective-permute-start.4
  130.3 1.3 copy-start.2
  132.3 47.7 %collective-permute-start.8 = (f32[4,512,256]{2,1,0:T(8,128)}, f32[4,512,256]{2,1,0:T(8,128)}, u32[]{:S(2)}, u32[]{:S(2)}) collective-permute-start(f32[4,512,256]{2,1,0:T(8,128)} %get-tuple-element.190.refs_0_), channel_id=1, source_target_pairs={{0,4},{4,0},{8,12},{12,8},{16,20},{20,16},{24,28},{28,24},{1,5},{5... | collective-permute-start | bytes 6291464 | tf_op jit(solution)/shard_map/ppermute | solution.py:448
  132.8 52.8 %all-to-all-start.1 = ((f32[4,512,256]{2,1,0:T(8,128)}), f32[4,512,256]{2,1,0:T(8,128)S(1)}, u32[]{:S(2)}, u32[]{:S(2)}) async-start(f32[4,512,256]{2,1,0:T(8,128)} %get-tuple-element.185), calls=%async_computation.1 | async-start | bytes 4194304 | tf_op jit(solution)/shard_map/all_to_all | solution.py:442
  157.9 22.7 %collective-permute-start.7 = (f32[4,512,256]{2,1,0:T(8,128)}, f32[4,512,256]{2,1,0:T(8,128)}, u32[]{:S(2)}, u32[]{:S(2)}) collective-permute-start(f32[4,512,256]{2,1,0:T(8,128)} %get-tuple-element.189), channel_id=1, source_target_pairs={{0,1},{1,0},{2,3},{3,2},{4,5},{5,4},{6,7},{7,6},{8,9},{9,8},{10,11... | collective-permute-start | bytes 6291464 | tf_op jit(solution)/shard_map/ppermute | solution.py:460
  185.7 1.4 copy-start.1
  187.8 48.1 %collective-permute-start.9 = (f32[4,512,256]{2,1,0:T(8,128)}, f32[4,512,256]{2,1,0:T(8,128)S(1)}, u32[]{:S(2)}, u32[]{:S(2)}) collective-permute-start(f32[4,512,256]{2,1,0:T(8,128)} %get-tuple-element.208.refs_0_), channel_id=1, source_target_pairs={{0,4},{4,0},{8,12},{12,8},{16,20},{20,16},{24,28},{28,24},{1,5},{5... | collective-permute-start | bytes 6291464 | tf_op jit(solution)/shard_map/ppermute | solution.py:448
  189.3 27.7 %collective-permute-start.10 = (f32[512,256]{1,0:T(8,128)}, f32[512,256]{1,0:T(8,128)S(1)}, u32[]{:S(2)}, u32[]{:S(2)}) collective-permute-start(f32[512,256]{1,0:T(8,128)} %get-tuple-element.220), channel_id=1, source_target_pairs={{0,8},{4,12},{8,16},{12,20},{16,24},{20,28},{24,0},{28,4},{1,9},{5... | collective-permute-start | bytes 1572872 | tf_op jit(solution)/shard_map/ppermute | solution.py:437
  191.2 36.9 %collective-permute-start.11 = (f32[512,256]{1,0:T(8,128)}, f32[512,256]{1,0:T(8,128)S(1)}, u32[]{:S(2)}, u32[]{:S(2)}) collective-permute-start(f32[512,256]{1,0:T(8,128)} %get-tuple-element.221), channel_id=1, source_target_pairs={{0,16},{4,20},{8,24},{12,28},{16,0},{20,4},{24,8},{28,12},{1,17},{... | collective-permute-start | bytes 1572872 | tf_op jit(solution)/shard_map/ppermute | solution.py:437
  193.6 34.6 %collective-permute-start.12 = (f32[512,256]{1,0:T(8,128)}, f32[512,256]{1,0:T(8,128)S(1)}, u32[]{:S(2)}, u32[]{:S(2)}) collective-permute-start(f32[512,256]{1,0:T(8,128)} %get-tuple-element.222), channel_id=1, source_target_pairs={{0,24},{4,28},{8,0},{12,4},{16,8},{20,12},{24,16},{28,20},{1,25},{... | collective-permute-start | bytes 1572872 | tf_op jit(solution)/shard_map/ppermute | solution.py:437
  217.0 11.1 %copy-start.15 = (f32[512,256]{1,0:T(8,128)}, f32[512,256]{1,0:T(8,128)S(1)}, u32[]{:S(2)}) copy-start(f32[512,256]{1,0:T(8,128)S(1)} %collective-permute-done.10.refs_1_) | copy-start | bytes 1572868
  228.1 0.8 copy-start.18
  228.1 1.0 copy-start.21
  233.6 56.4 %collective-permute-start.17 = (f32[4,512,256]{2,1,0:T(8,128)}, f32[4,512,256]{2,1,0:T(8,128)}, u32[]{:S(2)}, u32[]{:S(2)}) collective-permute-start(f32[4,512,256]{2,1,0:T(8,128)} %get-tuple-element.233.refs_0_), channel_id=1, source_target_pairs={{0,4},{4,0},{8,12},{12,8},{16,20},{20,16},{24,28},{28,24},{1,5},{5... | collective-permute-start | bytes 6291464 | tf_op jit(solution)/shard_map/ppermute | solution.py:448
  235.9 1.3 copy-start.8
  237.9 34.3 %collective-permute-start.13 = (f32[512,256]{1,0:T(8,128)}, f32[512,256]{1,0:T(8,128)S(1)}, u32[]{:S(2)}, u32[]{:S(2)}) collective-permute-start(f32[512,256]{1,0:T(8,128)} %get-tuple-element.226), channel_id=1, source_target_pairs={{0,8},{4,12},{8,16},{12,20},{16,24},{20,28},{24,0},{28,4},{1,9},{5... | collective-permute-start | bytes 1572872 | tf_op jit(solution)/shard_map/ppermute | solution.py:437
  247.7 35.4 %collective-permute-start.14 = (f32[512,256]{1,0:T(8,128)}, f32[512,256]{1,0:T(8,128)S(1)}, u32[]{:S(2)}, u32[]{:S(2)}) collective-permute-start(f32[512,256]{1,0:T(8,128)} %get-tuple-element.227), channel_id=1, source_target_pairs={{0,16},{4,20},{8,24},{12,28},{16,0},{20,4},{24,8},{28,12},{1,17},{... | collective-permute-start | bytes 1572872 | tf_op jit(solution)/shard_map/ppermute | solution.py:437
  249.6 33.5 %collective-permute-start.15 = (f32[512,256]{1,0:T(8,128)}, f32[512,256]{1,0:T(8,128)S(1)}, u32[]{:S(2)}, u32[]{:S(2)}) collective-permute-start(f32[512,256]{1,0:T(8,128)} %get-tuple-element.228), channel_id=1, source_target_pairs={{0,24},{4,28},{8,0},{12,4},{16,8},{20,12},{24,16},{28,20},{1,25},{... | collective-permute-start | bytes 1572872 | tf_op jit(solution)/shard_map/ppermute | solution.py:437
  272.2 10.9 %copy-start.17 = (f32[512,256]{1,0:T(8,128)}, f32[512,256]{1,0:T(8,128)S(1)}, u32[]{:S(2)}) copy-start(f32[512,256]{1,0:T(8,128)S(1)} %collective-permute-done.13.refs_1_) | copy-start | bytes 1572868
  283.0 0.8 copy-start.20
  283.1 1.0 copy-start.22
  288.6 54.8 %collective-permute-start.16 = (f32[4,512,256]{2,1,0:T(8,128)}, f32[4,512,256]{2,1,0:T(8,128)S(1)}, u32[]{:S(2)}, u32[]{:S(2)}) collective-permute-start(f32[4,512,256]{2,1,0:T(8,128)} %get-tuple-element.232.refs_0_), channel_id=1, source_target_pairs={{0,2},{1,3},{2,0},{3,1},{4,6},{5,7},{6,4},{7,5},{8,10},{9,11},{10,... | collective-permute-start | bytes 6291464 | tf_op jit(solution)/shard_map/ppermute | solution.py:455
  290.7 36.0 %collective-permute-start.18 = (f32[512,256]{1,0:T(8,128)}, f32[512,256]{1,0:T(8,128)S(1)}, u32[]{:S(2)}, u32[]{:S(2)}) collective-permute-start(f32[512,256]{1,0:T(8,128)} %get-tuple-element.254), channel_id=1, source_target_pairs={{0,8},{4,12},{8,16},{12,20},{16,24},{20,28},{24,0},{28,4},{1,9},{5... | collective-permute-start | bytes 1572872 | tf_op jit(solution)/shard_map/ppermute | solution.py:437
  302.3 35.0 %collective-permute-start.19 = (f32[512,256]{1,0:T(8,128)}, f32[512,256]{1,0:T(8,128)S(1)}, u32[]{:S(2)}, u32[]{:S(2)}) collective-permute-start(f32[512,256]{1,0:T(8,128)} %get-tuple-element.255), channel_id=1, source_target_pairs={{0,16},{4,20},{8,24},{12,28},{16,0},{20,4},{24,8},{28,12},{1,17},{... | collective-permute-start | bytes 1572872 | tf_op jit(solution)/shard_map/ppermute | solution.py:437
  304.1 33.2 %collective-permute-start.20 = (f32[512,256]{1,0:T(8,128)}, f32[512,256]{1,0:T(8,128)S(1)}, u32[]{:S(2)}, u32[]{:S(2)}) collective-permute-start(f32[512,256]{1,0:T(8,128)} %get-tuple-element.256), channel_id=1, source_target_pairs={{0,24},{4,28},{8,0},{12,4},{16,8},{20,12},{24,16},{28,20},{1,25},{... | collective-permute-start | bytes 1572872 | tf_op jit(solution)/shard_map/ppermute | solution.py:437
  326.8 10.6 %copy-start.14 = (f32[512,256]{1,0:T(8,128)}, f32[512,256]{1,0:T(8,128)S(1)}, u32[]{:S(2)}) copy-start(f32[512,256]{1,0:T(8,128)S(1)} %collective-permute-done.18.refs_1_) | copy-start | bytes 1572868
  337.3 0.8 copy-start.16
  337.3 1.0 copy-start.19
  342.8 49.5 %collective-permute-start.24 = (f32[4,512,256]{2,1,0:T(8,128)}, f32[4,512,256]{2,1,0:T(8,128)}, u32[]{:S(2)}, u32[]{:S(2)}) collective-permute-start(f32[4,512,256]{2,1,0:T(8,128)} %get-tuple-element.263.refs_0_), channel_id=1, source_target_pairs={{0,2},{1,3},{2,0},{3,1},{4,6},{5,7},{6,4},{7,5},{8,10},{9,11},{10,... | collective-permute-start | bytes 6291464 | tf_op jit(solution)/shard_map/ppermute | solution.py:455
  343.4 1.3 copy-start.6
  345.4 34.5 %collective-permute-start.21 = (f32[512,256]{1,0:T(8,128)}, f32[512,256]{1,0:T(8,128)S(1)}, u32[]{:S(2)}, u32[]{:S(2)}) collective-permute-start(f32[512,256]{1,0:T(8,128)} %get-tuple-element.260), channel_id=1, source_target_pairs={{0,8},{4,12},{8,16},{12,20},{16,24},{20,28},{24,0},{28,4},{1,9},{5... | collective-permute-start | bytes 1572872 | tf_op jit(solution)/shard_map/ppermute | solution.py:437
  356.9 35.4 %collective-permute-start.22 = (f32[512,256]{1,0:T(8,128)}, f32[512,256]{1,0:T(8,128)S(1)}, u32[]{:S(2)}, u32[]{:S(2)}) collective-permute-start(f32[512,256]{1,0:T(8,128)} %get-tuple-element.261), channel_id=1, source_target_pairs={{0,16},{4,20},{8,24},{12,28},{16,0},{20,4},{24,8},{28,12},{1,17},{... | collective-permute-start | bytes 1572872 | tf_op jit(solution)/shard_map/ppermute | solution.py:437
  359.1 33.2 %collective-permute-start.23 = (f32[512,256]{1,0:T(8,128)}, f32[512,256]{1,0:T(8,128)S(1)}, u32[]{:S(2)}, u32[]{:S(2)}) collective-permute-start(f32[512,256]{1,0:T(8,128)} %get-tuple-element.262), channel_id=1, source_target_pairs={{0,24},{4,28},{8,0},{12,4},{16,8},{20,12},{24,16},{28,20},{1,25},{... | collective-permute-start | bytes 1572872 | tf_op jit(solution)/shard_map/ppermute | solution.py:437
  379.8 12.5 %copy-start.3 = (f32[512,256]{1,0:T(8,128)}, f32[512,256]{1,0:T(8,128)S(1)}, u32[]{:S(2)}) copy-start(f32[512,256]{1,0:T(8,128)S(1)} %collective-permute-done.21.refs_1_) | copy-start | bytes 1572868
  392.3 0.8 copy-start.4
  392.3 1.0 copy-start.5
  393.3 14.9 %copy-start.26 = (f32[512]{0:T(512)S(1)}, f32[512]{0:T(512)}, u32[]{:S(2)}) copy-start(f32[512]{0:T(512)} %param.13) | copy-start | bytes 6148
  394.1 20.7 %collective-permute-start.25 = (f32[4,512,256]{2,1,0:T(8,128)}, f32[4,512,256]{2,1,0:T(8,128)S(1)}, u32[]{:S(2)}, u32[]{:S(2)}) collective-permute-start(f32[4,512,256]{2,1,0:T(8,128)} %get-tuple-element.274), channel_id=1, source_target_pairs={{0,1},{1,0},{2,3},{3,2},{4,5},{5,4},{6,7},{7,6},{8,9},{9,8},{10,11... | collective-permute-start | bytes 6291464 | tf_op jit(solution)/shard_map/ppermute | solution.py:460
  394.2 48.8 %collective-permute-start.27 = (f32[512,256]{1,0:T(8,128)}, f32[512,256]{1,0:T(8,128)S(1)}, u32[]{:S(2)}, u32[]{:S(2)}) collective-permute-start(f32[512,256]{1,0:T(8,128)} %get-tuple-element.287), channel_id=1, source_target_pairs={{0,8},{4,12},{8,16},{12,20},{16,24},{20,28},{24,0},{28,4},{1,9},{5... | collective-permute-start | bytes 1572872 | tf_op jit(solution)/shard_map/ppermute | solution.py:437
  405.7 37.3 %collective-permute-start.28 = (f32[512,256]{1,0:T(8,128)}, f32[512,256]{1,0:T(8,128)S(1)}, u32[]{:S(2)}, u32[]{:S(2)}) collective-permute-start(f32[512,256]{1,0:T(8,128)} %get-tuple-element.288), channel_id=1, source_target_pairs={{0,16},{4,20},{8,24},{12,28},{16,0},{20,4},{24,8},{28,12},{1,17},{... | collective-permute-start | bytes 1572872 | tf_op jit(solution)/shard_map/ppermute | solution.py:437
  407.5 35.5 %collective-permute-start.29 = (f32[512,256]{1,0:T(8,128)}, f32[512,256]{1,0:T(8,128)}, u32[]{:S(2)}, u32[]{:S(2)}) collective-permute-start(f32[512,256]{1,0:T(8,128)} %get-tuple-element.289), channel_id=1, source_target_pairs={{0,24},{4,28},{8,0},{12,4},{16,8},{20,12},{24,16},{28,20},{1,25},{... | collective-permute-start | bytes 1572872 | tf_op jit(solution)/shard_map/ppermute | solution.py:437
  414.8 1.4 copy-start
  443.0 6.8 %collective-permute-start.26 = (f32[4,512,256]{2,1,0:T(8,128)}, f32[4,512,256]{2,1,0:T(8,128)}, u32[]{:S(2)}, u32[]{:S(2)}) collective-permute-start(f32[4,512,256]{2,1,0:T(8,128)} %get-tuple-element.285), channel_id=1, source_target_pairs={{0,1},{1,0},{2,3},{3,2},{4,5},{5,4},{6,7},{7,6},{8,9},{9,8},{10,11... | collective-permute-start | bytes 6291464 | tf_op jit(solution)/shard_map/ppermute | solution.py:460
  443.0 0.8 copy-start.9
  443.0 1.0 copy-start.10
  449.7 6.4 %copy-start.23 = (f32[8,128]{1,0:T(8,128)S(1)}, f32[8,128]{1,0:T(8,128)}, u32[]{:S(2)}) copy-start(f32[8,128]{1,0:T(8,128)} %get-tuple-element.293) | copy-start | bytes 12292
  449.7 6.4 %copy-start.24 = (f32[8,128]{1,0:T(8,128)S(1)}, f32[8,128]{1,0:T(8,128)}, u32[]{:S(2)}) copy-start(f32[8,128]{1,0:T(8,128)} %get-tuple-element.281) | copy-start | bytes 12292
  449.8 6.4 %copy-start.25 = (f32[8,128]{1,0:T(8,128)S(1)}, f32[8,128]{1,0:T(8,128)}, u32[]{:S(2)}) copy-start(f32[8,128]{1,0:T(8,128)} %get-tuple-element.294) | copy-start | bytes 12292

commit v4 on v3

--- a/solution.py
+++ b/solution.py
@@ -66,7 +66,7 @@
     return pl.ds(pl.multiple_of(block * width, width), width)
 
 
-CHUNKS = 4
+CHUNKS = 2
 
 
 def mask_call(chain, observed, direction, probe, parts, together):
@@ -91,30 +91,14 @@
         "mask",
         (CHUNKS,),
         (observed, direction),
-        [rows_spec(rows, t_loc), pl.BlockSpec((1, rows, t_loc), lambda i, place: (probe, i, 0))],
+        [
+            rows_spec(rows, t_loc),
+            pl.BlockSpec((1, rows, t_loc), lambda i, place: (probe, i, 0)),
+        ],
         outs,
         specs,
     )
     return found[0] if together else found
-
-
-def stack_call(chain, pieces):
-    s_loc, width = pieces[0].shape
-    parts, rows = len(pieces), s_loc // CHUNKS
-
-    def body(place, *refs):
-        for k in range(parts):
-            refs[parts][lax.rem(place[0] + parts - k, parts)] = refs[k][...]
-
-    return chain(
-        body,
-        "stack",
-        (CHUNKS,),
-        pieces,
-        [rows_spec(rows, width)] * parts,
-        [((parts, s_loc, width), F32)],
-        [rows_spec(parts, rows, width)],
-    )[0]
 
 
 def add_call(chain, terms, together):
@@ -140,12 +124,35 @@
     return found[0] if together else found
 
 
-def gate_call(chain, *arrays):
-    anywhere = [pl.BlockSpec(memory_space=pl.ANY)] * len(arrays)
+def gate_call(chain, arrays, pieces=()):
+    n, parts = len(arrays), len(pieces)
+    anywhere = pl.BlockSpec(memory_space=pl.ANY)
     outs = [(array.shape, array.dtype) for array in arrays]
-    same = [(k, k) for k in range(len(arrays))]
+
+    def body(place, *refs):
+        if parts:
+            given, whole, sems = refs[n : n + parts], refs[2 * n + parts], refs[-1]
+            copies = []
+            for k in range(parts):
+                block = lax.rem(place[0] + parts - k, parts)
+                copies.append(pltpu.make_async_copy(given[k], whole.at[block], sems.at[k]))
+                copies[-1].start()
+            for copy in copies:
+                copy.wait()
+
+    if parts:
+        outs.append(((parts, *pieces[0].shape), F32))
     return chain(
-        lambda place, *refs: None, "gate", (), arrays, anywhere, outs, anywhere, aliases=same, bytes_hint=20 << 20
+        body,
+        "gate",
+        (),
+        [*arrays, *pieces],
+        [anywhere] * (n + parts),
+        outs,
+        [anywhere] * len(outs),
+        scratch=[pltpu.SemaphoreType.DMA((parts,))] if parts else (),
+        aliases=[(k, k) for k in range(n)],
+        bytes_hint=20 << 20,
     )
 
 
@@ -323,7 +330,8 @@
         self.width = refs[0].shape[-1]
 
     def specs(self, rows):
-        one = rows_spec(self.parts, rows, self.width) if self.whole else rows_spec(rows, self.width)
+        shape = (self.parts, rows, self.width) if self.whole else (rows, self.width)
+        one = rows_spec(*shape)
         return [one] * len(self.operands)
 
     def each(self, place, refs):
@@ -374,46 +382,59 @@
     )[0]
 
 
-def update_call(chain, stats, row, observed, noise, solution, residual, direction, outer, probe, earlier):
-    _, s_loc, t_loc = direction.shape
+def update_call(chain, stats, observed, noise, solution, residual, direction, outers):
+    probes, s_loc, t_loc = direction.shape
     rows = s_loc // CHUNKS
-    n = len(outer.operands)
 
     def body(place, given, seen, var, sol_ref, res_ref, way_ref, *refs):
         new_solution, new_residual, new_direction = refs[-3:]
-        totals = jnp.sum(given[:, row * 8 : row * 8 + 8, :], axis=0)
-        rr, pap, cross, square = (totals[k : k + 1, :1] for k in range(4))
-        alpha = rr / pap
-        rr_next = rr + alpha * (alpha * square - 2.0 * cross)
-        beta = rr_next / rr
-        for at, value in outer.each(place, refs[:n]):
-            way = way_ref[0, :, at]
-            image = seen[:, at].astype(F32) * value + var[...] * way
-            fresh = res_ref[0, :, at] - alpha * image
-            new_solution[0, :, at] = sol_ref[0, :, at] + alpha * way
-            new_residual[0, :, at] = fresh
-            new_direction[0, :, at] = fresh + beta * way
-
-    probe_rows = pl.BlockSpec((1, rows, t_loc), lambda i, place: (probe, i, 0))
-    operands = [stats, observed, noise, solution, residual, direction, *outer.operands]
+        taken = 0
+        for p, outer in enumerate(outers):
+            mine = refs[taken : taken + len(outer.operands)]
+            taken += len(outer.operands)
+
+            @pl.when(pl.program_id(0) // CHUNKS == p)
+            def _():
+                totals = jnp.sum(given[:, p * 8 : p * 8 + 8, :], axis=0)
+                rr, pap, cross, square = (totals[k : k + 1, :1] for k in range(4))
+                alpha = rr / pap
+                rr_next = rr + alpha * (alpha * square - 2.0 * cross)
+                beta = rr_next / rr
+                for at, value in outer.each(place, mine):
+                    way = way_ref[0, :, at]
+                    image = seen[:, at].astype(F32) * value + var[...] * way
+                    fresh = res_ref[0, :, at] - alpha * image
+                    new_solution[0, :, at] = sol_ref[0, :, at] + alpha * way
+                    new_residual[0, :, at] = fresh
+                    new_direction[0, :, at] = fresh + beta * way
+
+    def outer_specs(p, outer):
+        def row(i):
+            return jnp.clip(i - p * CHUNKS, 0, CHUNKS - 1)
+
+        if outer.whole:
+            one = pl.BlockSpec((outer.parts, rows, outer.width), lambda i, place: (0, row(i), 0))
+        else:
+            one = pl.BlockSpec((rows, outer.width), lambda i, place: (row(i), 0))
+        return [one] * len(outer.operands)
+
+    probe_rows = pl.BlockSpec((1, rows, t_loc), lambda i, place: (i // CHUNKS, i % CHUNKS, 0))
     return chain(
         body,
         "update",
-        (CHUNKS,),
-        operands + list(earlier),
+        (probes * CHUNKS,),
+        [stats, observed, noise, solution, residual, direction] + [ref for outer in outers for ref in outer.operands],
         [
             pl.BlockSpec(stats.shape, lambda i, place: (0, 0, 0)),
-            rows_spec(rows, t_loc),
-            rows_spec(rows, 1),
+            pl.BlockSpec((rows, t_loc), lambda i, place: (i % CHUNKS, 0)),
+            pl.BlockSpec((rows, 1), lambda i, place: (i % CHUNKS, 0)),
             probe_rows,
             probe_rows,
             probe_rows,
         ]
-        + outer.specs(rows)
-        + [pl.BlockSpec(memory_space=HBM)] * len(earlier),
+        + [spec for p, outer in enumerate(outers) for spec in outer_specs(p, outer)],
         [(direction.shape, F32)] * 3,
         [probe_rows] * 3,
-        aliases=[(len(operands) + k, k) for k in range(len(earlier))],
     )
 
 
@@ -496,15 +517,14 @@
     def sums(outer, p, hint=0):
         return sums_call(chain, observed, noise, residual, direction, outer, p, hint)
 
-    def update(stats, row, outer, p, earlier):
-        return update_call(chain, stats, row, observed, noise, solution, residual, direction, outer, p, earlier)
-
     def mask(p, together):
         return mask_call(chain, observed, direction, p, n_z, together)
 
-    def pass_on(*groups):
-        flat = iter(gate_call(chain, *[array for group in groups for array in group]))
-        return [[next(flat) for _ in group] for group in groups]
+    def pass_on(*groups, pieces=()):
+        found = gate_call(chain, [array for group in groups for array in group], pieces)
+        flat = iter(found)
+        kept = [[next(flat) for _ in group] for group in groups]
+        return kept + [found[-1]] if pieces else kept
 
     mask0 = mask(0, False)
     mask2 = mask(2, True)
@@ -513,16 +533,13 @@
     mask1 = mask(1, True)
     mask3 = mask(3, True)
     time = entries_call(chain, day_features, t_loc, n_x, n_c, time_row, time_col, time_range, DAYS, "time_entries")
-    matrices = [space_entries(0, (0, 1), ())]
-    cells0 = stack_call(chain, out0)
-    (mask1,), (mask3,), x2 = pass_on([mask1], [mask3], x2[1:])
+    (mask1,), (mask3,), x2, cells0 = pass_on([mask1], [mask3], x2[1:], pieces=out0)
 
     out1 = over_z_at_once(mask1)
     x3 = over_x(mask3)
     y0 = over_y(cells0)
     terms2 = time_call(chain, [mask2] + x2, time, n_c)
-    for k in range(1, n_y):
-        matrices.append(space_entries(k, (0, 1), ()))
+    matrices = [space_entries(0, (0, 1), ())]
     x3, y0 = pass_on(x3[1:], y0[1:])
     inner2 = add_call(chain, over_core(terms2), True)
     (cells1,), (inner2,) = pass_on([out1], [inner2])
@@ -530,31 +547,30 @@
     out2 = over_z_at_once(inner2)
     y1 = over_y(cells1)
     terms3 = time_call(chain, [mask3] + x3, time, n_c)
-    smooth0 = space([cells0] + y0, False)
+    for k in range(1, n_y):
+        matrices.append(space_entries(k, (0, 1), ()))
     (y1,) = pass_on(y1[1:])
     inner3 = add_call(chain, over_core(terms3), False)
-    (cells2,), inner3, smooth0 = pass_on([out2], inner3, smooth0)
+    (cells2,), inner3 = pass_on([out2], inner3)
 
     out3 = over_z(inner3)
     y2 = over_y(cells2)
-    smooth1 = space([cells1] + y1, False)
-    cells3 = stack_call(chain, out3)
-    y2, smooth0, smooth1 = pass_on(y2[1:], smooth0, smooth1)
+    smooth0 = space([cells0] + y0, False)
+    y2, smooth0, cells3 = pass_on(y2[1:], smooth0, pieces=out3)
 
     home0 = over_z(smooth0)
     y3 = over_y(cells3)
-    smooth2 = space([cells2] + y2, False)
-    home0 = stack_call(chain, home0)
-    y3, smooth1, smooth2 = pass_on(y3[1:], smooth1, smooth2)
+    smooth1 = space([cells1] + y1, False)
+    y3, smooth1, home0 = pass_on(y3[1:], smooth1, pieces=home0)
 
     home1 = over_z(smooth1)
     x0 = over_x(home0)
-    smooth3 = space([cells3] + y3, False)
-    home1 = stack_call(chain, home1)
-    x0, smooth2, smooth3 = pass_on(x0[1:], smooth2, smooth3)
+    smooth2 = space([cells2] + y2, False)
+    x0, smooth2, home1 = pass_on(x0[1:], smooth2, pieces=home1)
 
     home2 = over_z(smooth2)
     x1 = over_x(home1)
+    smooth3 = space([cells3] + y3, False)
     terms0 = time_call(chain, [home0] + x0, time, n_c)
     home2, x1, terms0, smooth3 = pass_on(home2, x1[1:], terms0, smooth3)
 
@@ -569,10 +585,8 @@
     sums3 = sums(outer3, 3, 200 << 20)
     sums1 = sums(outer1, 1)
     stats = over_all(sums0, sums1, sums2, sums3)
-    new = ()
-    for p, outer in enumerate((outer0, outer1, outer2, outer3)):
-        new = update(stats, p, outer, p, new)
-    return tuple(new)
+    outers = (outer0, outer1, outer2, outer3)
+    return tuple(update_call(chain, stats, observed, noise, solution, residual, direction, outers))
 
 
 def solution(mesh):

time: 522 us -> 739 us (1.42)
  Pallas kernels: 339 us -> 564 us
  starting transfers between devices: 83.5 us -> 60.5 us
  waiting for transfers between devices: 51.2 us -> 69.3 us
    pallas_call x38 -> x31, Pallas kernels: 339 us -> 564 us  [__call__(): pl.pallas_call(kernel, grid_spec=pltpu.PrefetchScalarGridSpec(num_scalar_...]
    ppermute x18, starting transfers between devices: 65.5 us -> 38.5 us  [over_z(): found.append(lax.ppermute(pieces[k], 'sta', pairs))]
    ppermute x4, waiting for transfers between devices: 2.62 us -> 20.5 us  [over_y(): found.append(lax.ppermute(cells, 'sta', pairs))]
    ppermute x18, waiting for transfers between devices: 45 us -> 34.9 us  [over_z(): found.append(lax.ppermute(pieces[k], 'sta', pairs))]
    ppermute x4, waiting for transfers between devices: 3.38 us -> 11.6 us  [over_x(): found.append(lax.ppermute(cells, 'day', pairs))]
  transfers between devices with their start and end apart: 32 -> 32, of which waited for: 8 -> 13; matrix products, arithmetic and copies ran while one was open for 0% -> 0% of each run, Pallas kernels for 55% -> 35%
where the time goes in v4:
time: 739 us; the launch traced here: 738 us
  Pallas kernels  564 us (76%)
  waiting for transfers between devices  69.3 us (9%)
  starting transfers between devices  60.5 us (8%)
  blocking collectives  28.9 us (4%)
  local copies, waits for them, and re-layouts  12.8 us (2%)
    pallas_call x31, Pallas kernels, __call__(): pl.pallas_call(kernel, grid_spec=pltpu.PrefetchScalarGridSpec(num_scalar_...  564 us
    ppermute x18, starting transfers between devices, over_z(): found.append(lax.ppermute(pieces[k], 'sta', pairs))  38.5 us
    ppermute x18, waiting for transfers between devices, over_z(): found.append(lax.ppermute(pieces[k], 'sta', pairs))  34.9 us
    all_to_all x1, blocking collectives, over_all(): return lax.all_to_all(many, ('sta', 'day'), 0, 0, tiled=True)  28.9 us
    ppermute x4, waiting for transfers between devices, over_y(): found.append(lax.ppermute(cells, 'sta', pairs))  20.5 us
  transfers between devices with their start and end apart: 32, of which 13 were waited for; matrix products, arithmetic and copies ran while one was open for 0% of the time, Pallas kernels for 35%

profile of v4, /device:TPU:0, one launch (start us, length us, event | category | flops | bytes accessed | tf_op | source)
XLA Modules:
  0.0 738.2 jit_solution(17341410096663291842)
XLA Ops:
  1.2 4.0 mask.4
  5.2 4.1 mask.5
  9.3 2.9 collective-permute-start
  12.2 1.6 collective-permute-start.1
  13.8 2.6 collective-permute-start.2
  16.4 1.3 collective-permute-start.3
  17.7 4.0 mask.6
  21.7 3.9 mask.7
  25.6 22.3 %time_entries.1 = (bf16[2048,2048]{1,0:T(8,128)(2,1)}, bf16[2048,2048]{1,0:T(8,128)(2,1)}, f32[8,128]{1,0:T(8,128)}) custom-call(s32[4]{0:T(128)} %pad_add_fusion.place, f32[4,4096]{1,0:T(4,128)} %refs_1_.12, f32[4,4096]{1,0:T(4,128)} %refs_1_.12, f32[8,128]{1,0:T(8,128)} %get-tuple-element.135.refs_2_), custom_call_target="tpu_custom_call" | custom-call | tf_op jit(solution)/shard_map/time_entries/pallas_call | solution.py:40
  47.9 2.3 collective-permute-done.2.refs_5_
  50.3 7.8 %collective-permute-done.refs_2_ = f32[4,512,256]{2,1,0:T(8,128)S(1)} collective-permute-done((f32[4,512,256]{2,1,0:T(8,128)}, f32[4,512,256]{2,1,0:T(8,128)S(1)}, u32[]{:S(2)}, u32[]{:S(2)}) %collective-permute-start) | collective-permute-done | bytes 2097184 | tf_op jit(solution)/shard_map/ppermute | solution.py:476
  58.1 1.3 copy-done.7
  59.4 65.3 %gate.9 = (f32[4,512,256]{2,1,0:T(8,128)}, f32[4,512,256]{2,1,0:T(8,128)}, f32[4,512,256]{2,1,0:T(8,128)}, f32[4,512,256]{2,1,0:T(8,128)}, f32[8,128]{1,0:T(8,128)}) custom-call(s32[4]{0:T(128)} %pad_add_fusion.place, f32[4,512,256]{2,1,0:T(8,128)} %get-tuple-element.127.refs_0_, ...), custom_call_target="tpu_custom_call", output_to_operand_aliasing={{0}: (1, {}), {1}: (2, {}), {2}: (3, {})} | custom-call | flops 24117248000 | bytes 20971520 | tf_op jit(solution)/shard_map/gate/pallas_call | solution.py:40
  124.7 1.8 collective-permute-start.5
  126.5 1.5 collective-permute-start.6
  128.0 5.2 all-to-all-start
  133.2 20.4 %time.4 = (f32[4,512,256]{2,1,0:T(8,128)}, f32[4,512,256]{2,1,0:T(8,128)}, f32[8,128]{1,0:T(8,128)}) custom-call(s32[4]{0:T(128)} %pad_add_fusion.place, f32[4,512,256]{2,1,0:T(8,128)} %get-tuple-element.130.refs_0_, f32[4,512,256]{2,1,0:T(8,128)} %get-tuple-element.138.refs_1_, bf16[2048,2048]{1,0:T(8,128)(2,1)} %get-tuple-element.139.refs_2_, ...), custom_call_target="tpu_custom_call" | custom-call | tf_op jit(solution)/shard_map/time/pallas_call | solution.py:40
  153.6 17.4 %space_entries.2 = (bf16[2048,2048]{1,0:T(8,128)(2,1)}, bf16[2048,2048]{1,0:T(8,128)(2,1)}, f32[8,128]{1,0:T(8,128)}) custom-call(s32[4]{0:T(128)} %pad_add_fusion.place, f32[2,4096]{1,0:T(2,128)} %refs_3_.8, f32[2,4096]{1,0:T(2,128)} %refs_3_.8, f32[2,4096]{1,0:T(2,128)} %refs_3_.8, f32[2,4096]{1,0:T(2,128)} %refs_3_.8, f32[8,128]{1,0:T(8,128)} %get-tuple-element.146.refs_4_), custom_call_target="tpu_custom_call" | custom-call | tf_op jit(solution)/shard_map/space_entries/pallas_call | solution.py:40
  173.7 3.9 add.19
  177.6 2.3 all-to-all-done.refs_0_
  179.9 1.3 copy-done.1
  182.5 3.9 all-to-all-start.1
  186.4 20.5 %time.5 = (f32[4,512,256]{2,1,0:T(8,128)}, f32[4,512,256]{2,1,0:T(8,128)}, f32[8,128]{1,0:T(8,128)}) custom-call(s32[4]{0:T(128)} %pad_add_fusion.place, f32[4,512,256]{2,1,0:T(8,128)} %get-tuple-element.144.refs_0_, f32[4,512,256]{2,1,0:T(8,128)} %get-tuple-element.152.refs_1_, bf16[2048,2048]{1,0:T(8,128)(2,1)} %get-tuple-element.139.refs_2_, ...), custom_call_target="tpu_custom_call" | custom-call | tf_op jit(solution)/shard_map/time/pallas_call | solution.py:40
  206.8 17.4 %space_entries.3 = (bf16[2048,2048]{1,0:T(8,128)(2,1)}, bf16[2048,2048]{1,0:T(8,128)(2,1)}, f32[8,128]{1,0:T(8,128)}) custom-call(s32[4]{0:T(128)} %pad_add_fusion.place, f32[2,4096]{1,0:T(2,128)} %refs_3_.8, f32[2,4096]{1,0:T(2,128)} %refs_3_.8, f32[2,4096]{1,0:T(2,128)} %refs_3_.8, f32[2,4096]{1,0:T(2,128)} %refs_3_.8, f32[8,128]{1,0:T(8,128)} %get-tuple-element.157.refs_4_), custom_call_target="tpu_custom_call" | custom-call | tf_op jit(solution)/shard_map/space_entries/pallas_call | solution.py:40
  224.2 4.7 collective-permute-done.8.refs_0_
  229.6 3.9 add.20
  233.6 1.3 copy-done.2
  235.5 1.5 collective-permute-start.9
  237.1 1.5 collective-permute-start.10
  238.6 1.7 collective-permute-start.11
  240.3 1.5 collective-permute-start.12
  241.8 22.0 %space.4 = (f32[512,256]{1,0:T(8,128)}, f32[512,256]{1,0:T(8,128)}, f32[512,256]{1,0:T(8,128)}, f32[512,256]{1,0:T(8,128)}, f32[8,128]{1,0:T(8,128)}) custom-call(s32[4]{0:T(128)} %pad_add_fusion.place, f32[4,512,256]{2,1,0:T(8,128)} %get-tuple-element.145.refs_0_, f32[4,512,256]{2,1,0:T(8,128)} %get-tuple-element.166.refs_1_, ...), custom_call_target="tpu_custom_call" | custom-call | tf_op jit(solution)/shard_map/space/pallas_call | solution.py:40
  263.8 10.7 %collective-permute-done.11.refs_7_ = f32[512,256]{1,0:T(8,128)S(1)} collective-permute-done((f32[512,256]{1,0:T(8,128)}, f32[512,256]{1,0:T(8,128)S(1)}, u32[]{:S(2)}, u32[]{:S(2)}) %collective-permute-start.11) | collective-permute-done | bytes 524320 | tf_op jit(solution)/shard_map/ppermute | solution.py:458
  274.5 8.1 %collective-permute-done.9.refs_0_ = f32[4,512,256]{2,1,0:T(8,128)S(1)} collective-permute-done((f32[4,512,256]{2,1,0:T(8,128)}, f32[4,512,256]{2,1,0:T(8,128)S(1)}, u32[]{:S(2)}, u32[]{:S(2)}) %collective-permute-start.9) | collective-permute-done | bytes 2097184 | tf_op jit(solution)/shard_map/ppermute | solution.py:469
  282.6 1.4 copy-done.9
  284.0 65.3 %gate.14 = (f32[4,512,256]{2,1,0:T(8,128)}, f32[512,256]{1,0:T(8,128)}, f32[512,256]{1,0:T(8,128)}, f32[512,256]{1,0:T(8,128)}, f32[512,256]{1,0:T(8,128)}, /*index=5*/f32[4,512,256]{2,1,0:T(8,128)}, f32[8,128]{1,0:T(8,128)}) custom-call(s32[4]{0:T(128)} %pad_add_fusion.place, ...), custom_call_target="tpu_custom_call", output_to_operand_aliasing={{0}: (1, {}), {1}: (2, {}), {2}: (3, {}), {3}: (4, {}), {4}... | custom-call | flops 24117248000 | bytes 20971520 | tf_op jit(solution)/shard_map/gate/pallas_call | solution.py:40
  349.3 1.4 collective-permute-start.13
  350.7 3.3 collective-permute-start.14
  354.0 1.9 collective-permute-start.15
  356.5 22.0 %space.5 = (f32[512,256]{1,0:T(8,128)}, f32[512,256]{1,0:T(8,128)}, f32[512,256]{1,0:T(8,128)}, f32[512,256]{1,0:T(8,128)}, f32[8,128]{1,0:T(8,128)}) custom-call(s32[4]{0:T(128)} %pad_add_fusion.place, f32[4,512,256]{2,1,0:T(8,128)} %get-tuple-element.156.refs_0_, f32[4,512,256]{2,1,0:T(8,128)} %get-tuple-element.182.refs_1_, ...), custom_call_target="tpu_custom_call" | custom-call | tf_op jit(solution)/shard_map/space/pallas_call | solution.py:40
  378.5 10.4 %collective-permute-done.15.refs_7_ = f32[512,256]{1,0:T(8,128)S(1)} collective-permute-done((f32[512,256]{1,0:T(8,128)}, f32[512,256]{1,0:T(8,128)S(1)}, u32[]{:S(2)}, u32[]{:S(2)}) %collective-permute-start.15) | collective-permute-done | bytes 524320 | tf_op jit(solution)/shard_map/ppermute | solution.py:458
  388.9 6.6 collective-permute-done.13.refs_0_
  396.7 65.3 %gate.15 = (f32[4,512,256]{2,1,0:T(8,128)}, f32[512,256]{1,0:T(8,128)}, f32[512,256]{1,0:T(8,128)}, f32[512,256]{1,0:T(8,128)}, f32[512,256]{1,0:T(8,128)}, /*index=5*/f32[4,512,256]{2,1,0:T(8,128)}, f32[8,128]{1,0:T(8,128)}) custom-call(s32[4]{0:T(128)} %pad_add_fusion.place, ...), custom_call_target="tpu_custom_call", output_to_operand_aliasing={{0}: (1, {}), {1}: (2, {}), {2}: (3, {}), {3}: (4, {}), {4}... | custom-call | flops 24117248000 | bytes 20971520 | tf_op jit(solution)/shard_map/gate/pallas_call | solution.py:40
  462.1 1.6 collective-permute-start.17
  463.6 5.5 collective-permute-start.18
  469.1 2.0 collective-permute-start.19
  471.5 22.0 %space.6 = (f32[512,256]{1,0:T(8,128)}, f32[512,256]{1,0:T(8,128)}, f32[512,256]{1,0:T(8,128)}, f32[512,256]{1,0:T(8,128)}, f32[8,128]{1,0:T(8,128)}) custom-call(s32[4]{0:T(128)} %pad_add_fusion.place, f32[4,512,256]{2,1,0:T(8,128)} %get-tuple-element.165.refs_0_, f32[4,512,256]{2,1,0:T(8,128)} %get-tuple-element.194.refs_1_, ...), custom_call_target="tpu_custom_call" | custom-call | tf_op jit(solution)/shard_map/space/pallas_call | solution.py:40
  493.5 10.7 %collective-permute-done.19.refs_7_ = f32[512,256]{1,0:T(8,128)S(1)} collective-permute-done((f32[512,256]{1,0:T(8,128)}, f32[512,256]{1,0:T(8,128)S(1)}, u32[]{:S(2)}, u32[]{:S(2)}) %collective-permute-start.19) | collective-permute-done | bytes 524320 | tf_op jit(solution)/shard_map/ppermute | solution.py:458
  504.3 3.0 collective-permute-done.17.refs_0_
  508.6 65.3 %gate.16 = (f32[4,512,256]{2,1,0:T(8,128)}, f32[512,256]{1,0:T(8,128)}, f32[512,256]{1,0:T(8,128)}, f32[512,256]{1,0:T(8,128)}, f32[512,256]{1,0:T(8,128)}, /*index=5*/f32[4,512,256]{2,1,0:T(8,128)}, f32[8,128]{1,0:T(8,128)}) custom-call(s32[4]{0:T(128)} %pad_add_fusion.place, ...), custom_call_target="tpu_custom_call", output_to_operand_aliasing={{0}: (1, {}), {1}: (2, {}), {2}: (3, {}), {3}: (4, {}), {4}... | custom-call | flops 24117248000 | bytes 20971520 | tf_op jit(solution)/shard_map/gate/pallas_call | solution.py:40
  573.9 1.6 collective-permute-start.24
  575.5 7.9 %collective-permute-start.21 = (f32[512,256]{1,0:T(8,128)}, f32[512,256]{1,0:T(8,128)S(1)}, u32[]{:S(2)}, u32[]{:S(2)}) collective-permute-start(f32[512,256]{1,0:T(8,128)} %get-tuple-element.206), channel_id=1, source_target_pairs={{0,8},{4,12},{8,16},{12,20},{16,24},{20,28},{24,0},{28,4},{1,9},{5... | collective-permute-start | bytes 1572872 | tf_op jit(solution)/shard_map/ppermute | solution.py:458
  583.4 1.8 collective-permute-start.22
  585.8 22.0 %space.7 = (f32[512,256]{1,0:T(8,128)}, f32[512,256]{1,0:T(8,128)}, f32[512,256]{1,0:T(8,128)}, f32[512,256]{1,0:T(8,128)}, f32[8,128]{1,0:T(8,128)}) custom-call(s32[4]{0:T(128)} %pad_add_fusion.place, f32[4,512,256]{2,1,0:T(8,128)} %get-tuple-element.181.refs_0_, f32[4,512,256]{2,1,0:T(8,128)} %get-tuple-element.211.refs_1_, ...), custom_call_target="tpu_custom_call" | custom-call | tf_op jit(solution)/shard_map/space/pallas_call | solution.py:40
  607.8 20.5 %time.6 = (f32[4,512,256]{2,1,0:T(8,128)}, f32[4,512,256]{2,1,0:T(8,128)}, f32[8,128]{1,0:T(8,128)}) custom-call(s32[4]{0:T(128)} %pad_add_fusion.place, f32[4,512,256]{2,1,0:T(8,128)} %get-tuple-element.193.refs_0_, f32[4,512,256]{2,1,0:T(8,128)} %get-tuple-element.210.refs_1_, bf16[2048,2048]{1,0:T(8,128)(2,1)} %get-tuple-element.139.refs_2_, ...), custom_call_target="tpu_custom_call" | custom-call | tf_op jit(solution)/shard_map/time/pallas_call | solution.py:40
  631.0 1.9 collective-permute-start.27
  632.9 1.8 collective-permute-start.28
  636.2 5.3 sums.4
  642.8 6.0 sums.5
  648.8 20.4 %time.7 = (f32[4,512,256]{2,1,0:T(8,128)}, f32[4,512,256]{2,1,0:T(8,128)}, f32[8,128]{1,0:T(8,128)}) custom-call(s32[4]{0:T(128)} %pad_add_fusion.place, f32[4,512,256]{2,1,0:T(8,128)} %get-tuple-element.209.refs_0_, f32[4,512,256]{2,1,0:T(8,128)} %get-tuple-element.230.refs_1_, bf16[2048,2048]{1,0:T(8,128)(2,1)} %get-tuple-element.139.refs_2_, ...), custom_call_target="tpu_custom_call" | custom-call | tf_op jit(solution)/shard_map/time/pallas_call | solution.py:40
  670.7 5.3 sums.6
  676.1 6.0 sums.7
  682.8 28.9 %all_to_all.15.refs_0_ = f32[32,32,128]{2,1,0:T(8,128)} all-to-all(f32[32,32,128]{2,1,0:T(8,128)S(1)} %broadcast_in_dim.10), channel_id=1, replica_groups=mesh['sta'=8,'day'=4] {'sta','day'}, dimensions={0} | all-to-all | bytes 1048576 | tf_op jit(solution)/shard_map/all_to_all | solution.py:486
  711.7 26.3 %update.1 = (f32[4,512,1024]{2,1,0:T(8,128)}, f32[4,512,1024]{2,1,0:T(8,128)}, f32[4,512,1024]{2,1,0:T(8,128)}, f32[8,128]{1,0:T(8,128)}) custom-call(s32[4]{0:T(128)} %pad_add_fusion.place, f32[32,32,128]{2,1,0:T(8,128)} %all_to_all.15.refs_0_, s32[512,1024]{1,0:T(8,128)} %refs_1_.15, f32[512,1]{1,0:T(8,128)} %copy.50.refs_1_.refs_2_, ...), custom_call_target="tpu_custom_call" | custom-call | tf_op jit(solution)/shard_map/update/pallas_call | solution.py:40
  (94 shorter events, 17.6 us)
Async XLA Ops:
  5.2 11.2 %copy-start.20 = (f32[512,256]{1,0:T(8,128)S(1)}, f32[512,256]{1,0:T(8,128)}, u32[]{:S(2)}) copy-start(f32[512,256]{1,0:T(8,128)} %get-tuple-element.134) | copy-start | bytes 1572868
  9.3 48.8 %collective-permute-start = (f32[4,512,256]{2,1,0:T(8,128)}, f32[4,512,256]{2,1,0:T(8,128)S(1)}, u32[]{:S(2)}, u32[]{:S(2)}) collective-permute-start(f32[4,512,256]{2,1,0:T(8,128)} %get-tuple-element.130.refs_0_), channel_id=1, source_target_pairs={{0,2},{1,3},{2,0},{3,1},{4,6},{5,7},{6,4},{7,5},{8,10},{9,11},{10,... | collective-permute-start | bytes 6291464 | tf_op jit(solution)/shard_map/ppermute | solution.py:476
  12.2 35.7 %collective-permute-start.1 = (f32[512,256]{1,0:T(8,128)}, f32[512,256]{1,0:T(8,128)S(1)}, u32[]{:S(2)}, u32[]{:S(2)}) collective-permute-start(f32[512,256]{1,0:T(8,128)} %get-tuple-element.132), channel_id=1, source_target_pairs={{0,8},{4,12},{8,16},{12,20},{16,24},{20,28},{24,0},{28,4},{1,9},{5... | collective-permute-start | bytes 1572872 | tf_op jit(solution)/shard_map/ppermute | solution.py:458
  13.8 36.5 %collective-permute-start.2 = (f32[512,256]{1,0:T(8,128)}, f32[512,256]{1,0:T(8,128)S(1)}, u32[]{:S(2)}, u32[]{:S(2)}) collective-permute-start(f32[512,256]{1,0:T(8,128)} %get-tuple-element.133), channel_id=1, source_target_pairs={{0,16},{4,20},{8,24},{12,28},{16,0},{20,4},{24,8},{28,12},{1,17},{... | collective-permute-start | bytes 1572872 | tf_op jit(solution)/shard_map/ppermute | solution.py:458
  16.4 33.9 %collective-permute-start.3 = (f32[512,256]{1,0:T(8,128)S(1)}, f32[512,256]{1,0:T(8,128)}, u32[]{:S(2)}, u32[]{:S(2)}) collective-permute-start(f32[512,256]{1,0:T(8,128)S(1)} %copy-done.20), channel_id=1, source_target_pairs={{0,24},{4,28},{8,0},{12,4},{16,8},{20,12},{24,16},{28,20},{1,25},{... | collective-permute-start | bytes 1572872 | tf_op jit(solution)/shard_map/ppermute | solution.py:458
  47.9 10.1 %copy-start.17 = (f32[512,256]{1,0:T(8,128)}, f32[512,256]{1,0:T(8,128)S(1)}, u32[]{:S(2)}) copy-start(f32[512,256]{1,0:T(8,128)S(1)} %collective-permute-done.1.refs_4_) | copy-start | bytes 1572868
  50.3 7.8 %copy-start.19 = (f32[512,256]{1,0:T(8,128)}, f32[512,256]{1,0:T(8,128)S(1)}, u32[]{:S(2)}) copy-start(f32[512,256]{1,0:T(8,128)S(1)} %collective-permute-done.2.refs_5_) | copy-start | bytes 1572868
  58.0 1.3 copy-start.7
  124.7 47.2 %collective-permute-start.5 = (f32[4,512,256]{2,1,0:T(8,128)}, f32[4,512,256]{2,1,0:T(8,128)}, u32[]{:S(2)}, u32[]{:S(2)}) collective-permute-start(f32[4,512,256]{2,1,0:T(8,128)} %get-tuple-element.144.refs_0_), channel_id=1, source_target_pairs={{0,2},{1,3},{2,0},{3,1},{4,6},{5,7},{6,4},{7,5},{8,10},{9,11},{10,... | collective-permute-start | bytes 6291464 | tf_op jit(solution)/shard_map/ppermute | solution.py:476
  126.5 46.5 %collective-permute-start.6 = (f32[4,512,256]{2,1,0:T(8,128)}, f32[4,512,256]{2,1,0:T(8,128)}, u32[]{:S(2)}, u32[]{:S(2)}) collective-permute-start(f32[4,512,256]{2,1,0:T(8,128)} %get-tuple-element.145.refs_0_), channel_id=1, source_target_pairs={{0,4},{4,0},{8,12},{12,8},{16,20},{20,16},{24,28},{28,24},{1,5},{5... | collective-permute-start | bytes 6291464 | tf_op jit(solution)/shard_map/ppermute | solution.py:469
  128.0 51.9 %all-to-all-start = ((f32[4,512,256]{2,1,0:T(8,128)}), f32[4,512,256]{2,1,0:T(8,128)S(1)}, u32[]{:S(2)}, u32[]{:S(2)}) async-start(f32[4,512,256]{2,1,0:T(8,128)} %get-tuple-element.137), calls=%async_computation | async-start | bytes 4194304 | tf_op jit(solution)/shard_map/all_to_all | solution.py:463
  153.6 20.1 %collective-permute-start.4 = (f32[4,512,256]{2,1,0:T(8,128)}, f32[4,512,256]{2,1,0:T(8,128)}, u32[]{:S(2)}, u32[]{:S(2)}) collective-permute-start(f32[4,512,256]{2,1,0:T(8,128)} %get-tuple-element.143), channel_id=1, source_target_pairs={{0,1},{1,0},{2,3},{3,2},{4,5},{5,4},{6,7},{7,6},{8,9},{9,8},{10,11... | collective-permute-start | bytes 6291464 | tf_op jit(solution)/shard_map/ppermute | solution.py:481
  179.9 1.3 copy-start.1
  181.9 47.0 %collective-permute-start.8 = (f32[4,512,256]{2,1,0:T(8,128)}, f32[4,512,256]{2,1,0:T(8,128)}, u32[]{:S(2)}, u32[]{:S(2)}) collective-permute-start(f32[4,512,256]{2,1,0:T(8,128)} %get-tuple-element.156.refs_0_), channel_id=1, source_target_pairs={{0,4},{4,0},{8,12},{12,8},{16,20},{20,16},{24,28},{28,24},{1,5},{5... | collective-permute-start | bytes 6291464 | tf_op jit(solution)/shard_map/ppermute | solution.py:469
  182.5 51.0 %all-to-all-start.1 = ((f32[4,512,256]{2,1,0:T(8,128)}), f32[4,512,256]{2,1,0:T(8,128)S(1)}, u32[]{:S(2)}, u32[]{:S(2)}) async-start(f32[4,512,256]{2,1,0:T(8,128)} %get-tuple-element.151), calls=%async_computation.1 | async-start | bytes 4194304 | tf_op jit(solution)/shard_map/all_to_all | solution.py:463
  224.2 5.4 collective-permute-start.7
  233.5 1.3 copy-start.2
  235.5 47.0 %collective-permute-start.9 = (f32[4,512,256]{2,1,0:T(8,128)}, f32[4,512,256]{2,1,0:T(8,128)S(1)}, u32[]{:S(2)}, u32[]{:S(2)}) collective-permute-start(f32[4,512,256]{2,1,0:T(8,128)} %get-tuple-element.165.refs_0_), channel_id=1, source_target_pairs={{0,4},{4,0},{8,12},{12,8},{16,20},{20,16},{24,28},{28,24},{1,5},{5... | collective-permute-start | bytes 6291464 | tf_op jit(solution)/shard_map/ppermute | solution.py:469
  237.1 26.7 %collective-permute-start.10 = (f32[512,256]{1,0:T(8,128)}, f32[512,256]{1,0:T(8,128)S(1)}, u32[]{:S(2)}, u32[]{:S(2)}) collective-permute-start(f32[512,256]{1,0:T(8,128)} %get-tuple-element.177), channel_id=1, source_target_pairs={{0,8},{4,12},{8,16},{12,20},{16,24},{20,28},{24,0},{28,4},{1,9},{5... | collective-permute-start | bytes 1572872 | tf_op jit(solution)/shard_map/ppermute | solution.py:458
  238.6 35.9 %collective-permute-start.11 = (f32[512,256]{1,0:T(8,128)}, f32[512,256]{1,0:T(8,128)S(1)}, u32[]{:S(2)}, u32[]{:S(2)}) collective-permute-start(f32[512,256]{1,0:T(8,128)} %get-tuple-element.178), channel_id=1, source_target_pairs={{0,16},{4,20},{8,24},{12,28},{16,0},{20,4},{24,8},{28,12},{1,17},{... | collective-permute-start | bytes 1572872 | tf_op jit(solution)/shard_map/ppermute | solution.py:458
  240.3 34.2 %collective-permute-start.12 = (f32[512,256]{1,0:T(8,128)}, f32[512,256]{1,0:T(8,128)S(1)}, u32[]{:S(2)}, u32[]{:S(2)}) collective-permute-start(f32[512,256]{1,0:T(8,128)} %get-tuple-element.179), channel_id=1, source_target_pairs={{0,24},{4,28},{8,0},{12,4},{16,8},{20,12},{24,16},{28,20},{1,25},{... | collective-permute-start | bytes 1572872 | tf_op jit(solution)/shard_map/ppermute | solution.py:458
  263.8 18.8 %copy-start.18 = (f32[512,256]{1,0:T(8,128)}, f32[512,256]{1,0:T(8,128)S(1)}, u32[]{:S(2)}) copy-start(f32[512,256]{1,0:T(8,128)S(1)} %collective-permute-done.10.refs_6_) | copy-start | bytes 1572868
  274.5 8.1 %copy-start.21 = (f32[512,256]{1,0:T(8,128)}, f32[512,256]{1,0:T(8,128)S(1)}, u32[]{:S(2)}) copy-start(f32[512,256]{1,0:T(8,128)S(1)} %collective-permute-done.11.refs_7_) | copy-start | bytes 1572868
  274.5 8.1 %copy-start.24 = (f32[512,256]{1,0:T(8,128)}, f32[512,256]{1,0:T(8,128)S(1)}, u32[]{:S(2)}) copy-start(f32[512,256]{1,0:T(8,128)S(1)} %collective-permute-done.12.refs_8_) | copy-start | bytes 1572868
  282.6 1.4 copy-start.9
  349.3 46.1 %collective-permute-start.13 = (f32[4,512,256]{2,1,0:T(8,128)}, f32[4,512,256]{2,1,0:T(8,128)S(1)}, u32[]{:S(2)}, u32[]{:S(2)}) collective-permute-start(f32[4,512,256]{2,1,0:T(8,128)} %get-tuple-element.181.refs_0_), channel_id=1, source_target_pairs={{0,4},{4,0},{8,12},{12,8},{16,20},{20,16},{24,28},{28,24},{1,5},{5... | collective-permute-start | bytes 6291464 | tf_op jit(solution)/shard_map/ppermute | solution.py:469
  350.7 27.8 %collective-permute-start.14 = (f32[512,256]{1,0:T(8,128)}, f32[512,256]{1,0:T(8,128)S(1)}, u32[]{:S(2)}, u32[]{:S(2)}) collective-permute-start(f32[512,256]{1,0:T(8,128)} %get-tuple-element.189), channel_id=1, source_target_pairs={{0,8},{4,12},{8,16},{12,20},{16,24},{20,28},{24,0},{28,4},{1,9},{5... | collective-permute-start | bytes 1572872 | tf_op jit(solution)/shard_map/ppermute | solution.py:458
  354.0 34.9 %collective-permute-start.15 = (f32[512,256]{1,0:T(8,128)}, f32[512,256]{1,0:T(8,128)S(1)}, u32[]{:S(2)}, u32[]{:S(2)}) collective-permute-start(f32[512,256]{1,0:T(8,128)} %get-tuple-element.190), channel_id=1, source_target_pairs={{0,16},{4,20},{8,24},{12,28},{16,0},{20,4},{24,8},{28,12},{1,17},{... | collective-permute-start | bytes 1572872 | tf_op jit(solution)/shard_map/ppermute | solution.py:458
  355.8 33.0 %collective-permute-start.16 = (f32[512,256]{1,0:T(8,128)}, f32[512,256]{1,0:T(8,128)S(1)}, u32[]{:S(2)}, u32[]{:S(2)}) collective-permute-start(f32[512,256]{1,0:T(8,128)} %get-tuple-element.191), channel_id=1, source_target_pairs={{0,24},{4,28},{8,0},{12,4},{16,8},{20,12},{24,16},{28,20},{1,25},{... | collective-permute-start | bytes 1572872 | tf_op jit(solution)/shard_map/ppermute | solution.py:458
  378.5 17.0 %copy-start.22 = (f32[512,256]{1,0:T(8,128)}, f32[512,256]{1,0:T(8,128)S(1)}, u32[]{:S(2)}) copy-start(f32[512,256]{1,0:T(8,128)S(1)} %collective-permute-done.14.refs_6_) | copy-start | bytes 1572868
  388.9 6.6 copy-start.25
  388.9 6.6 copy-start.27
  395.5 1.3 copy-start.10
  462.1 45.2 %collective-permute-start.17 = (f32[4,512,256]{2,1,0:T(8,128)}, f32[4,512,256]{2,1,0:T(8,128)S(1)}, u32[]{:S(2)}, u32[]{:S(2)}) collective-permute-start(f32[4,512,256]{2,1,0:T(8,128)} %get-tuple-element.193.refs_0_), channel_id=1, source_target_pairs={{0,2},{1,3},{2,0},{3,1},{4,6},{5,7},{6,4},{7,5},{8,10},{9,11},{10,... | collective-permute-start | bytes 6291464 | tf_op jit(solution)/shard_map/ppermute | solution.py:476
  463.6 29.9 %collective-permute-start.18 = (f32[512,256]{1,0:T(8,128)}, f32[512,256]{1,0:T(8,128)S(1)}, u32[]{:S(2)}, u32[]{:S(2)}) collective-permute-start(f32[512,256]{1,0:T(8,128)} %get-tuple-element.201), channel_id=1, source_target_pairs={{0,8},{4,12},{8,16},{12,20},{16,24},{20,28},{24,0},{28,4},{1,9},{5... | collective-permute-start | bytes 1572872 | tf_op jit(solution)/shard_map/ppermute | solution.py:458
  469.1 35.1 %collective-permute-start.19 = (f32[512,256]{1,0:T(8,128)}, f32[512,256]{1,0:T(8,128)S(1)}, u32[]{:S(2)}, u32[]{:S(2)}) collective-permute-start(f32[512,256]{1,0:T(8,128)} %get-tuple-element.202), channel_id=1, source_target_pairs={{0,16},{4,20},{8,24},{12,28},{16,0},{20,4},{24,8},{28,12},{1,17},{... | collective-permute-start | bytes 1572872 | tf_op jit(solution)/shard_map/ppermute | solution.py:458
  471.2 33.1 %collective-permute-start.20 = (f32[512,256]{1,0:T(8,128)}, f32[512,256]{1,0:T(8,128)S(1)}, u32[]{:S(2)}, u32[]{:S(2)}) collective-permute-start(f32[512,256]{1,0:T(8,128)} %get-tuple-element.203), channel_id=1, source_target_pairs={{0,24},{4,28},{8,0},{12,4},{16,8},{20,12},{24,16},{28,20},{1,25},{... | collective-permute-start | bytes 1572872 | tf_op jit(solution)/shard_map/ppermute | solution.py:458
  493.5 13.8 %copy-start.23 = (f32[512,256]{1,0:T(8,128)}, f32[512,256]{1,0:T(8,128)S(1)}, u32[]{:S(2)}) copy-start(f32[512,256]{1,0:T(8,128)S(1)} %collective-permute-done.18.refs_6_) | copy-start | bytes 1572868
  504.3 3.0 copy-start.26
  504.3 3.0 copy-start.28
  507.3 1.3 copy-start.8
  573.9 54.4 %collective-permute-start.24 = (f32[4,512,256]{2,1,0:T(8,128)}, f32[4,512,256]{2,1,0:T(8,128)S(1)}, u32[]{:S(2)}, u32[]{:S(2)}) collective-permute-start(f32[4,512,256]{2,1,0:T(8,128)} %get-tuple-element.209.refs_0_), channel_id=1, source_target_pairs={{0,2},{1,3},{2,0},{3,1},{4,6},{5,7},{6,4},{7,5},{8,10},{9,11},{10,... | collective-permute-start | bytes 6291464 | tf_op jit(solution)/shard_map/ppermute | solution.py:476
  575.5 52.8 %collective-permute-start.21 = (f32[512,256]{1,0:T(8,128)}, f32[512,256]{1,0:T(8,128)S(1)}, u32[]{:S(2)}, u32[]{:S(2)}) collective-permute-start(f32[512,256]{1,0:T(8,128)} %get-tuple-element.206), channel_id=1, source_target_pairs={{0,8},{4,12},{8,16},{12,20},{16,24},{20,28},{24,0},{28,4},{1,9},{5... | collective-permute-start | bytes 1572872 | tf_op jit(solution)/shard_map/ppermute | solution.py:458
  583.4 44.9 %collective-permute-start.22 = (f32[512,256]{1,0:T(8,128)}, f32[512,256]{1,0:T(8,128)S(1)}, u32[]{:S(2)}, u32[]{:S(2)}) collective-permute-start(f32[512,256]{1,0:T(8,128)} %get-tuple-element.207), channel_id=1, source_target_pairs={{0,16},{4,20},{8,24},{12,28},{16,0},{20,4},{24,8},{28,12},{1,17},{... | collective-permute-start | bytes 1572872 | tf_op jit(solution)/shard_map/ppermute | solution.py:458
  585.2 43.1 %collective-permute-start.23 = (f32[512,256]{1,0:T(8,128)}, f32[512,256]{1,0:T(8,128)S(1)}, u32[]{:S(2)}, u32[]{:S(2)}) collective-permute-start(f32[512,256]{1,0:T(8,128)} %get-tuple-element.208), channel_id=1, source_target_pairs={{0,24},{4,28},{8,0},{12,4},{16,8},{20,12},{24,16},{28,20},{1,25},{... | collective-permute-start | bytes 1572872 | tf_op jit(solution)/shard_map/ppermute | solution.py:458
  628.3 0.8 copy-start.3
  628.3 1.0 copy-start.4
  628.3 1.1 copy-start.5
  628.4 1.8 copy-start.6
  630.1 5.2 copy-start.16
  630.9 10.6 %collective-permute-start.25 = (f32[4,512,256]{2,1,0:T(8,128)}, f32[4,512,256]{2,1,0:T(8,128)S(1)}, u32[]{:S(2)}, u32[]{:S(2)}) collective-permute-start(f32[4,512,256]{2,1,0:T(8,128)} %get-tuple-element.222), channel_id=1, source_target_pairs={{0,1},{1,0},{2,3},{3,2},{4,5},{5,4},{6,7},{7,6},{8,9},{9,8},{10,11... | collective-permute-start | bytes 6291464 | tf_op jit(solution)/shard_map/ppermute | solution.py:481
  631.0 38.2 %collective-permute-start.27 = (f32[512,256]{1,0:T(8,128)}, f32[512,256]{1,0:T(8,128)S(1)}, u32[]{:S(2)}, u32[]{:S(2)}) collective-permute-start(f32[512,256]{1,0:T(8,128)} %get-tuple-element.235), channel_id=1, source_target_pairs={{0,8},{4,12},{8,16},{12,20},{16,24},{20,28},{24,0},{28,4},{1,9},{5... | collective-permute-start | bytes 1572872 | tf_op jit(solution)/shard_map/ppermute | solution.py:458
  632.9 37.0 %collective-permute-start.28 = (f32[512,256]{1,0:T(8,128)}, f32[512,256]{1,0:T(8,128)S(1)}, u32[]{:S(2)}, u32[]{:S(2)}) collective-permute-start(f32[512,256]{1,0:T(8,128)} %get-tuple-element.236), channel_id=1, source_target_pairs={{0,16},{4,20},{8,24},{12,28},{16,0},{20,4},{24,8},{28,12},{1,17},{... | collective-permute-start | bytes 1572872 | tf_op jit(solution)/shard_map/ppermute | solution.py:458
  634.7 35.3 %collective-permute-start.29 = (f32[512,256]{1,0:T(8,128)}, f32[512,256]{1,0:T(8,128)}, u32[]{:S(2)}, u32[]{:S(2)}) collective-permute-start(f32[512,256]{1,0:T(8,128)} %get-tuple-element.237), channel_id=1, source_target_pairs={{0,24},{4,28},{8,0},{12,4},{16,8},{20,12},{24,16},{28,20},{1,25},{... | collective-permute-start | bytes 1572872 | tf_op jit(solution)/shard_map/ppermute | solution.py:458
  641.5 1.3 copy-start
  669.2 6.8 collective-permute-start.26
  669.3 0.8 copy-start.11
  669.9 0.8 copy-start.12
  676.0 6.0 copy-start.13
  676.1 6.0 copy-start.14
  676.1 6.0 copy-start.15

commit v5 on v4

--- a/solution.py
+++ b/solution.py
@@ -124,20 +124,24 @@
     return found[0] if together else found
 
 
-def gate_call(chain, arrays, pieces=()):
+def gate_call(chain, arrays, pieces=(), hint=0):
     n, parts = len(arrays), len(pieces)
     anywhere = pl.BlockSpec(memory_space=pl.ANY)
     outs = [(array.shape, array.dtype) for array in arrays]
 
     def body(place, *refs):
         if parts:
-            given, whole, sems = refs[n : n + parts], refs[2 * n + parts], refs[-1]
-            copies = []
+            given, whole, (held, sems) = refs[n : n + parts], refs[2 * n + parts], refs[-2:]
+            coming = [pltpu.make_async_copy(given[k], held.at[k], sems.at[k]) for k in range(parts)]
+            for copy in coming:
+                copy.start()
+            going = []
             for k in range(parts):
+                coming[k].wait()
                 block = lax.rem(place[0] + parts - k, parts)
-                copies.append(pltpu.make_async_copy(given[k], whole.at[block], sems.at[k]))
-                copies[-1].start()
-            for copy in copies:
+                going.append(pltpu.make_async_copy(held.at[k], whole.at[block], sems.at[parts + k]))
+                going[k].start()
+            for copy in going:
                 copy.wait()
 
     if parts:
@@ -150,9 +154,9 @@
         [anywhere] * (n + parts),
         outs,
         [anywhere] * len(outs),
-        scratch=[pltpu.SemaphoreType.DMA((parts,))] if parts else (),
+        scratch=[pltpu.VMEM(outs[-1][0], F32), pltpu.SemaphoreType.DMA((2 * parts,))] if parts else (),
         aliases=[(k, k) for k in range(n)],
-        bytes_hint=20 << 20,
+        bytes_hint=hint,
     )
 
 
@@ -520,16 +524,16 @@
     def mask(p, together):
         return mask_call(chain, observed, direction, p, n_z, together)
 
-    def pass_on(*groups, pieces=()):
-        found = gate_call(chain, [array for group in groups for array in group], pieces)
+    def pass_on(*groups, pieces=(), hint=0):
+        found = gate_call(chain, [array for group in groups for array in group], pieces, hint)
         flat = iter(found)
         kept = [[next(flat) for _ in group] for group in groups]
         return kept + [found[-1]] if pieces else kept
 
+    mask2 = mask(2, True)
     mask0 = mask(0, False)
-    mask2 = mask(2, True)
+    x2 = over_x(mask2)
     out0 = over_z(mask0)
-    x2 = over_x(mask2)
     mask1 = mask(1, True)
     mask3 = mask(3, True)
     time = entries_call(chain, day_features, t_loc, n_x, n_c, time_row, time_col, time_range, DAYS, "time_entries")
@@ -540,7 +544,7 @@
     y0 = over_y(cells0)
     terms2 = time_call(chain, [mask2] + x2, time, n_c)
     matrices = [space_entries(0, (0, 1), ())]
-    x3, y0 = pass_on(x3[1:], y0[1:])
+    x3, y0 = pass_on(x3[1:], y0[1:], hint=20 << 20)
     inner2 = add_call(chain, over_core(terms2), True)
     (cells1,), (inner2,) = pass_on([out1], [inner2])
 
@@ -549,29 +553,28 @@
     terms3 = time_call(chain, [mask3] + x3, time, n_c)
     for k in range(1, n_y):
         matrices.append(space_entries(k, (0, 1), ()))
-    (y1,) = pass_on(y1[1:])
     inner3 = add_call(chain, over_core(terms3), False)
     (cells2,), inner3 = pass_on([out2], inner3)
 
     out3 = over_z(inner3)
     y2 = over_y(cells2)
     smooth0 = space([cells0] + y0, False)
-    y2, smooth0, cells3 = pass_on(y2[1:], smooth0, pieces=out3)
+    smooth0, cells3 = pass_on(smooth0, pieces=out3)
 
     home0 = over_z(smooth0)
     y3 = over_y(cells3)
-    smooth1 = space([cells1] + y1, False)
-    y3, smooth1, home0 = pass_on(y3[1:], smooth1, pieces=home0)
+    smooth1 = space(y1, False)
+    smooth1, home0 = pass_on(smooth1, pieces=home0)
 
     home1 = over_z(smooth1)
     x0 = over_x(home0)
-    smooth2 = space([cells2] + y2, False)
-    x0, smooth2, home1 = pass_on(x0[1:], smooth2, pieces=home1)
+    smooth2 = space(y2, False)
+    smooth2, home1 = pass_on(smooth2, pieces=home1)
 
     home2 = over_z(smooth2)
     x1 = over_x(home1)
-    smooth3 = space([cells3] + y3, False)
-    terms0 = time_call(chain, [home0] + x0, time, n_c)
+    smooth3 = space(y3, False)
+    terms0 = time_call(chain, x0, time, n_c)
     home2, x1, terms0, smooth3 = pass_on(home2, x1[1:], terms0, smooth3)
 
     home3 = over_z(smooth3)

time: 739 us -> 483 us (0.65)
  Pallas kernels: 564 us -> 315 us
  waiting for transfers between devices: 69.3 us -> 44.8 us
  starting transfers between devices: 60.5 us -> 81.1 us
    pallas_call x31 -> x30, Pallas kernels: 564 us -> 315 us  [__call__(): pl.pallas_call(kernel, grid_spec=pltpu.PrefetchScalarGridSpec(num_scalar_...]
    ppermute x4, waiting for transfers between devices: 20.5 us -> 0.01 us  [over_y(): found.append(lax.ppermute(cells, 'sta', pairs))]
    ppermute x18, starting transfers between devices: 38.5 us -> 55.2 us  [over_z(): found.append(lax.ppermute(pieces[k], 'sta', pairs))]
    ppermute x4, waiting for transfers between devices: 11.6 us -> 3.8 us  [over_x(): found.append(lax.ppermute(cells, 'day', pairs))]
  transfers between devices with their start and end apart: 32 -> 32, of which waited for: 13 -> 9; matrix products, arithmetic and copies ran while one was open for 0% -> 0% of each run, Pallas kernels for 35% -> 57%
where the time goes in v5:
time: 483 us; the launch traced here: 482 us
  Pallas kernels  315 us (65%)
  starting transfers between devices  81.1 us (17%)
  waiting for transfers between devices  44.8 us (9%)
  blocking collectives  28.6 us (6%)
  local copies, waits for them, and re-layouts  10.1 us (2%)
    pallas_call x30, Pallas kernels, __call__(): pl.pallas_call(kernel, grid_spec=pltpu.PrefetchScalarGridSpec(num_scalar_...  315 us
    ppermute x18, starting transfers between devices, over_z(): found.append(lax.ppermute(pieces[k], 'sta', pairs))  55.2 us
    ppermute x18, waiting for transfers between devices, over_z(): found.append(lax.ppermute(pieces[k], 'sta', pairs))  31.5 us
    all_to_all x1, blocking collectives, over_all(): return lax.all_to_all(many, ('sta', 'day'), 0, 0, tiled=True)  28.6 us
    all_to_all x2, starting transfers between devices, over_z_at_once(): lax.all_to_all(pieces, 'sta', 0, 0, axis_index_groups=groups, tiled=True)  13.8 us
  transfers between devices with their start and end apart: 32, of which 9 were waited for; matrix products, arithmetic and copies ran while one was open for 0% of the time, Pallas kernels for 57%

profile of v5, /device:TPU:0, one launch (start us, length us, event | category | flops | bytes accessed | tf_op | source)
XLA Modules:
  0.0 482.1 jit_solution(8721807912390077867)
XLA Ops:
  1.3 4.0 mask.4
  5.3 2.9 collective-permute-start
  8.2 4.0 mask.5
  12.2 1.6 collective-permute-start.1
  13.8 2.6 collective-permute-start.2
  16.3 1.3 collective-permute-start.3
  17.7 4.0 mask.6
  21.7 4.0 mask.7
  25.6 22.3 %time_entries.1 = (bf16[2048,2048]{1,0:T(8,128)(2,1)}, bf16[2048,2048]{1,0:T(8,128)(2,1)}, f32[8,128]{1,0:T(8,128)}) custom-call(s32[4]{0:T(128)} %pad_add_fusion.place, f32[4,4096]{1,0:T(4,128)} %refs_1_.12, f32[4,4096]{1,0:T(4,128)} %refs_1_.12, f32[8,128]{1,0:T(8,128)} %get-tuple-element.130.refs_2_), custom_call_target="tpu_custom_call" | custom-call | tf_op jit(solution)/shard_map/time_entries/pallas_call | solution.py:40
  47.9 2.3 collective-permute-done.2.refs_5_
  50.2 3.8 collective-permute-done.refs_2_
  54.1 1.3 copy-done.3
  55.4 3.1 gate.8
  58.4 1.8 collective-permute-start.5
  60.2 1.5 collective-permute-start.6
  61.8 9.3 %all-to-all-start = ((f32[4,512,256]{2,1,0:T(8,128)}), f32[4,512,256]{2,1,0:T(8,128)S(1)}, u32[]{:S(2)}, u32[]{:S(2)}) async-start(f32[4,512,256]{2,1,0:T(8,128)} %get-tuple-element.132), calls=%async_computation | async-start | bytes 4194304 | tf_op jit(solution)/shard_map/all_to_all | solution.py:467
  71.1 20.5 %time.4 = (f32[4,512,256]{2,1,0:T(8,128)}, f32[4,512,256]{2,1,0:T(8,128)}, f32[8,128]{1,0:T(8,128)}) custom-call(s32[4]{0:T(128)} %pad_add_fusion.place, f32[4,512,256]{2,1,0:T(8,128)} %get-tuple-element.125.refs_0_, f32[4,512,256]{2,1,0:T(8,128)} %get-tuple-element.133.refs_1_, bf16[2048,2048]{1,0:T(8,128)(2,1)} %get-tuple-element.134.refs_2_, ...), custom_call_target="tpu_custom_call" | custom-call | tf_op jit(solution)/shard_map/time/pallas_call | solution.py:40
  91.5 17.4 %space_entries.2 = (bf16[2048,2048]{1,0:T(8,128)(2,1)}, bf16[2048,2048]{1,0:T(8,128)(2,1)}, f32[8,128]{1,0:T(8,128)}) custom-call(s32[4]{0:T(128)} %pad_add_fusion.place, f32[2,4096]{1,0:T(2,128)} %refs_3_.8, f32[2,4096]{1,0:T(2,128)} %refs_3_.8, f32[2,4096]{1,0:T(2,128)} %refs_3_.8, f32[2,4096]{1,0:T(2,128)} %refs_3_.8, f32[8,128]{1,0:T(8,128)} %get-tuple-element.141.refs_4_), custom_call_target="tpu_custom_call" | custom-call | tf_op jit(solution)/shard_map/space_entries/pallas_call | solution.py:40
  109.7 3.9 add.19
  113.6 4.1 all-to-all-done.refs_0_
  117.8 1.3 copy-done
  119.7 4.5 all-to-all-start.1
  124.2 20.6 %time.5 = (f32[4,512,256]{2,1,0:T(8,128)}, f32[4,512,256]{2,1,0:T(8,128)}, f32[8,128]{1,0:T(8,128)}) custom-call(s32[4]{0:T(128)} %pad_add_fusion.place, f32[4,512,256]{2,1,0:T(8,128)} %get-tuple-element.139.refs_0_, f32[4,512,256]{2,1,0:T(8,128)} %get-tuple-element.147.refs_1_, bf16[2048,2048]{1,0:T(8,128)(2,1)} %get-tuple-element.134.refs_2_, ...), custom_call_target="tpu_custom_call" | custom-call | tf_op jit(solution)/shard_map/time/pallas_call | solution.py:40
  145.4 17.3 %space_entries.3 = (bf16[2048,2048]{1,0:T(8,128)(2,1)}, bf16[2048,2048]{1,0:T(8,128)(2,1)}, f32[8,128]{1,0:T(8,128)}) custom-call(s32[4]{0:T(128)} %pad_add_fusion.place, f32[2,4096]{1,0:T(2,128)} %refs_3_.8, f32[2,4096]{1,0:T(2,128)} %refs_3_.8, f32[2,4096]{1,0:T(2,128)} %refs_3_.8, f32[2,4096]{1,0:T(2,128)} %refs_3_.8, f32[8,128]{1,0:T(8,128)} %get-tuple-element.151.refs_4_), custom_call_target="tpu_custom_call" | custom-call | tf_op jit(solution)/shard_map/space_entries/pallas_call | solution.py:40
  162.7 4.0 add.20
  166.7 5.3 %all-to-all-done.1.refs_0_ = f32[4,512,256]{2,1,0:T(8,128)} async-done(((f32[4,512,256]{2,1,0:T(8,128)}), f32[4,512,256]{2,1,0:T(8,128)}, u32[]{:S(2)}, u32[]{:S(2)}) %all-to-all-start.1) | async-done | bytes 2097184 | tf_op jit(solution)/shard_map/all_to_all | solution.py:467
  173.2 2.7 collective-permute-start.11
  176.0 1.1 collective-permute-start.12
  177.0 22.0 %space.4 = (f32[512,256]{1,0:T(8,128)}, f32[512,256]{1,0:T(8,128)}, f32[512,256]{1,0:T(8,128)}, f32[512,256]{1,0:T(8,128)}, f32[8,128]{1,0:T(8,128)}) custom-call(s32[4]{0:T(128)} %pad_add_fusion.place, f32[4,512,256]{2,1,0:T(8,128)} %get-tuple-element.140.refs_0_, f32[4,512,256]{2,1,0:T(8,128)} %get-tuple-element.164.refs_1_, ...), custom_call_target="tpu_custom_call" | custom-call | tf_op jit(solution)/shard_map/space/pallas_call | solution.py:40
  199.1 11.4 %collective-permute-done.11.refs_6_ = f32[512,256]{1,0:T(8,128)S(1)} collective-permute-done((f32[512,256]{1,0:T(8,128)}, f32[512,256]{1,0:T(8,128)S(1)}, u32[]{:S(2)}, u32[]{:S(2)}) %collective-permute-start.11) | collective-permute-done | bytes 524320 | tf_op jit(solution)/shard_map/ppermute | solution.py:462
  211.4 3.1 gate.12
  214.5 10.7 %collective-permute-start.13 = (f32[512,256]{1,0:T(8,128)}, f32[512,256]{1,0:T(8,128)S(1)}, u32[]{:S(2)}, u32[]{:S(2)}) collective-permute-start(f32[512,256]{1,0:T(8,128)} %get-tuple-element.181), channel_id=1, source_target_pairs={{0,8},{4,12},{8,16},{12,20},{16,24},{20,28},{24,0},{28,4},{1,9},{5... | collective-permute-start | bytes 1572872 | tf_op jit(solution)/shard_map/ppermute | solution.py:462
  225.2 2.4 collective-permute-start.15
  227.7 22.0 %space.5 = (f32[512,256]{1,0:T(8,128)}, f32[512,256]{1,0:T(8,128)}, f32[512,256]{1,0:T(8,128)}, f32[512,256]{1,0:T(8,128)}, f32[8,128]{1,0:T(8,128)}) custom-call(s32[4]{0:T(128)} %pad_add_fusion.place, f32[4,512,256]{2,1,0:T(8,128)} %get-tuple-element.163.refs_0_, f32[4,512,256]{2,1,0:T(8,128)} %collective-permute-done.9.refs_1_, ...), custom_call_target="tpu_custom_call" | custom-call | tf_op jit(solution)/shard_map/space/pallas_call | solution.py:40
  249.7 7.6 %collective-permute-done.14.refs_6_ = f32[512,256]{1,0:T(8,128)S(1)} collective-permute-done((f32[512,256]{1,0:T(8,128)}, f32[512,256]{1,0:T(8,128)S(1)}, u32[]{:S(2)}, u32[]{:S(2)}) %collective-permute-start.14) | collective-permute-done | bytes 524320 | tf_op jit(solution)/shard_map/ppermute | solution.py:462
  257.3 1.2 collective-permute-done.15.refs_7_
  258.6 0.8 copy-done.18
  259.4 3.1 gate.13
  262.4 11.7 %collective-permute-start.16 = (f32[512,256]{1,0:T(8,128)}, f32[512,256]{1,0:T(8,128)S(1)}, u32[]{:S(2)}, u32[]{:S(2)}) collective-permute-start(f32[512,256]{1,0:T(8,128)} %get-tuple-element.191), channel_id=1, source_target_pairs={{0,8},{4,12},{8,16},{12,20},{16,24},{20,28},{24,0},{28,4},{1,9},{5... | collective-permute-start | bytes 1572872 | tf_op jit(solution)/shard_map/ppermute | solution.py:462
  274.2 3.3 collective-permute-start.17
  277.4 1.5 collective-permute-start.24
  279.0 1.5 collective-permute-start.23
  280.4 22.0 %space.6 = (f32[512,256]{1,0:T(8,128)}, f32[512,256]{1,0:T(8,128)}, f32[512,256]{1,0:T(8,128)}, f32[512,256]{1,0:T(8,128)}, f32[8,128]{1,0:T(8,128)}) custom-call(s32[4]{0:T(128)} %pad_add_fusion.place, f32[4,512,256]{2,1,0:T(8,128)} %get-tuple-element.158.refs_0_, f32[4,512,256]{2,1,0:T(8,128)} %collective-permute-done.8.refs_1_, ...), custom_call_target="tpu_custom_call" | custom-call | tf_op jit(solution)/shard_map/space/pallas_call | solution.py:40
  302.5 7.8 %collective-permute-done.17.refs_6_ = f32[512,256]{1,0:T(8,128)S(1)} collective-permute-done((f32[512,256]{1,0:T(8,128)}, f32[512,256]{1,0:T(8,128)S(1)}, u32[]{:S(2)}, u32[]{:S(2)}) %collective-permute-start.17) | collective-permute-done | bytes 524320 | tf_op jit(solution)/shard_map/ppermute | solution.py:462
  310.3 0.8 copy-done.11
  311.3 3.2 gate.14
  314.5 1.6 collective-permute-start.22
  316.0 11.5 %collective-permute-start.19 = (f32[512,256]{1,0:T(8,128)}, f32[512,256]{1,0:T(8,128)S(1)}, u32[]{:S(2)}, u32[]{:S(2)}) collective-permute-start(f32[512,256]{1,0:T(8,128)} %get-tuple-element.196), channel_id=1, source_target_pairs={{0,8},{4,12},{8,16},{12,20},{16,24},{20,28},{24,0},{28,4},{1,9},{5... | collective-permute-start | bytes 1572872 | tf_op jit(solution)/shard_map/ppermute | solution.py:462
  327.7 2.2 collective-permute-start.21
  329.9 22.0 %space.7 = (f32[512,256]{1,0:T(8,128)}, f32[512,256]{1,0:T(8,128)}, f32[512,256]{1,0:T(8,128)}, f32[512,256]{1,0:T(8,128)}, f32[8,128]{1,0:T(8,128)}) custom-call(s32[4]{0:T(128)} %pad_add_fusion.place, f32[4,512,256]{2,1,0:T(8,128)} %get-tuple-element.201.refs_0_, f32[4,512,256]{2,1,0:T(8,128)} %collective-permute-done.24.refs_1_, ...), custom_call_target="tpu_custom_call" | custom-call | tf_op jit(solution)/shard_map/space/pallas_call | solution.py:40
  352.0 20.5 %time.6 = (f32[4,512,256]{2,1,0:T(8,128)}, f32[4,512,256]{2,1,0:T(8,128)}, f32[8,128]{1,0:T(8,128)}) custom-call(s32[4]{0:T(128)} %pad_add_fusion.place, f32[4,512,256]{2,1,0:T(8,128)} %get-tuple-element.200.refs_0_, f32[4,512,256]{2,1,0:T(8,128)} %collective-permute-done.23.refs_1_, bf16[2048,2048]{1,0:T(8,128)(2,1)} %get-tuple-element.134.refs_2_, ...), custom_call_target="tpu_custom_call" | custom-call | tf_op jit(solution)/shard_map/time/pallas_call | solution.py:40
  374.3 0.8 gate.15
  375.2 1.0 collective-permute-start.27
  376.2 2.7 collective-permute-start.28
  379.0 0.9 copy.46.refs_1_.refs_2_
  379.9 5.3 %sums.4 = (f32[8,128]{1,0:T(8,128)}, f32[8,128]{1,0:T(8,128)}) custom-call(s32[4]{0:T(128)} %pad_add_fusion.place, s32[512,1024]{1,0:T(8,128)} %refs_1_.15, f32[512,1]{1,0:T(8,128)} %copy.46.refs_1_.refs_2_, f32[4,512,1024]{2,1,0:T(8,128)} %refs_4_.1, f32[4,512,1024]{2,1,0:T(8,128)} %refs_5_.1, f32[512,256]{1,0:T(8,128)} %get-tuple-element.213.refs_4_.refs_10_, ...), custom_call_target="tpu_custom_call" | custom-call | tf_op jit(solution)/shard_map/sums/pallas_call | solution.py:40
  385.2 1.3 copy-done.4
  386.5 6.0 %sums.5 = (f32[8,128]{1,0:T(8,128)}, f32[8,128]{1,0:T(8,128)}) custom-call(s32[4]{0:T(128)} %pad_add_fusion.place, s32[512,1024]{1,0:T(8,128)} %refs_1_.15, f32[512,1]{1,0:T(8,128)} %copy.46.refs_1_.refs_2_, f32[4,512,1024]{2,1,0:T(8,128)} %refs_4_.1, f32[4,512,1024]{2,1,0:T(8,128)} %refs_5_.1, f32[4,512,256]{2,1,0:T(8,128)} %get-tuple-element.211.refs_4_.refs_6_, ...), custom_call_target="tpu_custom_call" | custom-call | tf_op jit(solution)/shard_map/sums/pallas_call | solution.py:40
  392.5 20.5 %time.7 = (f32[4,512,256]{2,1,0:T(8,128)}, f32[4,512,256]{2,1,0:T(8,128)}, f32[8,128]{1,0:T(8,128)}) custom-call(s32[4]{0:T(128)} %pad_add_fusion.place, f32[4,512,256]{2,1,0:T(8,128)} %get-tuple-element.199.refs_0_, f32[4,512,256]{2,1,0:T(8,128)} %get-tuple-element.220.refs_1_, bf16[2048,2048]{1,0:T(8,128)(2,1)} %get-tuple-element.134.refs_2_, ...), custom_call_target="tpu_custom_call" | custom-call | tf_op jit(solution)/shard_map/time/pallas_call | solution.py:40
  413.0 1.1 collective-permute-done.28.refs_6_.refs_16_
  414.9 5.3 %sums.6 = (f32[8,128]{1,0:T(8,128)}, f32[8,128]{1,0:T(8,128)}) custom-call(s32[4]{0:T(128)} %pad_add_fusion.place, s32[512,1024]{1,0:T(8,128)} %refs_1_.15, f32[512,1]{1,0:T(8,128)} %copy.46.refs_1_.refs_2_, f32[4,512,1024]{2,1,0:T(8,128)} %refs_4_.1, f32[4,512,1024]{2,1,0:T(8,128)} %refs_5_.1, f32[512,256]{1,0:T(8,128)} %get-tuple-element.224.refs_4_.refs_14_, ...), custom_call_target="tpu_custom_call" | custom-call | flops 241172480000 | bytes 209715200 | tf_op jit(solution)/shard_map/sums/pallas_call | solution.py:40
  420.2 6.0 %sums.7 = (f32[8,128]{1,0:T(8,128)}, f32[8,128]{1,0:T(8,128)}) custom-call(s32[4]{0:T(128)} %pad_add_fusion.place, s32[512,1024]{1,0:T(8,128)} %refs_1_.15, f32[512,1]{1,0:T(8,128)} %copy.46.refs_1_.refs_2_, f32[4,512,1024]{2,1,0:T(8,128)} %refs_4_.1, f32[4,512,1024]{2,1,0:T(8,128)} %refs_5_.1, f32[4,512,256]{2,1,0:T(8,128)} %get-tuple-element.222.refs_4_.refs_8_, ...), custom_call_target="tpu_custom_call" | custom-call | tf_op jit(solution)/shard_map/sums/pallas_call | solution.py:40
  427.0 28.6 %all_to_all.15.refs_0_ = f32[32,32,128]{2,1,0:T(8,128)} all-to-all(f32[32,32,128]{2,1,0:T(8,128)S(1)} %broadcast_in_dim.10), channel_id=1, replica_groups=mesh['sta'=8,'day'=4] {'sta','day'}, dimensions={0} | all-to-all | bytes 1048576 | tf_op jit(solution)/shard_map/all_to_all | solution.py:490
  455.6 26.3 %update.1 = (f32[4,512,1024]{2,1,0:T(8,128)}, f32[4,512,1024]{2,1,0:T(8,128)}, f32[4,512,1024]{2,1,0:T(8,128)}, f32[8,128]{1,0:T(8,128)}) custom-call(s32[4]{0:T(128)} %pad_add_fusion.place, f32[32,32,128]{2,1,0:T(8,128)} %all_to_all.15.refs_0_, s32[512,1024]{1,0:T(8,128)} %refs_1_.15, f32[512,1]{1,0:T(8,128)} %copy.46.refs_1_.refs_2_, ...), custom_call_target="tpu_custom_call" | custom-call | tf_op jit(solution)/shard_map/update/pallas_call | solution.py:40
  (87 shorter events, 8.7 us)
Async XLA Ops:
  5.3 48.8 %collective-permute-start = (f32[4,512,256]{2,1,0:T(8,128)}, f32[4,512,256]{2,1,0:T(8,128)S(1)}, u32[]{:S(2)}, u32[]{:S(2)}) collective-permute-start(f32[4,512,256]{2,1,0:T(8,128)} %get-tuple-element.125.refs_0_), channel_id=1, source_target_pairs={{0,2},{1,3},{2,0},{3,1},{4,6},{5,7},{6,4},{7,5},{8,10},{9,11},{10,... | collective-permute-start | bytes 6291464 | tf_op jit(solution)/shard_map/ppermute | solution.py:480
  12.2 35.8 %collective-permute-start.1 = (f32[512,256]{1,0:T(8,128)}, f32[512,256]{1,0:T(8,128)S(1)}, u32[]{:S(2)}, u32[]{:S(2)}) collective-permute-start(f32[512,256]{1,0:T(8,128)} %get-tuple-element.127), channel_id=1, source_target_pairs={{0,8},{4,12},{8,16},{12,20},{16,24},{20,28},{24,0},{28,4},{1,9},{5... | collective-permute-start | bytes 1572872 | tf_op jit(solution)/shard_map/ppermute | solution.py:462
  13.8 36.5 %collective-permute-start.2 = (f32[512,256]{1,0:T(8,128)}, f32[512,256]{1,0:T(8,128)S(1)}, u32[]{:S(2)}, u32[]{:S(2)}) collective-permute-start(f32[512,256]{1,0:T(8,128)} %get-tuple-element.128), channel_id=1, source_target_pairs={{0,16},{4,20},{8,24},{12,28},{16,0},{20,4},{24,8},{28,12},{1,17},{... | collective-permute-start | bytes 1572872 | tf_op jit(solution)/shard_map/ppermute | solution.py:462
  16.3 33.9 %collective-permute-start.3 = (f32[512,256]{1,0:T(8,128)}, f32[512,256]{1,0:T(8,128)S(1)}, u32[]{:S(2)}, u32[]{:S(2)}) collective-permute-start(f32[512,256]{1,0:T(8,128)} %get-tuple-element.129), channel_id=1, source_target_pairs={{0,24},{4,28},{8,0},{12,4},{16,8},{20,12},{24,16},{28,20},{1,25},{... | collective-permute-start | bytes 1572872 | tf_op jit(solution)/shard_map/ppermute | solution.py:462
  47.9 6.1 %copy-start.19 = (f32[512,256]{1,0:T(8,128)}, f32[512,256]{1,0:T(8,128)S(1)}, u32[]{:S(2)}) copy-start(f32[512,256]{1,0:T(8,128)S(1)} %collective-permute-done.1.refs_4_) | copy-start | bytes 1572868
  50.2 3.8 copy-start.20
  50.2 3.8 copy-start.21
  54.0 1.3 copy-start.3
  58.4 50.6 %collective-permute-start.5 = (f32[4,512,256]{2,1,0:T(8,128)}, f32[4,512,256]{2,1,0:T(8,128)}, u32[]{:S(2)}, u32[]{:S(2)}) collective-permute-start(f32[4,512,256]{2,1,0:T(8,128)} %get-tuple-element.139.refs_0_), channel_id=1, source_target_pairs={{0,2},{1,3},{2,0},{3,1},{4,6},{5,7},{6,4},{7,5},{8,10},{9,11},{10,... | collective-permute-start | bytes 6291464 | tf_op jit(solution)/shard_map/ppermute | solution.py:480
  60.2 48.7 %collective-permute-start.6 = (f32[4,512,256]{2,1,0:T(8,128)}, f32[4,512,256]{2,1,0:T(8,128)}, u32[]{:S(2)}, u32[]{:S(2)}) collective-permute-start(f32[4,512,256]{2,1,0:T(8,128)} %get-tuple-element.140.refs_0_), channel_id=1, source_target_pairs={{0,4},{4,0},{8,12},{12,8},{16,20},{20,16},{24,28},{28,24},{1,5},{5... | collective-permute-start | bytes 6291464 | tf_op jit(solution)/shard_map/ppermute | solution.py:473
  61.8 56.0 %all-to-all-start = ((f32[4,512,256]{2,1,0:T(8,128)}), f32[4,512,256]{2,1,0:T(8,128)S(1)}, u32[]{:S(2)}, u32[]{:S(2)}) async-start(f32[4,512,256]{2,1,0:T(8,128)} %get-tuple-element.132), calls=%async_computation | async-start | bytes 4194304 | tf_op jit(solution)/shard_map/all_to_all | solution.py:467
  91.5 18.1 %collective-permute-start.4 = (f32[4,512,256]{2,1,0:T(8,128)}, f32[4,512,256]{2,1,0:T(8,128)}, u32[]{:S(2)}, u32[]{:S(2)}) collective-permute-start(f32[4,512,256]{2,1,0:T(8,128)} %get-tuple-element.138), channel_id=1, source_target_pairs={{0,1},{1,0},{2,3},{3,2},{4,5},{5,4},{6,7},{7,6},{8,9},{9,8},{10,11... | collective-permute-start | bytes 6291464 | tf_op jit(solution)/shard_map/ppermute | solution.py:485
  117.8 1.3 copy-start
  119.7 52.2 %all-to-all-start.1 = ((f32[4,512,256]{2,1,0:T(8,128)}), f32[4,512,256]{2,1,0:T(8,128)}, u32[]{:S(2)}, u32[]{:S(2)}) async-start(f32[4,512,256]{2,1,0:T(8,128)} %get-tuple-element.146), calls=%async_computation.1 | async-start | bytes 4194304 | tf_op jit(solution)/shard_map/all_to_all | solution.py:467
  124.2 20.6 %copy-start.1 = (f32[4,512,256]{2,1,0:T(8,128)S(1)}, f32[4,512,256]{2,1,0:T(8,128)}, u32[]{:S(2)}) copy-start(f32[4,512,256]{2,1,0:T(8,128)} %get-tuple-element.163.refs_0_) | copy-start | bytes 6291460
  144.8 17.9 %collective-permute-start.7 = (f32[4,512,256]{2,1,0:T(8,128)}, f32[4,512,256]{2,1,0:T(8,128)}, u32[]{:S(2)}, u32[]{:S(2)}) collective-permute-start(f32[4,512,256]{2,1,0:T(8,128)} %get-tuple-element.150), channel_id=1, source_target_pairs={{0,1},{1,0},{2,3},{3,2},{4,5},{5,4},{6,7},{7,6},{8,9},{9,8},{10,11... | collective-permute-start | bytes 6291464 | tf_op jit(solution)/shard_map/ppermute | solution.py:485
  144.8 82.9 %collective-permute-start.9 = (f32[4,512,256]{2,1,0:T(8,128)S(1)}, f32[4,512,256]{2,1,0:T(8,128)}, u32[]{:S(2)}, u32[]{:S(2)}) collective-permute-start(f32[4,512,256]{2,1,0:T(8,128)S(1)} %copy-done.1), channel_id=1, source_target_pairs={{0,4},{4,0},{8,12},{12,8},{16,20},{20,16},{24,28},{28,24},{1,5},{5... | collective-permute-start | bytes 6291464 | tf_op jit(solution)/shard_map/ppermute | solution.py:473
  172.6 106.3 %collective-permute-start.8 = (f32[4,512,256]{2,1,0:T(8,128)}, f32[4,512,256]{2,1,0:T(8,128)}, u32[]{:S(2)}, u32[]{:S(2)}) collective-permute-start(f32[4,512,256]{2,1,0:T(8,128)} %get-tuple-element.158.refs_0_), channel_id=1, source_target_pairs={{0,4},{4,0},{8,12},{12,8},{16,20},{20,16},{24,28},{28,24},{1,5},{5... | collective-permute-start | bytes 6291464 | tf_op jit(solution)/shard_map/ppermute | solution.py:473
  173.2 25.8 %collective-permute-start.10 = (f32[512,256]{1,0:T(8,128)}, f32[512,256]{1,0:T(8,128)S(1)}, u32[]{:S(2)}, u32[]{:S(2)}) collective-permute-start(f32[512,256]{1,0:T(8,128)} %get-tuple-element.171), channel_id=1, source_target_pairs={{0,8},{4,12},{8,16},{12,20},{16,24},{20,28},{24,0},{28,4},{1,9},{5... | collective-permute-start | bytes 1572872 | tf_op jit(solution)/shard_map/ppermute | solution.py:462
  173.2 37.3 %collective-permute-start.11 = (f32[512,256]{1,0:T(8,128)}, f32[512,256]{1,0:T(8,128)S(1)}, u32[]{:S(2)}, u32[]{:S(2)}) collective-permute-start(f32[512,256]{1,0:T(8,128)} %get-tuple-element.172), channel_id=1, source_target_pairs={{0,16},{4,20},{8,24},{12,28},{16,0},{20,4},{24,8},{28,12},{1,17},{... | collective-permute-start | bytes 1572872 | tf_op jit(solution)/shard_map/ppermute | solution.py:462
  176.0 34.5 %collective-permute-start.12 = (f32[512,256]{1,0:T(8,128)}, f32[512,256]{1,0:T(8,128)S(1)}, u32[]{:S(2)}, u32[]{:S(2)}) collective-permute-start(f32[512,256]{1,0:T(8,128)} %get-tuple-element.173), channel_id=1, source_target_pairs={{0,24},{4,28},{8,0},{12,4},{16,8},{20,12},{24,16},{28,20},{1,25},{... | collective-permute-start | bytes 1572872 | tf_op jit(solution)/shard_map/ppermute | solution.py:462
  199.1 11.4 %copy-start.13 = (f32[512,256]{1,0:T(8,128)}, f32[512,256]{1,0:T(8,128)S(1)}, u32[]{:S(2)}) copy-start(f32[512,256]{1,0:T(8,128)S(1)} %collective-permute-done.10.refs_5_) | copy-start | bytes 1572868
  210.5 0.8 copy-start.15
  210.5 1.0 copy-start.17
  214.5 35.1 %collective-permute-start.13 = (f32[512,256]{1,0:T(8,128)}, f32[512,256]{1,0:T(8,128)S(1)}, u32[]{:S(2)}, u32[]{:S(2)}) collective-permute-start(f32[512,256]{1,0:T(8,128)} %get-tuple-element.181), channel_id=1, source_target_pairs={{0,8},{4,12},{8,16},{12,20},{16,24},{20,28},{24,0},{28,4},{1,9},{5... | collective-permute-start | bytes 1572872 | tf_op jit(solution)/shard_map/ppermute | solution.py:462
  225.2 32.1 %collective-permute-start.14 = (f32[512,256]{1,0:T(8,128)}, f32[512,256]{1,0:T(8,128)S(1)}, u32[]{:S(2)}, u32[]{:S(2)}) collective-permute-start(f32[512,256]{1,0:T(8,128)} %get-tuple-element.182), channel_id=1, source_target_pairs={{0,16},{4,20},{8,24},{12,28},{16,0},{20,4},{24,8},{28,12},{1,17},{... | collective-permute-start | bytes 1572872 | tf_op jit(solution)/shard_map/ppermute | solution.py:462
  225.2 33.3 %collective-permute-start.15 = (f32[512,256]{1,0:T(8,128)}, f32[512,256]{1,0:T(8,128)S(1)}, u32[]{:S(2)}, u32[]{:S(2)}) collective-permute-start(f32[512,256]{1,0:T(8,128)} %get-tuple-element.183), channel_id=1, source_target_pairs={{0,24},{4,28},{8,0},{12,4},{16,8},{20,12},{24,16},{28,20},{1,25},{... | collective-permute-start | bytes 1572872 | tf_op jit(solution)/shard_map/ppermute | solution.py:462
  249.7 8.9 %copy-start.14 = (f32[512,256]{1,0:T(8,128)}, f32[512,256]{1,0:T(8,128)S(1)}, u32[]{:S(2)}) copy-start(f32[512,256]{1,0:T(8,128)S(1)} %collective-permute-done.13.refs_5_) | copy-start | bytes 1572868
  257.3 1.2 copy-start.16
  258.6 0.8 copy-start.18
  262.4 40.0 %collective-permute-start.16 = (f32[512,256]{1,0:T(8,128)}, f32[512,256]{1,0:T(8,128)S(1)}, u32[]{:S(2)}, u32[]{:S(2)}) collective-permute-start(f32[512,256]{1,0:T(8,128)} %get-tuple-element.191), channel_id=1, source_target_pairs={{0,8},{4,12},{8,16},{12,20},{16,24},{20,28},{24,0},{28,4},{1,9},{5... | collective-permute-start | bytes 1572872 | tf_op jit(solution)/shard_map/ppermute | solution.py:462
  274.2 36.1 %collective-permute-start.17 = (f32[512,256]{1,0:T(8,128)}, f32[512,256]{1,0:T(8,128)S(1)}, u32[]{:S(2)}, u32[]{:S(2)}) collective-permute-start(f32[512,256]{1,0:T(8,128)} %get-tuple-element.192), channel_id=1, source_target_pairs={{0,16},{4,20},{8,24},{12,28},{16,0},{20,4},{24,8},{28,12},{1,17},{... | collective-permute-start | bytes 1572872 | tf_op jit(solution)/shard_map/ppermute | solution.py:462
  277.4 32.9 %collective-permute-start.18 = (f32[512,256]{1,0:T(8,128)}, f32[512,256]{1,0:T(8,128)S(1)}, u32[]{:S(2)}, u32[]{:S(2)}) collective-permute-start(f32[512,256]{1,0:T(8,128)} %get-tuple-element.193), channel_id=1, source_target_pairs={{0,24},{4,28},{8,0},{12,4},{16,8},{20,12},{24,16},{28,20},{1,25},{... | collective-permute-start | bytes 1572872 | tf_op jit(solution)/shard_map/ppermute | solution.py:462
  277.4 50.3 %collective-permute-start.24 = (f32[4,512,256]{2,1,0:T(8,128)}, f32[4,512,256]{2,1,0:T(8,128)}, u32[]{:S(2)}, u32[]{:S(2)}) collective-permute-start(f32[4,512,256]{2,1,0:T(8,128)} %get-tuple-element.201.refs_0_), channel_id=1, source_target_pairs={{0,4},{4,0},{8,12},{12,8},{16,20},{20,16},{24,28},{28,24},{1,5},{5... | collective-permute-start | bytes 6291464 | tf_op jit(solution)/shard_map/ppermute | solution.py:473
  279.0 73.0 %collective-permute-start.23 = (f32[4,512,256]{2,1,0:T(8,128)}, f32[4,512,256]{2,1,0:T(8,128)}, u32[]{:S(2)}, u32[]{:S(2)}) collective-permute-start(f32[4,512,256]{2,1,0:T(8,128)} %get-tuple-element.200.refs_0_), channel_id=1, source_target_pairs={{0,2},{1,3},{2,0},{3,1},{4,6},{5,7},{6,4},{7,5},{8,10},{9,11},{10,... | collective-permute-start | bytes 6291464 | tf_op jit(solution)/shard_map/ppermute | solution.py:480
  302.5 7.8 %copy-start.10 = (f32[512,256]{1,0:T(8,128)}, f32[512,256]{1,0:T(8,128)S(1)}, u32[]{:S(2)}) copy-start(f32[512,256]{1,0:T(8,128)S(1)} %collective-permute-done.16.refs_5_) | copy-start | bytes 1572868
  310.3 0.8 copy-start.11
  310.3 1.0 copy-start.12
  314.5 58.0 %collective-permute-start.22 = (f32[4,512,256]{2,1,0:T(8,128)}, f32[4,512,256]{2,1,0:T(8,128)S(1)}, u32[]{:S(2)}, u32[]{:S(2)}) collective-permute-start(f32[4,512,256]{2,1,0:T(8,128)} %get-tuple-element.199.refs_0_), channel_id=1, source_target_pairs={{0,2},{1,3},{2,0},{3,1},{4,6},{5,7},{6,4},{7,5},{8,10},{9,11},{10,... | collective-permute-start | bytes 6291464 | tf_op jit(solution)/shard_map/ppermute | solution.py:480
  316.0 56.4 %collective-permute-start.19 = (f32[512,256]{1,0:T(8,128)}, f32[512,256]{1,0:T(8,128)S(1)}, u32[]{:S(2)}, u32[]{:S(2)}) collective-permute-start(f32[512,256]{1,0:T(8,128)} %get-tuple-element.196), channel_id=1, source_target_pairs={{0,8},{4,12},{8,16},{12,20},{16,24},{20,28},{24,0},{28,4},{1,9},{5... | collective-permute-start | bytes 1572872 | tf_op jit(solution)/shard_map/ppermute | solution.py:462
  327.6 44.9 %collective-permute-start.20 = (f32[512,256]{1,0:T(8,128)}, f32[512,256]{1,0:T(8,128)S(1)}, u32[]{:S(2)}, u32[]{:S(2)}) collective-permute-start(f32[512,256]{1,0:T(8,128)} %get-tuple-element.197), channel_id=1, source_target_pairs={{0,16},{4,20},{8,24},{12,28},{16,0},{20,4},{24,8},{28,12},{1,17},{... | collective-permute-start | bytes 1572872 | tf_op jit(solution)/shard_map/ppermute | solution.py:462
  327.7 44.8 %collective-permute-start.21 = (f32[512,256]{1,0:T(8,128)}, f32[512,256]{1,0:T(8,128)S(1)}, u32[]{:S(2)}, u32[]{:S(2)}) collective-permute-start(f32[512,256]{1,0:T(8,128)} %get-tuple-element.198), channel_id=1, source_target_pairs={{0,24},{4,28},{8,0},{12,4},{16,8},{20,12},{24,16},{28,20},{1,25},{... | collective-permute-start | bytes 1572872 | tf_op jit(solution)/shard_map/ppermute | solution.py:462
  372.4 0.8 copy-start.5
  372.5 1.0 copy-start.6
  372.5 1.1 copy-start.7
  372.5 1.8 copy-start.2
  374.3 4.8 copy-start.25
  375.1 10.1 %collective-permute-start.25 = (f32[4,512,256]{2,1,0:T(8,128)}, f32[4,512,256]{2,1,0:T(8,128)S(1)}, u32[]{:S(2)}, u32[]{:S(2)}) collective-permute-start(f32[4,512,256]{2,1,0:T(8,128)} %get-tuple-element.212), channel_id=1, source_target_pairs={{0,1},{1,0},{2,3},{3,2},{4,5},{5,4},{6,7},{7,6},{8,9},{9,8},{10,11... | collective-permute-start | bytes 6291464 | tf_op jit(solution)/shard_map/ppermute | solution.py:485
  375.2 37.8 %collective-permute-start.27 = (f32[512,256]{1,0:T(8,128)}, f32[512,256]{1,0:T(8,128)S(1)}, u32[]{:S(2)}, u32[]{:S(2)}) collective-permute-start(f32[512,256]{1,0:T(8,128)} %get-tuple-element.225), channel_id=1, source_target_pairs={{0,8},{4,12},{8,16},{12,20},{16,24},{20,28},{24,0},{28,4},{1,9},{5... | collective-permute-start | bytes 1572872 | tf_op jit(solution)/shard_map/ppermute | solution.py:462
  376.2 37.9 %collective-permute-start.28 = (f32[512,256]{1,0:T(8,128)}, f32[512,256]{1,0:T(8,128)S(1)}, u32[]{:S(2)}, u32[]{:S(2)}) collective-permute-start(f32[512,256]{1,0:T(8,128)} %get-tuple-element.226), channel_id=1, source_target_pairs={{0,16},{4,20},{8,24},{12,28},{16,0},{20,4},{24,8},{28,12},{1,17},{... | collective-permute-start | bytes 1572872 | tf_op jit(solution)/shard_map/ppermute | solution.py:462
  378.9 35.2 %collective-permute-start.29 = (f32[512,256]{1,0:T(8,128)}, f32[512,256]{1,0:T(8,128)}, u32[]{:S(2)}, u32[]{:S(2)}) collective-permute-start(f32[512,256]{1,0:T(8,128)} %get-tuple-element.227), channel_id=1, source_target_pairs={{0,24},{4,28},{8,0},{12,4},{16,8},{20,12},{24,16},{28,20},{1,25},{... | collective-permute-start | bytes 1572872 | tf_op jit(solution)/shard_map/ppermute | solution.py:462
  385.2 1.3 copy-start.4
  412.9 7.2 %collective-permute-start.26 = (f32[4,512,256]{2,1,0:T(8,128)}, f32[4,512,256]{2,1,0:T(8,128)}, u32[]{:S(2)}, u32[]{:S(2)}) collective-permute-start(f32[4,512,256]{2,1,0:T(8,128)} %get-tuple-element.223), channel_id=1, source_target_pairs={{0,1},{1,0},{2,3},{3,2},{4,5},{5,4},{6,7},{7,6},{8,9},{9,8},{10,11... | collective-permute-start | bytes 6291464 | tf_op jit(solution)/shard_map/ppermute | solution.py:485
  413.0 1.1 copy-start.8
  414.1 0.8 copy-start.9
  420.2 6.0 %copy-start.22 = (f32[8,128]{1,0:T(8,128)S(1)}, f32[8,128]{1,0:T(8,128)}, u32[]{:S(2)}) copy-start(f32[8,128]{1,0:T(8,128)} %get-tuple-element.231) | copy-start | bytes 12292
  420.2 6.0 %copy-start.23 = (f32[8,128]{1,0:T(8,128)S(1)}, f32[8,128]{1,0:T(8,128)}, u32[]{:S(2)}) copy-start(f32[8,128]{1,0:T(8,128)} %get-tuple-element.219) | copy-start | bytes 12292
  420.2 6.0 %copy-start.24 = (f32[8,128]{1,0:T(8,128)S(1)}, f32[8,128]{1,0:T(8,128)}, u32[]{:S(2)}) copy-start(f32[8,128]{1,0:T(8,128)} %get-tuple-element.232) | copy-start | bytes 12292

commit v6 on v5

--- a/solution.py
+++ b/solution.py
@@ -386,8 +386,8 @@
     )[0]
 
 
-def update_call(chain, stats, observed, noise, solution, residual, direction, outers):
-    probes, s_loc, t_loc = direction.shape
+def update_call(chain, stats, observed, noise, solution, residual, direction, outers, first, earlier):
+    _, s_loc, t_loc = direction.shape
     rows = s_loc // CHUNKS
 
     def body(place, given, seen, var, sol_ref, res_ref, way_ref, *refs):
@@ -422,12 +422,14 @@
             one = pl.BlockSpec((rows, outer.width), lambda i, place: (row(i), 0))
         return [one] * len(outer.operands)
 
-    probe_rows = pl.BlockSpec((1, rows, t_loc), lambda i, place: (i // CHUNKS, i % CHUNKS, 0))
+    probe_rows = pl.BlockSpec((1, rows, t_loc), lambda i, place: (i // CHUNKS * 2 + first, i % CHUNKS, 0))
+    operands = [stats, observed, noise, solution, residual, direction]
+    operands += [ref for outer in outers for ref in outer.operands]
     return chain(
         body,
         "update",
-        (probes * CHUNKS,),
-        [stats, observed, noise, solution, residual, direction] + [ref for outer in outers for ref in outer.operands],
+        (len(outers) * CHUNKS,),
+        operands + list(earlier),
         [
             pl.BlockSpec(stats.shape, lambda i, place: (0, 0, 0)),
             pl.BlockSpec((rows, t_loc), lambda i, place: (i % CHUNKS, 0)),
@@ -436,9 +438,11 @@
             probe_rows,
             probe_rows,
         ]
-        + [spec for p, outer in enumerate(outers) for spec in outer_specs(p, outer)],
+        + [spec for p, outer in enumerate(outers) for spec in outer_specs(p, outer)]
+        + [pl.BlockSpec(memory_space=HBM)] * len(earlier),
         [(direction.shape, F32)] * 3,
         [probe_rows] * 3,
+        aliases=[(len(operands) + k, k) for k in range(len(earlier))],
     )
 
 
@@ -559,21 +563,21 @@
     out3 = over_z(inner3)
     y2 = over_y(cells2)
     smooth0 = space([cells0] + y0, False)
-    smooth0, cells3 = pass_on(smooth0, pieces=out3)
+    smooth1 = space(y1, False)
+    smooth0, smooth1, cells3 = pass_on(smooth0, smooth1, pieces=out3)
 
     home0 = over_z(smooth0)
     y3 = over_y(cells3)
-    smooth1 = space(y1, False)
-    smooth1, home0 = pass_on(smooth1, pieces=home0)
+    smooth2 = space(y2, False)
+    smooth1, smooth2, home0 = pass_on(smooth1, smooth2, pieces=home0)
 
     home1 = over_z(smooth1)
     x0 = over_x(home0)
-    smooth2 = space(y2, False)
-    smooth2, home1 = pass_on(smooth2, pieces=home1)
+    smooth3 = space(y3, False)
+    smooth2, smooth3, home1 = pass_on(smooth2, smooth3, pieces=home1)
 
     home2 = over_z(smooth2)
     x1 = over_x(home1)
-    smooth3 = space(y3, False)
     terms0 = time_call(chain, x0, time, n_c)
     home2, x1, terms0, smooth3 = pass_on(home2, x1[1:], terms0, smooth3)
 
@@ -587,9 +591,14 @@
     outer3 = Outer(home3)
     sums3 = sums(outer3, 3, 200 << 20)
     sums1 = sums(outer1, 1)
-    stats = over_all(sums0, sums1, sums2, sums3)
-    outers = (outer0, outer1, outer2, outer3)
-    return tuple(update_call(chain, stats, observed, noise, solution, residual, direction, outers))
+    def update(stats, outers, first, earlier):
+        given = (observed, noise, solution, residual, direction)
+        return update_call(chain, stats, *given, outers, first, earlier)
+
+    stats02 = over_all(sums0, sums2)
+    stats13 = over_all(sums1, sums3)
+    new = update(stats02, (outer0, outer2), 0, ())
+    return tuple(update(stats13, (outer1, outer3), 1, new))
 
 
 def solution(mesh):

time: 483 us -> 476 us (0.986)
  blocking collectives: 28.6 us -> 0 us
  starting transfers between devices: 81.1 us -> 90.4 us
  waiting for transfers between devices: 44.8 us -> 50.5 us
    all_to_all x1 -> x0, blocking collectives: 28.6 us -> none  [over_all(): return lax.all_to_all(many, ('sta', 'day'), 0, 0, tiled=True)]
    all_to_all x0 -> x2, starting transfers between devices: none -> 14.1 us  [over_all(): return lax.all_to_all(many, ('sta', 'day'), 0, 0, tiled=True)]
    ppermute x18, waiting for transfers between devices: 31.5 us -> 22.1 us  [over_z(): found.append(lax.ppermute(pieces[k], 'sta', pairs))]
    ppermute x4, waiting for transfers between devices: 0.01 us -> 8.81 us  [over_y(): found.append(lax.ppermute(cells, 'sta', pairs))]
    ppermute x4, waiting for transfers between devices: 3.8 us -> 10.2 us  [over_x(): found.append(lax.ppermute(cells, 'day', pairs))]
    pallas_call x30 -> x31, Pallas kernels: 315 us -> 317 us  [__call__(): pl.pallas_call(kernel, grid_spec=pltpu.PrefetchScalarGridSpec(num_scalar_...]
    unnamed x52 -> x54, local copies, waits for them, and re-layouts: 9.23 us -> 11.1 us
  transfers between devices with their start and end apart: 32 -> 34, of which waited for: 9 -> 11; matrix products, arithmetic and copies ran while one was open for 0% -> 1% of each run, Pallas kernels for 57% -> 62%
where the time goes in v6:
time: 476 us; the launch traced here: 475 us
  Pallas kernels  317 us (67%)
  starting transfers between devices  90.4 us (19%)
  waiting for transfers between devices  50.5 us (11%)
  local copies, waits for them, and re-layouts  13.4 us (3%)
    pallas_call x31, Pallas kernels, __call__(): pl.pallas_call(kernel, grid_spec=pltpu.PrefetchScalarGridSpec(num_scalar_...  317 us
    ppermute x18, starting transfers between devices, over_z(): found.append(lax.ppermute(pieces[k], 'sta', pairs))  51 us
    ppermute x18, waiting for transfers between devices, over_z(): found.append(lax.ppermute(pieces[k], 'sta', pairs))  22.1 us
    all_to_all x2, starting transfers between devices, over_all(): return lax.all_to_all(many, ('sta', 'day'), 0, 0, tiled=True)  14.1 us
    all_to_all x2, starting transfers between devices, over_z_at_once(): lax.all_to_all(pieces, 'sta', 0, 0, axis_index_groups=groups, tiled=True)  13.8 us
    unnamed x54, local copies, waits for them, and re-layouts  11.1 us
    ppermute x4, waiting for transfers between devices, over_x(): found.append(lax.ppermute(cells, 'day', pairs))  10.2 us
  transfers between devices with their start and end apart: 34, of which 11 were waited for; matrix products, arithmetic and copies ran while one was open for 1% of the time, Pallas kernels for 62%

profile of v6, /device:TPU:0, one launch (start us, length us, event | category | flops | bytes accessed | tf_op | source)
XLA Modules:
  0.0 474.8 jit_solution(1835951525665269313)
XLA Ops:
  1.3 4.0 mask.4
  5.2 2.9 collective-permute-start
  8.2 4.0 mask.5
  12.2 1.6 collective-permute-start.1
  13.7 2.6 collective-permute-start.2
  16.3 1.3 collective-permute-start.3
  17.7 4.0 mask.6
  21.6 3.9 mask.7
  25.6 22.3 %time_entries.1 = (bf16[2048,2048]{1,0:T(8,128)(2,1)}, bf16[2048,2048]{1,0:T(8,128)(2,1)}, f32[8,128]{1,0:T(8,128)}) custom-call(s32[4]{0:T(128)} %pad_add_fusion.place, f32[4,4096]{1,0:T(4,128)} %refs_1_.13, f32[4,4096]{1,0:T(4,128)} %refs_1_.13, f32[8,128]{1,0:T(8,128)} %get-tuple-element.146.refs_2_), custom_call_target="tpu_custom_call" | custom-call | tf_op jit(solution)/shard_map/time_entries/pallas_call | solution.py:40
  47.9 2.3 collective-permute-done.2.refs_5_
  50.2 3.8 collective-permute-done.refs_2_
  54.0 1.3 copy-done.3
  55.3 3.1 gate.8
  58.4 1.8 collective-permute-start.4
  60.2 1.5 collective-permute-start.5
  61.7 9.4 %all-to-all-start = ((f32[4,512,256]{2,1,0:T(8,128)}), f32[4,512,256]{2,1,0:T(8,128)S(1)}, u32[]{:S(2)}, u32[]{:S(2)}) async-start(f32[4,512,256]{2,1,0:T(8,128)} %get-tuple-element.160), calls=%async_computation | async-start | bytes 4194304 | tf_op jit(solution)/shard_map/all_to_all | solution.py:471
  71.1 20.4 %time.4 = (f32[4,512,256]{2,1,0:T(8,128)}, f32[4,512,256]{2,1,0:T(8,128)}, f32[8,128]{1,0:T(8,128)}) custom-call(s32[4]{0:T(128)} %pad_add_fusion.place, f32[4,512,256]{2,1,0:T(8,128)} %get-tuple-element.141.refs_0_, f32[4,512,256]{2,1,0:T(8,128)} %get-tuple-element.150.refs_1_, bf16[2048,2048]{1,0:T(8,128)(2,1)} %get-tuple-element.151.refs_2_, ...), custom_call_target="tpu_custom_call" | custom-call | tf_op jit(solution)/shard_map/time/pallas_call | solution.py:40
  91.6 17.4 %space_entries.2 = (bf16[2048,2048]{1,0:T(8,128)(2,1)}, bf16[2048,2048]{1,0:T(8,128)(2,1)}, f32[8,128]{1,0:T(8,128)}) custom-call(s32[4]{0:T(128)} %pad_add_fusion.place, f32[2,4096]{1,0:T(2,128)} %refs_3_.9, f32[2,4096]{1,0:T(2,128)} %refs_3_.9, f32[2,4096]{1,0:T(2,128)} %refs_3_.9, f32[2,4096]{1,0:T(2,128)} %refs_3_.9, f32[8,128]{1,0:T(8,128)} %get-tuple-element.154.refs_4_), custom_call_target="tpu_custom_call" | custom-call | tf_op jit(solution)/shard_map/space_entries/pallas_call | solution.py:40
  109.7 4.0 add.19
  113.6 4.1 all-to-all-done.refs_0_
  117.7 1.3 copy-done
  119.7 4.5 all-to-all-start.1
  124.1 20.5 %time.5 = (f32[4,512,256]{2,1,0:T(8,128)}, f32[4,512,256]{2,1,0:T(8,128)}, f32[8,128]{1,0:T(8,128)}) custom-call(s32[4]{0:T(128)} %pad_add_fusion.place, f32[4,512,256]{2,1,0:T(8,128)} %get-tuple-element.149.refs_0_, f32[4,512,256]{2,1,0:T(8,128)} %get-tuple-element.159.refs_1_, bf16[2048,2048]{1,0:T(8,128)(2,1)} %get-tuple-element.151.refs_2_, ...), custom_call_target="tpu_custom_call" | custom-call | tf_op jit(solution)/shard_map/time/pallas_call | solution.py:40
  145.3 17.4 %space_entries.3 = (bf16[2048,2048]{1,0:T(8,128)(2,1)}, bf16[2048,2048]{1,0:T(8,128)(2,1)}, f32[8,128]{1,0:T(8,128)}) custom-call(s32[4]{0:T(128)} %pad_add_fusion.place, f32[2,4096]{1,0:T(2,128)} %refs_3_.9, f32[2,4096]{1,0:T(2,128)} %refs_3_.9, f32[2,4096]{1,0:T(2,128)} %refs_3_.9, f32[2,4096]{1,0:T(2,128)} %refs_3_.9, f32[8,128]{1,0:T(8,128)} %get-tuple-element.167.refs_4_), custom_call_target="tpu_custom_call" | custom-call | tf_op jit(solution)/shard_map/space_entries/pallas_call | solution.py:40
  162.6 3.9 add.20
  166.6 5.3 %all-to-all-done.1.refs_0_ = f32[4,512,256]{2,1,0:T(8,128)} async-done(((f32[4,512,256]{2,1,0:T(8,128)}), f32[4,512,256]{2,1,0:T(8,128)}, u32[]{:S(2)}, u32[]{:S(2)}) %all-to-all-start.1) | async-done | bytes 2097184 | tf_op jit(solution)/shard_map/all_to_all | solution.py:471
  173.2 2.2 collective-permute-start.11
  175.9 22.0 %space.4 = (f32[512,256]{1,0:T(8,128)}, f32[512,256]{1,0:T(8,128)}, f32[512,256]{1,0:T(8,128)}, f32[512,256]{1,0:T(8,128)}, f32[8,128]{1,0:T(8,128)}) custom-call(s32[4]{0:T(128)} %pad_add_fusion.place, f32[4,512,256]{2,1,0:T(8,128)} %get-tuple-element.148.refs_0_, f32[4,512,256]{2,1,0:T(8,128)} %get-tuple-element.156.refs_1_, ...), custom_call_target="tpu_custom_call" | custom-call | tf_op jit(solution)/shard_map/space/pallas_call | solution.py:40
  198.0 22.0 %space.5 = (f32[512,256]{1,0:T(8,128)}, f32[512,256]{1,0:T(8,128)}, f32[512,256]{1,0:T(8,128)}, f32[512,256]{1,0:T(8,128)}, f32[8,128]{1,0:T(8,128)}) custom-call(s32[4]{0:T(128)} %pad_add_fusion.place, f32[4,512,256]{2,1,0:T(8,128)} %get-tuple-element.184.refs_0_, f32[4,512,256]{2,1,0:T(8,128)} %collective-permute-done.8.refs_1_, ...), custom_call_target="tpu_custom_call" | custom-call | tf_op jit(solution)/shard_map/space/pallas_call | solution.py:40
  221.1 3.1 gate.12
  225.1 2.0 collective-permute-start.13
  227.1 1.9 collective-permute-start.14
  229.0 2.0 collective-permute-start.15
  230.9 7.3 %collective-permute-done.12.refs_1_ = f32[4,512,256]{2,1,0:T(8,128)} collective-permute-done((f32[4,512,256]{2,1,0:T(8,128)}, f32[4,512,256]{2,1,0:T(8,128)}, u32[]{:S(2)}, u32[]{:S(2)}) %collective-permute-start.12) | collective-permute-done | bytes 2097184 | tf_op jit(solution)/shard_map/ppermute | solution.py:477
  238.2 22.0 %space.6 = (f32[512,256]{1,0:T(8,128)}, f32[512,256]{1,0:T(8,128)}, f32[512,256]{1,0:T(8,128)}, f32[512,256]{1,0:T(8,128)}, f32[8,128]{1,0:T(8,128)}) custom-call(s32[4]{0:T(128)} %pad_add_fusion.place, f32[4,512,256]{2,1,0:T(8,128)} %get-tuple-element.199.refs_0_, f32[4,512,256]{2,1,0:T(8,128)} %collective-permute-done.12.refs_1_, ...), custom_call_target="tpu_custom_call" | custom-call | tf_op jit(solution)/shard_map/space/pallas_call | solution.py:40
  262.5 3.2 gate.13
  265.6 11.6 %collective-permute-start.17 = (f32[512,256]{1,0:T(8,128)}, f32[512,256]{1,0:T(8,128)S(1)}, u32[]{:S(2)}, u32[]{:S(2)}) collective-permute-start(f32[512,256]{1,0:T(8,128)} %get-tuple-element.221), channel_id=1, source_target_pairs={{0,8},{4,12},{8,16},{12,20},{16,24},{20,28},{24,0},{28,4},{1,9},{5... | collective-permute-start | bytes 1572872 | tf_op jit(solution)/shard_map/ppermute | solution.py:466
  277.2 1.9 collective-permute-start.18
  279.6 1.5 collective-permute-start.24
  281.1 1.5 collective-permute-done.16.refs_1_
  282.6 1.3 copy-done.8
  283.9 22.0 %space.7 = (f32[512,256]{1,0:T(8,128)}, f32[512,256]{1,0:T(8,128)}, f32[512,256]{1,0:T(8,128)}, f32[512,256]{1,0:T(8,128)}, f32[8,128]{1,0:T(8,128)}) custom-call(s32[4]{0:T(128)} %pad_add_fusion.place, f32[4,512,256]{2,1,0:T(8,128)} %get-tuple-element.214.refs_0_, f32[4,512,256]{2,1,0:T(8,128)} %copy-done.8, bf16[2048,2048]{1,0:T(8,128)(2,1)} %get-tuple-element.157.refs_2_, ...), custom_call_target="tpu_custom_call" | custom-call | tf_op jit(solution)/shard_map/space/pallas_call | solution.py:40
  305.9 4.2 collective-permute-done.18.refs_10_
  310.1 1.3 collective-permute-done.19.refs_11_
  312.2 3.1 gate.14
  315.3 1.6 collective-permute-start.23
  316.8 11.7 %collective-permute-start.20 = (f32[512,256]{1,0:T(8,128)}, f32[512,256]{1,0:T(8,128)S(1)}, u32[]{:S(2)}, u32[]{:S(2)}) collective-permute-start(f32[512,256]{1,0:T(8,128)} %get-tuple-element.227), channel_id=1, source_target_pairs={{0,8},{4,12},{8,16},{12,20},{16,24},{20,28},{24,0},{28,4},{1,9},{5... | collective-permute-start | bytes 1572872 | tf_op jit(solution)/shard_map/ppermute | solution.py:466
  328.5 3.3 collective-permute-start.21
  331.8 20.5 %time.6 = (f32[4,512,256]{2,1,0:T(8,128)}, f32[4,512,256]{2,1,0:T(8,128)}, f32[8,128]{1,0:T(8,128)}) custom-call(s32[4]{0:T(128)} %pad_add_fusion.place, f32[4,512,256]{2,1,0:T(8,128)} %get-tuple-element.230.refs_0_, f32[4,512,256]{2,1,0:T(8,128)} %collective-permute-done.24.refs_1_, bf16[2048,2048]{1,0:T(8,128)(2,1)} %get-tuple-element.151.refs_2_, ...), custom_call_target="tpu_custom_call" | custom-call | tf_op jit(solution)/shard_map/time/pallas_call | solution.py:40
  352.3 13.0 %collective-permute-done.21.refs_2_ = f32[512,256]{1,0:T(8,128)S(1)} collective-permute-done((f32[512,256]{1,0:T(8,128)}, f32[512,256]{1,0:T(8,128)S(1)}, u32[]{:S(2)}, u32[]{:S(2)}) %collective-permute-start.21) | collective-permute-done | bytes 524320 | tf_op jit(solution)/shard_map/ppermute | solution.py:466
  365.3 6.4 %collective-permute-done.23.refs_4_ = f32[4,512,256]{2,1,0:T(8,128)S(1)} collective-permute-done((f32[4,512,256]{2,1,0:T(8,128)}, f32[4,512,256]{2,1,0:T(8,128)S(1)}, u32[]{:S(2)}, u32[]{:S(2)}) %collective-permute-start.23) | collective-permute-done | bytes 2097184 | tf_op jit(solution)/shard_map/ppermute | solution.py:484
  371.8 1.4 copy-done.2
  374.1 5.5 %collective-permute-start.27 = (f32[512,256]{1,0:T(8,128)}, f32[512,256]{1,0:T(8,128)S(1)}, u32[]{:S(2)}, u32[]{:S(2)}) collective-permute-start(f32[512,256]{1,0:T(8,128)} %get-tuple-element.252), channel_id=1, source_target_pairs={{0,8},{4,12},{8,16},{12,20},{16,24},{20,28},{24,0},{28,4},{1,9},{5... | collective-permute-start | bytes 1572872 | tf_op jit(solution)/shard_map/ppermute | solution.py:466
  379.8 2.1 collective-permute-start.29
  382.9 5.3 %sums.4 = (f32[8,128]{1,0:T(8,128)}, f32[8,128]{1,0:T(8,128)}) custom-call(s32[4]{0:T(128)} %pad_add_fusion.place, s32[512,1024]{1,0:T(8,128)} %refs_1_.17, f32[512,1]{1,0:T(8,128)} %copy.63.refs_1_.refs_2_, f32[4,512,1024]{2,1,0:T(8,128)} %refs_4_.3, f32[4,512,1024]{2,1,0:T(8,128)} %refs_5_.3, f32[512,256]{1,0:T(8,128)} %get-tuple-element.242.refs_4_.refs_8_, ...), custom_call_target="tpu_custom_call" | custom-call | tf_op jit(solution)/shard_map/sums/pallas_call | solution.py:40
  388.2 1.3 copy-done.4
  389.5 6.1 %sums.5 = (f32[8,128]{1,0:T(8,128)}, f32[8,128]{1,0:T(8,128)}) custom-call(s32[4]{0:T(128)} %pad_add_fusion.place, s32[512,1024]{1,0:T(8,128)} %refs_1_.17, f32[512,1]{1,0:T(8,128)} %copy.63.refs_1_.refs_2_, f32[4,512,1024]{2,1,0:T(8,128)} %refs_4_.3, f32[4,512,1024]{2,1,0:T(8,128)} %refs_5_.3, f32[4,512,256]{2,1,0:T(8,128)} %get-tuple-element.240.refs_4_.refs_6_, ...), custom_call_target="tpu_custom_call" | custom-call | tf_op jit(solution)/shard_map/sums/pallas_call | solution.py:40
  397.0 3.6 all-to-all-start.3
  400.6 20.5 %time.7 = (f32[4,512,256]{2,1,0:T(8,128)}, f32[4,512,256]{2,1,0:T(8,128)}, f32[8,128]{1,0:T(8,128)}) custom-call(s32[4]{0:T(128)} %pad_add_fusion.place, f32[4,512,256]{2,1,0:T(8,128)} %get-tuple-element.225.refs_0_, f32[4,512,256]{2,1,0:T(8,128)} %get-tuple-element.239.refs_1_, bf16[2048,2048]{1,0:T(8,128)(2,1)} %get-tuple-element.151.refs_2_, ...), custom_call_target="tpu_custom_call" | custom-call | tf_op jit(solution)/shard_map/time/pallas_call | solution.py:40
  422.0 5.3 %sums.6 = (f32[8,128]{1,0:T(8,128)}, f32[8,128]{1,0:T(8,128)}) custom-call(s32[4]{0:T(128)} %pad_add_fusion.place, s32[512,1024]{1,0:T(8,128)} %refs_1_.17, f32[512,1]{1,0:T(8,128)} %copy.63.refs_1_.refs_2_, f32[4,512,1024]{2,1,0:T(8,128)} %refs_4_.3, f32[4,512,1024]{2,1,0:T(8,128)} %refs_5_.3, f32[512,256]{1,0:T(8,128)} %get-tuple-element.251.refs_4_.refs_8_, ...), custom_call_target="tpu_custom_call" | custom-call | flops 241172480000 | bytes 209715200 | tf_op jit(solution)/shard_map/sums/pallas_call | solution.py:40
  427.4 6.0 %sums.7 = (f32[8,128]{1,0:T(8,128)}, f32[8,128]{1,0:T(8,128)}) custom-call(s32[4]{0:T(128)} %pad_add_fusion.place, s32[512,1024]{1,0:T(8,128)} %refs_1_.17, f32[512,1]{1,0:T(8,128)} %copy.63.refs_1_.refs_2_, f32[4,512,1024]{2,1,0:T(8,128)} %refs_4_.3, f32[4,512,1024]{2,1,0:T(8,128)} %refs_5_.3, f32[4,512,256]{2,1,0:T(8,128)} %get-tuple-element.249.refs_4_.refs_6_, ...), custom_call_target="tpu_custom_call" | custom-call | tf_op jit(solution)/shard_map/sums/pallas_call | solution.py:40
  434.7 10.5 %all-to-all-start.2 = ((f32[32,16,128]{2,1,0:T(8,128)}), f32[32,16,128]{2,1,0:T(8,128)S(1)}, u32[]{:S(2)}, u32[]{:S(2)}) async-start(f32[32,16,128]{2,1,0:T(8,128)} %broadcast_in_dim.7), calls=%async_computation.2 | async-start | bytes 524288 | tf_op jit(solution)/shard_map/all_to_all | solution.py:494
  445.3 14.3 %update.2 = (f32[4,512,1024]{2,1,0:T(8,128)}, f32[4,512,1024]{2,1,0:T(8,128)}, f32[4,512,1024]{2,1,0:T(8,128)}, f32[8,128]{1,0:T(8,128)}) custom-call(s32[4]{0:T(128)} %pad_add_fusion.place, f32[32,16,128]{2,1,0:T(8,128)} %all-to-all-done.3.refs_0_, s32[512,1024]{1,0:T(8,128)} %refs_1_.17, f32[512,1]{1,0:T(8,128)} %copy.63.refs_1_.refs_2_, ...), custom_call_target="tpu_custom_call" | custom-call | tf_op jit(solution)/shard_map/update/pallas_call | solution.py:40
  460.3 14.3 %update.3 = (f32[4,512,1024]{2,1,0:T(8,128)}, f32[4,512,1024]{2,1,0:T(8,128)}, f32[4,512,1024]{2,1,0:T(8,128)}, f32[8,128]{1,0:T(8,128)}) custom-call(s32[4]{0:T(128)} %pad_add_fusion.place, f32[32,16,128]{2,1,0:T(8,128)} %copy-done.9, s32[512,1024]{1,0:T(8,128)} %refs_1_.17, ...), custom_call_target="tpu_custom_call", output_to_operand_aliasing={{0}: (13, {}), {1}: (14, {}), {2}: (15, {})} | custom-call | tf_op jit(solution)/shard_map/update/pallas_call | solution.py:40
  (95 shorter events, 16.4 us)
Async XLA Ops:
  5.2 48.8 %collective-permute-start = (f32[4,512,256]{2,1,0:T(8,128)}, f32[4,512,256]{2,1,0:T(8,128)S(1)}, u32[]{:S(2)}, u32[]{:S(2)}) collective-permute-start(f32[4,512,256]{2,1,0:T(8,128)} %get-tuple-element.141.refs_0_), channel_id=1, source_target_pairs={{0,2},{1,3},{2,0},{3,1},{4,6},{5,7},{6,4},{7,5},{8,10},{9,11},{10,... | collective-permute-start | bytes 6291464 | tf_op jit(solution)/shard_map/ppermute | solution.py:484
  12.2 35.7 %collective-permute-start.1 = (f32[512,256]{1,0:T(8,128)}, f32[512,256]{1,0:T(8,128)S(1)}, u32[]{:S(2)}, u32[]{:S(2)}) collective-permute-start(f32[512,256]{1,0:T(8,128)} %get-tuple-element.143), channel_id=1, source_target_pairs={{0,8},{4,12},{8,16},{12,20},{16,24},{20,28},{24,0},{28,4},{1,9},{5... | collective-permute-start | bytes 1572872 | tf_op jit(solution)/shard_map/ppermute | solution.py:466
  13.7 36.5 %collective-permute-start.2 = (f32[512,256]{1,0:T(8,128)}, f32[512,256]{1,0:T(8,128)S(1)}, u32[]{:S(2)}, u32[]{:S(2)}) collective-permute-start(f32[512,256]{1,0:T(8,128)} %get-tuple-element.144), channel_id=1, source_target_pairs={{0,16},{4,20},{8,24},{12,28},{16,0},{20,4},{24,8},{28,12},{1,17},{... | collective-permute-start | bytes 1572872 | tf_op jit(solution)/shard_map/ppermute | solution.py:466
  16.3 33.9 %collective-permute-start.3 = (f32[512,256]{1,0:T(8,128)}, f32[512,256]{1,0:T(8,128)S(1)}, u32[]{:S(2)}, u32[]{:S(2)}) collective-permute-start(f32[512,256]{1,0:T(8,128)} %get-tuple-element.145), channel_id=1, source_target_pairs={{0,24},{4,28},{8,0},{12,4},{16,8},{20,12},{24,16},{28,20},{1,25},{... | collective-permute-start | bytes 1572872 | tf_op jit(solution)/shard_map/ppermute | solution.py:466
  47.9 6.1 %copy-start.21 = (f32[512,256]{1,0:T(8,128)}, f32[512,256]{1,0:T(8,128)S(1)}, u32[]{:S(2)}) copy-start(f32[512,256]{1,0:T(8,128)S(1)} %collective-permute-done.1.refs_4_) | copy-start | bytes 1572868
  50.2 3.8 copy-start.22
  50.2 3.8 copy-start.23
  54.0 1.3 copy-start.3
  58.4 50.6 %collective-permute-start.4 = (f32[4,512,256]{2,1,0:T(8,128)}, f32[4,512,256]{2,1,0:T(8,128)}, u32[]{:S(2)}, u32[]{:S(2)}) collective-permute-start(f32[4,512,256]{2,1,0:T(8,128)} %get-tuple-element.149.refs_0_), channel_id=1, source_target_pairs={{0,2},{1,3},{2,0},{3,1},{4,6},{5,7},{6,4},{7,5},{8,10},{9,11},{10,... | collective-permute-start | bytes 6291464 | tf_op jit(solution)/shard_map/ppermute | solution.py:484
  60.2 48.8 %collective-permute-start.5 = (f32[4,512,256]{2,1,0:T(8,128)}, f32[4,512,256]{2,1,0:T(8,128)}, u32[]{:S(2)}, u32[]{:S(2)}) collective-permute-start(f32[4,512,256]{2,1,0:T(8,128)} %get-tuple-element.148.refs_0_), channel_id=1, source_target_pairs={{0,4},{4,0},{8,12},{12,8},{16,20},{20,16},{24,28},{28,24},{1,5},{5... | collective-permute-start | bytes 6291464 | tf_op jit(solution)/shard_map/ppermute | solution.py:477
  61.7 56.0 %all-to-all-start = ((f32[4,512,256]{2,1,0:T(8,128)}), f32[4,512,256]{2,1,0:T(8,128)S(1)}, u32[]{:S(2)}, u32[]{:S(2)}) async-start(f32[4,512,256]{2,1,0:T(8,128)} %get-tuple-element.160), calls=%async_computation | async-start | bytes 4194304 | tf_op jit(solution)/shard_map/all_to_all | solution.py:471
  91.5 18.1 %collective-permute-start.6 = (f32[4,512,256]{2,1,0:T(8,128)}, f32[4,512,256]{2,1,0:T(8,128)}, u32[]{:S(2)}, u32[]{:S(2)}) collective-permute-start(f32[4,512,256]{2,1,0:T(8,128)} %get-tuple-element.162), channel_id=1, source_target_pairs={{0,1},{1,0},{2,3},{3,2},{4,5},{5,4},{6,7},{7,6},{8,9},{9,8},{10,11... | collective-permute-start | bytes 6291464 | tf_op jit(solution)/shard_map/ppermute | solution.py:489
  117.7 1.3 copy-start
  119.7 52.2 %all-to-all-start.1 = ((f32[4,512,256]{2,1,0:T(8,128)}), f32[4,512,256]{2,1,0:T(8,128)}, u32[]{:S(2)}, u32[]{:S(2)}) async-start(f32[4,512,256]{2,1,0:T(8,128)} %get-tuple-element.170), calls=%async_computation.1 | async-start | bytes 4194304 | tf_op jit(solution)/shard_map/all_to_all | solution.py:471
  124.1 20.5 %copy-start.1 = (f32[4,512,256]{2,1,0:T(8,128)S(1)}, f32[4,512,256]{2,1,0:T(8,128)}, u32[]{:S(2)}) copy-start(f32[4,512,256]{2,1,0:T(8,128)} %get-tuple-element.184.refs_0_) | copy-start | bytes 6291460
  144.7 17.9 %collective-permute-start.7 = (f32[4,512,256]{2,1,0:T(8,128)}, f32[4,512,256]{2,1,0:T(8,128)}, u32[]{:S(2)}, u32[]{:S(2)}) collective-permute-start(f32[4,512,256]{2,1,0:T(8,128)} %get-tuple-element.172), channel_id=1, source_target_pairs={{0,1},{1,0},{2,3},{3,2},{4,5},{5,4},{6,7},{7,6},{8,9},{9,8},{10,11... | collective-permute-start | bytes 6291464 | tf_op jit(solution)/shard_map/ppermute | solution.py:489
  144.7 53.3 %collective-permute-start.8 = (f32[4,512,256]{2,1,0:T(8,128)S(1)}, f32[4,512,256]{2,1,0:T(8,128)}, u32[]{:S(2)}, u32[]{:S(2)}) collective-permute-start(f32[4,512,256]{2,1,0:T(8,128)S(1)} %copy-done.1), channel_id=1, source_target_pairs={{0,4},{4,0},{8,12},{12,8},{16,20},{20,16},{24,28},{28,24},{1,5},{5... | collective-permute-start | bytes 6291464 | tf_op jit(solution)/shard_map/ppermute | solution.py:477
  172.6 47.4 %collective-permute-start.10 = (f32[512,256]{1,0:T(8,128)}, f32[512,256]{1,0:T(8,128)S(1)}, u32[]{:S(2)}, u32[]{:S(2)}) collective-permute-start(f32[512,256]{1,0:T(8,128)} %get-tuple-element.192), channel_id=1, source_target_pairs={{0,16},{4,20},{8,24},{12,28},{16,0},{20,4},{24,8},{28,12},{1,17},{... | collective-permute-start | bytes 1572872 | tf_op jit(solution)/shard_map/ppermute | solution.py:466
  172.6 65.6 %collective-permute-start.12 = (f32[4,512,256]{2,1,0:T(8,128)}, f32[4,512,256]{2,1,0:T(8,128)}, u32[]{:S(2)}, u32[]{:S(2)}) collective-permute-start(f32[4,512,256]{2,1,0:T(8,128)} %get-tuple-element.199.refs_0_), channel_id=1, source_target_pairs={{0,4},{4,0},{8,12},{12,8},{16,20},{20,16},{24,28},{28,24},{1,5},{5... | collective-permute-start | bytes 6291464 | tf_op jit(solution)/shard_map/ppermute | solution.py:477
  173.2 46.8 %collective-permute-start.11 = (f32[512,256]{1,0:T(8,128)}, f32[512,256]{1,0:T(8,128)S(1)}, u32[]{:S(2)}, u32[]{:S(2)}) collective-permute-start(f32[512,256]{1,0:T(8,128)} %get-tuple-element.193), channel_id=1, source_target_pairs={{0,24},{4,28},{8,0},{12,4},{16,8},{20,12},{24,16},{28,20},{1,25},{... | collective-permute-start | bytes 1572872 | tf_op jit(solution)/shard_map/ppermute | solution.py:466
  175.4 44.6 %collective-permute-start.9 = (f32[512,256]{1,0:T(8,128)}, f32[512,256]{1,0:T(8,128)S(1)}, u32[]{:S(2)}, u32[]{:S(2)}) collective-permute-start(f32[512,256]{1,0:T(8,128)} %get-tuple-element.191), channel_id=1, source_target_pairs={{0,8},{4,12},{8,16},{12,20},{16,24},{20,28},{24,0},{28,4},{1,9},{5... | collective-permute-start | bytes 1572872 | tf_op jit(solution)/shard_map/ppermute | solution.py:466
  220.0 0.8 copy-start.12
  220.0 1.0 copy-start.14
  220.0 1.1 copy-start.16
  224.2 58.4 %collective-permute-start.16 = (f32[4,512,256]{2,1,0:T(8,128)}, f32[4,512,256]{2,1,0:T(8,128)S(1)}, u32[]{:S(2)}, u32[]{:S(2)}) collective-permute-start(f32[4,512,256]{2,1,0:T(8,128)} %get-tuple-element.214.refs_0_), channel_id=1, source_target_pairs={{0,4},{4,0},{8,12},{12,8},{16,20},{20,16},{24,28},{28,24},{1,5},{5... | collective-permute-start | bytes 6291464 | tf_op jit(solution)/shard_map/ppermute | solution.py:477
  225.1 35.1 %collective-permute-start.13 = (f32[512,256]{1,0:T(8,128)}, f32[512,256]{1,0:T(8,128)S(1)}, u32[]{:S(2)}, u32[]{:S(2)}) collective-permute-start(f32[512,256]{1,0:T(8,128)} %get-tuple-element.206), channel_id=1, source_target_pairs={{0,8},{4,12},{8,16},{12,20},{16,24},{20,28},{24,0},{28,4},{1,9},{5... | collective-permute-start | bytes 1572872 | tf_op jit(solution)/shard_map/ppermute | solution.py:466
  227.1 34.4 %collective-permute-start.14 = (f32[512,256]{1,0:T(8,128)}, f32[512,256]{1,0:T(8,128)S(1)}, u32[]{:S(2)}, u32[]{:S(2)}) collective-permute-start(f32[512,256]{1,0:T(8,128)} %get-tuple-element.207), channel_id=1, source_target_pairs={{0,16},{4,20},{8,24},{12,28},{16,0},{20,4},{24,8},{28,12},{1,17},{... | collective-permute-start | bytes 1572872 | tf_op jit(solution)/shard_map/ppermute | solution.py:466
  229.0 32.5 %collective-permute-start.15 = (f32[512,256]{1,0:T(8,128)}, f32[512,256]{1,0:T(8,128)S(1)}, u32[]{:S(2)}, u32[]{:S(2)}) collective-permute-start(f32[512,256]{1,0:T(8,128)} %get-tuple-element.208), channel_id=1, source_target_pairs={{0,24},{4,28},{8,0},{12,4},{16,8},{20,12},{24,16},{28,20},{1,25},{... | collective-permute-start | bytes 1572872 | tf_op jit(solution)/shard_map/ppermute | solution.py:466
  260.2 1.2 copy-start.18
  261.5 0.8 copy-start.19
  261.5 1.0 copy-start.20
  265.6 40.3 %collective-permute-start.17 = (f32[512,256]{1,0:T(8,128)}, f32[512,256]{1,0:T(8,128)S(1)}, u32[]{:S(2)}, u32[]{:S(2)}) collective-permute-start(f32[512,256]{1,0:T(8,128)} %get-tuple-element.221), channel_id=1, source_target_pairs={{0,8},{4,12},{8,16},{12,20},{16,24},{20,28},{24,0},{28,4},{1,9},{5... | collective-permute-start | bytes 1572872 | tf_op jit(solution)/shard_map/ppermute | solution.py:466
  277.2 32.9 %collective-permute-start.18 = (f32[512,256]{1,0:T(8,128)}, f32[512,256]{1,0:T(8,128)S(1)}, u32[]{:S(2)}, u32[]{:S(2)}) collective-permute-start(f32[512,256]{1,0:T(8,128)} %get-tuple-element.222), channel_id=1, source_target_pairs={{0,16},{4,20},{8,24},{12,28},{16,0},{20,4},{24,8},{28,12},{1,17},{... | collective-permute-start | bytes 1572872 | tf_op jit(solution)/shard_map/ppermute | solution.py:466
  279.1 32.3 %collective-permute-start.19 = (f32[512,256]{1,0:T(8,128)}, f32[512,256]{1,0:T(8,128)S(1)}, u32[]{:S(2)}, u32[]{:S(2)}) collective-permute-start(f32[512,256]{1,0:T(8,128)} %get-tuple-element.223), channel_id=1, source_target_pairs={{0,24},{4,28},{8,0},{12,4},{16,8},{20,12},{24,16},{28,20},{1,25},{... | collective-permute-start | bytes 1572872 | tf_op jit(solution)/shard_map/ppermute | solution.py:466
  279.6 52.1 %collective-permute-start.24 = (f32[4,512,256]{2,1,0:T(8,128)}, f32[4,512,256]{2,1,0:T(8,128)}, u32[]{:S(2)}, u32[]{:S(2)}) collective-permute-start(f32[4,512,256]{2,1,0:T(8,128)} %get-tuple-element.230.refs_0_), channel_id=1, source_target_pairs={{0,2},{1,3},{2,0},{3,1},{4,6},{5,7},{6,4},{7,5},{8,10},{9,11},{10,... | collective-permute-start | bytes 6291464 | tf_op jit(solution)/shard_map/ppermute | solution.py:484
  282.6 1.3 copy-start.8
  305.9 5.5 %copy-start.13 = (f32[512,256]{1,0:T(8,128)}, f32[512,256]{1,0:T(8,128)S(1)}, u32[]{:S(2)}) copy-start(f32[512,256]{1,0:T(8,128)S(1)} %collective-permute-done.17.refs_9_) | copy-start | bytes 1572868
  310.1 1.3 copy-start.15
  311.4 0.8 copy-start.17
  315.3 56.5 %collective-permute-start.23 = (f32[4,512,256]{2,1,0:T(8,128)}, f32[4,512,256]{2,1,0:T(8,128)S(1)}, u32[]{:S(2)}, u32[]{:S(2)}) collective-permute-start(f32[4,512,256]{2,1,0:T(8,128)} %get-tuple-element.225.refs_0_), channel_id=1, source_target_pairs={{0,2},{1,3},{2,0},{3,1},{4,6},{5,7},{6,4},{7,5},{8,10},{9,11},{10,... | collective-permute-start | bytes 6291464 | tf_op jit(solution)/shard_map/ppermute | solution.py:484
  316.8 35.4 %collective-permute-start.20 = (f32[512,256]{1,0:T(8,128)}, f32[512,256]{1,0:T(8,128)S(1)}, u32[]{:S(2)}, u32[]{:S(2)}) collective-permute-start(f32[512,256]{1,0:T(8,128)} %get-tuple-element.227), channel_id=1, source_target_pairs={{0,8},{4,12},{8,16},{12,20},{16,24},{20,28},{24,0},{28,4},{1,9},{5... | collective-permute-start | bytes 1572872 | tf_op jit(solution)/shard_map/ppermute | solution.py:466
  328.5 36.8 %collective-permute-start.21 = (f32[512,256]{1,0:T(8,128)}, f32[512,256]{1,0:T(8,128)S(1)}, u32[]{:S(2)}, u32[]{:S(2)}) collective-permute-start(f32[512,256]{1,0:T(8,128)} %get-tuple-element.228), channel_id=1, source_target_pairs={{0,16},{4,20},{8,24},{12,28},{16,0},{20,4},{24,8},{28,12},{1,17},{... | collective-permute-start | bytes 1572872 | tf_op jit(solution)/shard_map/ppermute | solution.py:466
  331.8 33.6 %collective-permute-start.22 = (f32[512,256]{1,0:T(8,128)}, f32[512,256]{1,0:T(8,128)S(1)}, u32[]{:S(2)}, u32[]{:S(2)}) collective-permute-start(f32[512,256]{1,0:T(8,128)} %get-tuple-element.229), channel_id=1, source_target_pairs={{0,24},{4,28},{8,0},{12,4},{16,8},{20,12},{24,16},{28,20},{1,25},{... | collective-permute-start | bytes 1572872 | tf_op jit(solution)/shard_map/ppermute | solution.py:466
  352.3 19.5 %copy-start.5 = (f32[512,256]{1,0:T(8,128)}, f32[512,256]{1,0:T(8,128)S(1)}, u32[]{:S(2)}) copy-start(f32[512,256]{1,0:T(8,128)S(1)} %collective-permute-done.20.refs_1_) | copy-start | bytes 1572868
  365.3 6.5 %copy-start.6 = (f32[512,256]{1,0:T(8,128)}, f32[512,256]{1,0:T(8,128)S(1)}, u32[]{:S(2)}) copy-start(f32[512,256]{1,0:T(8,128)S(1)} %collective-permute-done.21.refs_2_) | copy-start | bytes 1572868
  365.3 6.5 %copy-start.7 = (f32[512,256]{1,0:T(8,128)}, f32[512,256]{1,0:T(8,128)S(1)}, u32[]{:S(2)}) copy-start(f32[512,256]{1,0:T(8,128)S(1)} %collective-permute-done.22.refs_3_) | copy-start | bytes 1572868
  371.8 1.4 copy-start.2
  373.2 8.8 %copy-start.26 = (f32[512]{0:T(512)S(1)}, f32[512]{0:T(512)}, u32[]{:S(2)}) copy-start(f32[512]{0:T(512)} %param.13) | copy-start | bytes 6148
  374.0 14.2 %collective-permute-start.25 = (f32[4,512,256]{2,1,0:T(8,128)}, f32[4,512,256]{2,1,0:T(8,128)S(1)}, u32[]{:S(2)}, u32[]{:S(2)}) collective-permute-start(f32[4,512,256]{2,1,0:T(8,128)} %get-tuple-element.241), channel_id=1, source_target_pairs={{0,1},{1,0},{2,3},{3,2},{4,5},{5,4},{6,7},{7,6},{8,9},{9,8},{10,11... | collective-permute-start | bytes 6291464 | tf_op jit(solution)/shard_map/ppermute | solution.py:489
  374.1 47.0 %collective-permute-start.27 = (f32[512,256]{1,0:T(8,128)}, f32[512,256]{1,0:T(8,128)S(1)}, u32[]{:S(2)}, u32[]{:S(2)}) collective-permute-start(f32[512,256]{1,0:T(8,128)} %get-tuple-element.252), channel_id=1, source_target_pairs={{0,8},{4,12},{8,16},{12,20},{16,24},{20,28},{24,0},{28,4},{1,9},{5... | collective-permute-start | bytes 1572872 | tf_op jit(solution)/shard_map/ppermute | solution.py:466
  379.5 41.5 %collective-permute-start.28 = (f32[512,256]{1,0:T(8,128)}, f32[512,256]{1,0:T(8,128)S(1)}, u32[]{:S(2)}, u32[]{:S(2)}) collective-permute-start(f32[512,256]{1,0:T(8,128)} %get-tuple-element.253), channel_id=1, source_target_pairs={{0,16},{4,20},{8,24},{12,28},{16,0},{20,4},{24,8},{28,12},{1,17},{... | collective-permute-start | bytes 1572872 | tf_op jit(solution)/shard_map/ppermute | solution.py:466
  379.8 41.2 %collective-permute-start.29 = (f32[512,256]{1,0:T(8,128)}, f32[512,256]{1,0:T(8,128)}, u32[]{:S(2)}, u32[]{:S(2)}) collective-permute-start(f32[512,256]{1,0:T(8,128)} %get-tuple-element.254), channel_id=1, source_target_pairs={{0,24},{4,28},{8,0},{12,4},{16,8},{20,12},{24,16},{28,20},{1,25},{... | collective-permute-start | bytes 1572872 | tf_op jit(solution)/shard_map/ppermute | solution.py:466
  388.2 1.3 copy-start.4
  389.5 6.1 %copy-start.25 = (f32[8,128]{1,0:T(8,128)S(1)}, f32[8,128]{1,0:T(8,128)}, u32[]{:S(2)}) copy-start(f32[8,128]{1,0:T(8,128)} %get-tuple-element.260) | copy-start | bytes 12292
  397.0 37.0 %all-to-all-start.3 = ((f32[32,16,128]{2,1,0:T(8,128)}), f32[32,16,128]{2,1,0:T(8,128)}, u32[]{:S(2)}, u32[]{:S(2)}) async-start(f32[32,16,128]{2,1,0:T(8,128)} %broadcast_in_dim.8), calls=%async_computation.3 | async-start | bytes 524288 | tf_op jit(solution)/shard_map/all_to_all | solution.py:494
  421.0 6.3 %collective-permute-start.26 = (f32[4,512,256]{2,1,0:T(8,128)}, f32[4,512,256]{2,1,0:T(8,128)}, u32[]{:S(2)}, u32[]{:S(2)}) collective-permute-start(f32[4,512,256]{2,1,0:T(8,128)} %get-tuple-element.250), channel_id=1, source_target_pairs={{0,1},{1,0},{2,3},{3,2},{4,5},{5,4},{6,7},{7,6},{8,9},{9,8},{10,11... | collective-permute-start | bytes 6291464 | tf_op jit(solution)/shard_map/ppermute | solution.py:489
  421.1 0.8 copy-start.10
  421.1 1.0 copy-start.11
  427.4 6.0 %copy-start.24 = (f32[8,128]{1,0:T(8,128)S(1)}, f32[8,128]{1,0:T(8,128)}, u32[]{:S(2)}) copy-start(f32[8,128]{1,0:T(8,128)} %get-tuple-element.258) | copy-start | bytes 12292
  434.7 24.9 %all-to-all-start.2 = ((f32[32,16,128]{2,1,0:T(8,128)}), f32[32,16,128]{2,1,0:T(8,128)S(1)}, u32[]{:S(2)}, u32[]{:S(2)}) async-start(f32[32,16,128]{2,1,0:T(8,128)} %broadcast_in_dim.7), calls=%async_computation.2 | async-start | bytes 524288 | tf_op jit(solution)/shard_map/all_to_all | solution.py:494
  459.6 0.7 copy-start.9

commit v7 on v6

--- a/solution.py
+++ b/solution.py
@@ -579,12 +579,13 @@
     home2 = over_z(smooth2)
     x1 = over_x(home1)
     terms0 = time_call(chain, x0, time, n_c)
-    home2, x1, terms0, smooth3 = pass_on(home2, x1[1:], terms0, smooth3)
+    home2, terms0, smooth3 = pass_on(home2, terms0, smooth3)
 
     home3 = over_z(smooth3)
     outer0 = Outer(over_core(terms0))
     outer2 = Outer(home2)
     sums2 = sums(outer2, 2)
+    (x1,) = pass_on(x1[1:], hint=20 << 20)
     sums0 = sums(outer0, 0)
     terms1 = time_call(chain, [home1] + x1, time, n_c)
     outer1 = Outer(over_core(terms1))

time: 476 us -> 475 us (level)
  waiting for transfers between devices: 50.5 us -> 43 us
  starting transfers between devices: 90.4 us -> 96.5 us
    ppermute x4, waiting for transfers between devices: 10.2 us -> 3.76 us  [over_x(): found.append(lax.ppermute(cells, 'day', pairs))]
    ppermute x18, starting transfers between devices: 51 us -> 57 us  [over_z(): found.append(lax.ppermute(pieces[k], 'sta', pairs))]
    pallas_call x31 -> x32, Pallas kernels: 317 us -> 318 us  [__call__(): pl.pallas_call(kernel, grid_spec=pltpu.PrefetchScalarGridSpec(num_scalar_...]
  transfers between devices with their start and end apart: 34 -> 34, of which waited for: 11 -> 10; matrix products, arithmetic and copies ran while one was open for 1% -> 1% of each run, Pallas kernels for 62% -> 62%
where the time goes in v7:
time: 475 us; the launch traced here: 474 us
  Pallas kernels  318 us (67%)
  starting transfers between devices  96.5 us (20%)
  waiting for transfers between devices  43 us (9%)
  local copies, waits for them, and re-layouts  13.2 us (3%)
    pallas_call x32, Pallas kernels, __call__(): pl.pallas_call(kernel, grid_spec=pltpu.PrefetchScalarGridSpec(num_scalar_...  318 us
    ppermute x18, starting transfers between devices, over_z(): found.append(lax.ppermute(pieces[k], 'sta', pairs))  57 us
    ppermute x18, waiting for transfers between devices, over_z(): found.append(lax.ppermute(pieces[k], 'sta', pairs))  21.2 us
    all_to_all x2, starting transfers between devices, over_all(): return lax.all_to_all(many, ('sta', 'day'), 0, 0, tiled=True)  14.2 us
    all_to_all x2, starting transfers between devices, over_z_at_once(): lax.all_to_all(pieces, 'sta', 0, 0, axis_index_groups=groups, tiled=True)  13.8 us
    unnamed x54, local copies, waits for them, and re-layouts  10.9 us
  transfers between devices with their start and end apart: 34, of which 10 were waited for; matrix products, arithmetic and copies ran while one was open for 1% of the time, Pallas kernels for 62%

profile of v7, /device:TPU:0, one launch (start us, length us, event | category | flops | bytes accessed | tf_op | source)
XLA Modules:
  0.0 474.3 jit_solution(6265728107352753699)
XLA Ops:
  1.3 4.0 mask.4
  5.3 2.9 collective-permute-start
  8.2 4.0 mask.5
  12.2 1.6 collective-permute-start.1
  13.8 2.6 collective-permute-start.2
  16.4 1.3 collective-permute-start.3
  17.7 4.0 mask.6
  21.7 4.0 mask.7
  25.7 22.3 %time_entries.1 = (bf16[2048,2048]{1,0:T(8,128)(2,1)}, bf16[2048,2048]{1,0:T(8,128)(2,1)}, f32[8,128]{1,0:T(8,128)}) custom-call(s32[4]{0:T(128)} %pad_add_fusion.place, f32[4,4096]{1,0:T(4,128)} %refs_1_.13, f32[4,4096]{1,0:T(4,128)} %refs_1_.13, f32[8,128]{1,0:T(8,128)} %get-tuple-element.147.refs_2_), custom_call_target="tpu_custom_call" | custom-call | tf_op jit(solution)/shard_map/time_entries/pallas_call | solution.py:40
  48.0 2.3 collective-permute-done.2.refs_5_
  50.3 3.8 collective-permute-done.refs_2_
  54.1 1.3 copy-done.2
  55.3 3.1 gate.9
  58.4 1.8 collective-permute-start.4
  60.2 1.5 collective-permute-start.5
  61.8 9.4 %all-to-all-start = ((f32[4,512,256]{2,1,0:T(8,128)}), f32[4,512,256]{2,1,0:T(8,128)S(1)}, u32[]{:S(2)}, u32[]{:S(2)}) async-start(f32[4,512,256]{2,1,0:T(8,128)} %get-tuple-element.161), calls=%async_computation | async-start | bytes 4194304 | tf_op jit(solution)/shard_map/all_to_all | solution.py:471
  71.1 20.5 %time.4 = (f32[4,512,256]{2,1,0:T(8,128)}, f32[4,512,256]{2,1,0:T(8,128)}, f32[8,128]{1,0:T(8,128)}) custom-call(s32[4]{0:T(128)} %pad_add_fusion.place, f32[4,512,256]{2,1,0:T(8,128)} %get-tuple-element.142.refs_0_, f32[4,512,256]{2,1,0:T(8,128)} %get-tuple-element.151.refs_1_, bf16[2048,2048]{1,0:T(8,128)(2,1)} %get-tuple-element.152.refs_2_, ...), custom_call_target="tpu_custom_call" | custom-call | tf_op jit(solution)/shard_map/time/pallas_call | solution.py:40
  91.6 17.4 %space_entries.2 = (bf16[2048,2048]{1,0:T(8,128)(2,1)}, bf16[2048,2048]{1,0:T(8,128)(2,1)}, f32[8,128]{1,0:T(8,128)}) custom-call(s32[4]{0:T(128)} %pad_add_fusion.place, f32[2,4096]{1,0:T(2,128)} %refs_3_.9, f32[2,4096]{1,0:T(2,128)} %refs_3_.9, f32[2,4096]{1,0:T(2,128)} %refs_3_.9, f32[2,4096]{1,0:T(2,128)} %refs_3_.9, f32[8,128]{1,0:T(8,128)} %get-tuple-element.155.refs_4_), custom_call_target="tpu_custom_call" | custom-call | tf_op jit(solution)/shard_map/space_entries/pallas_call | solution.py:40
  109.8 4.0 add.19
  113.7 4.1 all-to-all-done.refs_0_
  117.8 1.3 copy-done
  119.7 4.5 all-to-all-start.1
  124.2 20.5 %time.5 = (f32[4,512,256]{2,1,0:T(8,128)}, f32[4,512,256]{2,1,0:T(8,128)}, f32[8,128]{1,0:T(8,128)}) custom-call(s32[4]{0:T(128)} %pad_add_fusion.place, f32[4,512,256]{2,1,0:T(8,128)} %get-tuple-element.150.refs_0_, f32[4,512,256]{2,1,0:T(8,128)} %get-tuple-element.160.refs_1_, bf16[2048,2048]{1,0:T(8,128)(2,1)} %get-tuple-element.152.refs_2_, ...), custom_call_target="tpu_custom_call" | custom-call | tf_op jit(solution)/shard_map/time/pallas_call | solution.py:40
  145.3 17.5 %space_entries.3 = (bf16[2048,2048]{1,0:T(8,128)(2,1)}, bf16[2048,2048]{1,0:T(8,128)(2,1)}, f32[8,128]{1,0:T(8,128)}) custom-call(s32[4]{0:T(128)} %pad_add_fusion.place, f32[2,4096]{1,0:T(2,128)} %refs_3_.9, f32[2,4096]{1,0:T(2,128)} %refs_3_.9, f32[2,4096]{1,0:T(2,128)} %refs_3_.9, f32[2,4096]{1,0:T(2,128)} %refs_3_.9, f32[8,128]{1,0:T(8,128)} %get-tuple-element.168.refs_4_), custom_call_target="tpu_custom_call" | custom-call | tf_op jit(solution)/shard_map/space_entries/pallas_call | solution.py:40
  162.8 3.9 add.20
  166.7 5.3 %all-to-all-done.1.refs_0_ = f32[4,512,256]{2,1,0:T(8,128)} async-done(((f32[4,512,256]{2,1,0:T(8,128)}), f32[4,512,256]{2,1,0:T(8,128)}, u32[]{:S(2)}, u32[]{:S(2)}) %all-to-all-start.1) | async-done | bytes 2097184 | tf_op jit(solution)/shard_map/all_to_all | solution.py:471
  173.3 2.2 collective-permute-start.11
  176.0 22.0 %space.4 = (f32[512,256]{1,0:T(8,128)}, f32[512,256]{1,0:T(8,128)}, f32[512,256]{1,0:T(8,128)}, f32[512,256]{1,0:T(8,128)}, f32[8,128]{1,0:T(8,128)}) custom-call(s32[4]{0:T(128)} %pad_add_fusion.place, f32[4,512,256]{2,1,0:T(8,128)} %get-tuple-element.149.refs_0_, f32[4,512,256]{2,1,0:T(8,128)} %get-tuple-element.157.refs_1_, ...), custom_call_target="tpu_custom_call" | custom-call | tf_op jit(solution)/shard_map/space/pallas_call | solution.py:40
  198.0 22.0 %space.5 = (f32[512,256]{1,0:T(8,128)}, f32[512,256]{1,0:T(8,128)}, f32[512,256]{1,0:T(8,128)}, f32[512,256]{1,0:T(8,128)}, f32[8,128]{1,0:T(8,128)}) custom-call(s32[4]{0:T(128)} %pad_add_fusion.place, f32[4,512,256]{2,1,0:T(8,128)} %get-tuple-element.185.refs_0_, f32[4,512,256]{2,1,0:T(8,128)} %collective-permute-done.8.refs_1_, ...), custom_call_target="tpu_custom_call" | custom-call | tf_op jit(solution)/shard_map/space/pallas_call | solution.py:40
  221.2 3.1 gate.13
  224.3 0.9 collective-permute-start.16
  225.2 2.0 collective-permute-start.13
  227.2 1.9 collective-permute-start.14
  229.0 1.9 collective-permute-start.15
  231.0 7.3 %collective-permute-done.12.refs_1_ = f32[4,512,256]{2,1,0:T(8,128)} collective-permute-done((f32[4,512,256]{2,1,0:T(8,128)}, f32[4,512,256]{2,1,0:T(8,128)}, u32[]{:S(2)}, u32[]{:S(2)}) %collective-permute-start.12) | collective-permute-done | bytes 2097184 | tf_op jit(solution)/shard_map/ppermute | solution.py:477
  238.3 22.0 %space.6 = (f32[512,256]{1,0:T(8,128)}, f32[512,256]{1,0:T(8,128)}, f32[512,256]{1,0:T(8,128)}, f32[512,256]{1,0:T(8,128)}, f32[8,128]{1,0:T(8,128)}) custom-call(s32[4]{0:T(128)} %pad_add_fusion.place, f32[4,512,256]{2,1,0:T(8,128)} %get-tuple-element.200.refs_0_, f32[4,512,256]{2,1,0:T(8,128)} %collective-permute-done.12.refs_1_, ...), custom_call_target="tpu_custom_call" | custom-call | tf_op jit(solution)/shard_map/space/pallas_call | solution.py:40
  260.3 1.3 collective-permute-done.14.refs_10_
  262.6 3.2 gate.14
  265.7 11.6 %collective-permute-start.17 = (f32[512,256]{1,0:T(8,128)}, f32[512,256]{1,0:T(8,128)S(1)}, u32[]{:S(2)}, u32[]{:S(2)}) collective-permute-start(f32[512,256]{1,0:T(8,128)} %get-tuple-element.222), channel_id=1, source_target_pairs={{0,8},{4,12},{8,16},{12,20},{16,24},{20,28},{24,0},{28,4},{1,9},{5... | collective-permute-start | bytes 1572872 | tf_op jit(solution)/shard_map/ppermute | solution.py:466
  277.3 1.8 collective-permute-start.18
  279.7 1.5 collective-permute-start.24
  281.2 1.4 collective-permute-done.16.refs_1_
  282.7 1.3 copy-done.7
  284.0 22.0 %space.7 = (f32[512,256]{1,0:T(8,128)}, f32[512,256]{1,0:T(8,128)}, f32[512,256]{1,0:T(8,128)}, f32[512,256]{1,0:T(8,128)}, f32[8,128]{1,0:T(8,128)}) custom-call(s32[4]{0:T(128)} %pad_add_fusion.place, f32[4,512,256]{2,1,0:T(8,128)} %get-tuple-element.215.refs_0_, f32[4,512,256]{2,1,0:T(8,128)} %copy-done.7, bf16[2048,2048]{1,0:T(8,128)(2,1)} %get-tuple-element.158.refs_2_, ...), custom_call_target="tpu_custom_call" | custom-call | tf_op jit(solution)/shard_map/space/pallas_call | solution.py:40
  306.0 4.2 collective-permute-done.18.refs_10_
  310.2 1.3 collective-permute-done.19.refs_11_
  312.3 3.2 gate.15
  315.5 1.6 collective-permute-start.20
  317.0 11.7 %collective-permute-start.21 = (f32[512,256]{1,0:T(8,128)}, f32[512,256]{1,0:T(8,128)S(1)}, u32[]{:S(2)}, u32[]{:S(2)}) collective-permute-start(f32[512,256]{1,0:T(8,128)} %get-tuple-element.228), channel_id=1, source_target_pairs={{0,8},{4,12},{8,16},{12,20},{16,24},{20,28},{24,0},{28,4},{1,9},{5... | collective-permute-start | bytes 1572872 | tf_op jit(solution)/shard_map/ppermute | solution.py:466
  328.7 3.3 collective-permute-start.22
  332.9 20.5 %time.6 = (f32[4,512,256]{2,1,0:T(8,128)}, f32[4,512,256]{2,1,0:T(8,128)}, f32[8,128]{1,0:T(8,128)}) custom-call(s32[4]{0:T(128)} %pad_add_fusion.place, f32[4,512,256]{2,1,0:T(8,128)} %get-tuple-element.231.refs_0_, f32[4,512,256]{2,1,0:T(8,128)} %collective-permute-done.24.refs_1_, bf16[2048,2048]{1,0:T(8,128)(2,1)} %get-tuple-element.152.refs_2_, ...), custom_call_target="tpu_custom_call" | custom-call | tf_op jit(solution)/shard_map/time/pallas_call | solution.py:40
  353.4 12.1 %collective-permute-done.22.refs_2_ = f32[512,256]{1,0:T(8,128)S(1)} collective-permute-done((f32[512,256]{1,0:T(8,128)}, f32[512,256]{1,0:T(8,128)S(1)}, u32[]{:S(2)}, u32[]{:S(2)}) %collective-permute-start.22) | collective-permute-done | bytes 524320 | tf_op jit(solution)/shard_map/ppermute | solution.py:466
  367.3 11.5 %collective-permute-start.27 = (f32[512,256]{1,0:T(8,128)}, f32[512,256]{1,0:T(8,128)S(1)}, u32[]{:S(2)}, u32[]{:S(2)}) collective-permute-start(f32[512,256]{1,0:T(8,128)} %get-tuple-element.254), channel_id=1, source_target_pairs={{0,8},{4,12},{8,16},{12,20},{16,24},{20,28},{24,0},{28,4},{1,9},{5... | collective-permute-start | bytes 1572872 | tf_op jit(solution)/shard_map/ppermute | solution.py:466
  378.9 2.5 collective-permute-start.29
  381.3 5.3 %sums.4 = (f32[8,128]{1,0:T(8,128)}, f32[8,128]{1,0:T(8,128)}) custom-call(s32[4]{0:T(128)} %pad_add_fusion.place, s32[512,1024]{1,0:T(8,128)} %refs_1_.17, f32[512,1]{1,0:T(8,128)} %copy.63.refs_1_.refs_2_, f32[4,512,1024]{2,1,0:T(8,128)} %refs_4_.3, f32[4,512,1024]{2,1,0:T(8,128)} %refs_5_.3, f32[512,256]{1,0:T(8,128)} %get-tuple-element.240.refs_4_.refs_8_, ...), custom_call_target="tpu_custom_call" | custom-call | tf_op jit(solution)/shard_map/sums/pallas_call | solution.py:40
  387.4 1.3 copy-done.3
  388.7 6.1 %sums.5 = (f32[8,128]{1,0:T(8,128)}, f32[8,128]{1,0:T(8,128)}) custom-call(s32[4]{0:T(128)} %pad_add_fusion.place, s32[512,1024]{1,0:T(8,128)} %refs_1_.17, f32[512,1]{1,0:T(8,128)} %copy.63.refs_1_.refs_2_, f32[4,512,1024]{2,1,0:T(8,128)} %refs_4_.3, f32[4,512,1024]{2,1,0:T(8,128)} %refs_5_.3, f32[4,512,256]{2,1,0:T(8,128)} %get-tuple-element.247.refs_4_.refs_6_, ...), custom_call_target="tpu_custom_call" | custom-call | tf_op jit(solution)/shard_map/sums/pallas_call | solution.py:40
  396.2 3.6 all-to-all-start.3
  399.8 20.5 %time.7 = (f32[4,512,256]{2,1,0:T(8,128)}, f32[4,512,256]{2,1,0:T(8,128)}, f32[8,128]{1,0:T(8,128)}) custom-call(s32[4]{0:T(128)} %pad_add_fusion.place, f32[4,512,256]{2,1,0:T(8,128)} %get-tuple-element.226.refs_0_, f32[4,512,256]{2,1,0:T(8,128)} %get-tuple-element.246.refs_1_, bf16[2048,2048]{1,0:T(8,128)(2,1)} %get-tuple-element.152.refs_2_, ...), custom_call_target="tpu_custom_call" | custom-call | tf_op jit(solution)/shard_map/time/pallas_call | solution.py:40
  421.4 5.3 %sums.6 = (f32[8,128]{1,0:T(8,128)}, f32[8,128]{1,0:T(8,128)}) custom-call(s32[4]{0:T(128)} %pad_add_fusion.place, s32[512,1024]{1,0:T(8,128)} %refs_1_.17, f32[512,1]{1,0:T(8,128)} %copy.63.refs_1_.refs_2_, f32[4,512,1024]{2,1,0:T(8,128)} %refs_4_.3, f32[4,512,1024]{2,1,0:T(8,128)} %refs_5_.3, f32[512,256]{1,0:T(8,128)} %get-tuple-element.253.refs_4_.refs_8_, ...), custom_call_target="tpu_custom_call" | custom-call | flops 241172480000 | bytes 209715200 | tf_op jit(solution)/shard_map/sums/pallas_call | solution.py:40
  426.7 6.0 %sums.7 = (f32[8,128]{1,0:T(8,128)}, f32[8,128]{1,0:T(8,128)}) custom-call(s32[4]{0:T(128)} %pad_add_fusion.place, s32[512,1024]{1,0:T(8,128)} %refs_1_.17, f32[512,1]{1,0:T(8,128)} %copy.63.refs_1_.refs_2_, f32[4,512,1024]{2,1,0:T(8,128)} %refs_4_.3, f32[4,512,1024]{2,1,0:T(8,128)} %refs_5_.3, f32[4,512,256]{2,1,0:T(8,128)} %get-tuple-element.251.refs_4_.refs_6_, ...), custom_call_target="tpu_custom_call" | custom-call | tf_op jit(solution)/shard_map/sums/pallas_call | solution.py:40
  434.1 10.7 %all-to-all-start.2 = ((f32[32,16,128]{2,1,0:T(8,128)}), f32[32,16,128]{2,1,0:T(8,128)S(1)}, u32[]{:S(2)}, u32[]{:S(2)}) async-start(f32[32,16,128]{2,1,0:T(8,128)} %broadcast_in_dim.7), calls=%async_computation.2 | async-start | bytes 524288 | tf_op jit(solution)/shard_map/all_to_all | solution.py:494
  444.8 14.3 %update.2 = (f32[4,512,1024]{2,1,0:T(8,128)}, f32[4,512,1024]{2,1,0:T(8,128)}, f32[4,512,1024]{2,1,0:T(8,128)}, f32[8,128]{1,0:T(8,128)}) custom-call(s32[4]{0:T(128)} %pad_add_fusion.place, f32[32,16,128]{2,1,0:T(8,128)} %all-to-all-done.3.refs_0_, s32[512,1024]{1,0:T(8,128)} %refs_1_.17, f32[512,1]{1,0:T(8,128)} %copy.63.refs_1_.refs_2_, ...), custom_call_target="tpu_custom_call" | custom-call | tf_op jit(solution)/shard_map/update/pallas_call | solution.py:40
  459.8 14.3 %update.3 = (f32[4,512,1024]{2,1,0:T(8,128)}, f32[4,512,1024]{2,1,0:T(8,128)}, f32[4,512,1024]{2,1,0:T(8,128)}, f32[8,128]{1,0:T(8,128)}) custom-call(s32[4]{0:T(128)} %pad_add_fusion.place, f32[32,16,128]{2,1,0:T(8,128)} %copy-done.8, s32[512,1024]{1,0:T(8,128)} %refs_1_.17, ...), custom_call_target="tpu_custom_call", output_to_operand_aliasing={{0}: (13, {}), {1}: (14, {}), {2}: (15, {})} | custom-call | tf_op jit(solution)/shard_map/update/pallas_call | solution.py:40
  (96 shorter events, 15.8 us)
Async XLA Ops:
  5.3 48.8 %collective-permute-start = (f32[4,512,256]{2,1,0:T(8,128)}, f32[4,512,256]{2,1,0:T(8,128)S(1)}, u32[]{:S(2)}, u32[]{:S(2)}) collective-permute-start(f32[4,512,256]{2,1,0:T(8,128)} %get-tuple-element.142.refs_0_), channel_id=1, source_target_pairs={{0,2},{1,3},{2,0},{3,1},{4,6},{5,7},{6,4},{7,5},{8,10},{9,11},{10,... | collective-permute-start | bytes 6291464 | tf_op jit(solution)/shard_map/ppermute | solution.py:484
  12.2 35.8 %collective-permute-start.1 = (f32[512,256]{1,0:T(8,128)}, f32[512,256]{1,0:T(8,128)S(1)}, u32[]{:S(2)}, u32[]{:S(2)}) collective-permute-start(f32[512,256]{1,0:T(8,128)} %get-tuple-element.144), channel_id=1, source_target_pairs={{0,8},{4,12},{8,16},{12,20},{16,24},{20,28},{24,0},{28,4},{1,9},{5... | collective-permute-start | bytes 1572872 | tf_op jit(solution)/shard_map/ppermute | solution.py:466
  13.8 36.5 %collective-permute-start.2 = (f32[512,256]{1,0:T(8,128)}, f32[512,256]{1,0:T(8,128)S(1)}, u32[]{:S(2)}, u32[]{:S(2)}) collective-permute-start(f32[512,256]{1,0:T(8,128)} %get-tuple-element.145), channel_id=1, source_target_pairs={{0,16},{4,20},{8,24},{12,28},{16,0},{20,4},{24,8},{28,12},{1,17},{... | collective-permute-start | bytes 1572872 | tf_op jit(solution)/shard_map/ppermute | solution.py:466
  16.4 33.9 %collective-permute-start.3 = (f32[512,256]{1,0:T(8,128)}, f32[512,256]{1,0:T(8,128)S(1)}, u32[]{:S(2)}, u32[]{:S(2)}) collective-permute-start(f32[512,256]{1,0:T(8,128)} %get-tuple-element.146), channel_id=1, source_target_pairs={{0,24},{4,28},{8,0},{12,4},{16,8},{20,12},{24,16},{28,20},{1,25},{... | collective-permute-start | bytes 1572872 | tf_op jit(solution)/shard_map/ppermute | solution.py:466
  48.0 6.1 %copy-start.21 = (f32[512,256]{1,0:T(8,128)}, f32[512,256]{1,0:T(8,128)S(1)}, u32[]{:S(2)}) copy-start(f32[512,256]{1,0:T(8,128)S(1)} %collective-permute-done.1.refs_4_) | copy-start | bytes 1572868
  50.3 3.8 copy-start.22
  50.3 3.8 copy-start.23
  54.0 1.3 copy-start.2
  58.4 50.6 %collective-permute-start.4 = (f32[4,512,256]{2,1,0:T(8,128)}, f32[4,512,256]{2,1,0:T(8,128)}, u32[]{:S(2)}, u32[]{:S(2)}) collective-permute-start(f32[4,512,256]{2,1,0:T(8,128)} %get-tuple-element.150.refs_0_), channel_id=1, source_target_pairs={{0,2},{1,3},{2,0},{3,1},{4,6},{5,7},{6,4},{7,5},{8,10},{9,11},{10,... | collective-permute-start | bytes 6291464 | tf_op jit(solution)/shard_map/ppermute | solution.py:484
  60.2 48.8 %collective-permute-start.5 = (f32[4,512,256]{2,1,0:T(8,128)}, f32[4,512,256]{2,1,0:T(8,128)}, u32[]{:S(2)}, u32[]{:S(2)}) collective-permute-start(f32[4,512,256]{2,1,0:T(8,128)} %get-tuple-element.149.refs_0_), channel_id=1, source_target_pairs={{0,4},{4,0},{8,12},{12,8},{16,20},{20,16},{24,28},{28,24},{1,5},{5... | collective-permute-start | bytes 6291464 | tf_op jit(solution)/shard_map/ppermute | solution.py:477
  61.8 56.0 %all-to-all-start = ((f32[4,512,256]{2,1,0:T(8,128)}), f32[4,512,256]{2,1,0:T(8,128)S(1)}, u32[]{:S(2)}, u32[]{:S(2)}) async-start(f32[4,512,256]{2,1,0:T(8,128)} %get-tuple-element.161), calls=%async_computation | async-start | bytes 4194304 | tf_op jit(solution)/shard_map/all_to_all | solution.py:471
  91.6 18.1 %collective-permute-start.6 = (f32[4,512,256]{2,1,0:T(8,128)}, f32[4,512,256]{2,1,0:T(8,128)}, u32[]{:S(2)}, u32[]{:S(2)}) collective-permute-start(f32[4,512,256]{2,1,0:T(8,128)} %get-tuple-element.163), channel_id=1, source_target_pairs={{0,1},{1,0},{2,3},{3,2},{4,5},{5,4},{6,7},{7,6},{8,9},{9,8},{10,11... | collective-permute-start | bytes 6291464 | tf_op jit(solution)/shard_map/ppermute | solution.py:489
  117.8 1.3 copy-start
  119.7 52.2 %all-to-all-start.1 = ((f32[4,512,256]{2,1,0:T(8,128)}), f32[4,512,256]{2,1,0:T(8,128)}, u32[]{:S(2)}, u32[]{:S(2)}) async-start(f32[4,512,256]{2,1,0:T(8,128)} %get-tuple-element.171), calls=%async_computation.1 | async-start | bytes 4194304 | tf_op jit(solution)/shard_map/all_to_all | solution.py:471
  124.2 20.5 %copy-start.1 = (f32[4,512,256]{2,1,0:T(8,128)S(1)}, f32[4,512,256]{2,1,0:T(8,128)}, u32[]{:S(2)}) copy-start(f32[4,512,256]{2,1,0:T(8,128)} %get-tuple-element.185.refs_0_) | copy-start | bytes 6291460
  144.7 18.0 %collective-permute-start.7 = (f32[4,512,256]{2,1,0:T(8,128)}, f32[4,512,256]{2,1,0:T(8,128)}, u32[]{:S(2)}, u32[]{:S(2)}) collective-permute-start(f32[4,512,256]{2,1,0:T(8,128)} %get-tuple-element.173), channel_id=1, source_target_pairs={{0,1},{1,0},{2,3},{3,2},{4,5},{5,4},{6,7},{7,6},{8,9},{9,8},{10,11... | collective-permute-start | bytes 6291464 | tf_op jit(solution)/shard_map/ppermute | solution.py:489
  144.7 53.3 %collective-permute-start.8 = (f32[4,512,256]{2,1,0:T(8,128)S(1)}, f32[4,512,256]{2,1,0:T(8,128)}, u32[]{:S(2)}, u32[]{:S(2)}) collective-permute-start(f32[4,512,256]{2,1,0:T(8,128)S(1)} %copy-done.1), channel_id=1, source_target_pairs={{0,4},{4,0},{8,12},{12,8},{16,20},{20,16},{24,28},{28,24},{1,5},{5... | collective-permute-start | bytes 6291464 | tf_op jit(solution)/shard_map/ppermute | solution.py:477
  172.6 47.4 %collective-permute-start.10 = (f32[512,256]{1,0:T(8,128)}, f32[512,256]{1,0:T(8,128)S(1)}, u32[]{:S(2)}, u32[]{:S(2)}) collective-permute-start(f32[512,256]{1,0:T(8,128)} %get-tuple-element.193), channel_id=1, source_target_pairs={{0,16},{4,20},{8,24},{12,28},{16,0},{20,4},{24,8},{28,12},{1,17},{... | collective-permute-start | bytes 1572872 | tf_op jit(solution)/shard_map/ppermute | solution.py:466
  172.7 65.6 %collective-permute-start.12 = (f32[4,512,256]{2,1,0:T(8,128)}, f32[4,512,256]{2,1,0:T(8,128)}, u32[]{:S(2)}, u32[]{:S(2)}) collective-permute-start(f32[4,512,256]{2,1,0:T(8,128)} %get-tuple-element.200.refs_0_), channel_id=1, source_target_pairs={{0,4},{4,0},{8,12},{12,8},{16,20},{20,16},{24,28},{28,24},{1,5},{5... | collective-permute-start | bytes 6291464 | tf_op jit(solution)/shard_map/ppermute | solution.py:477
  173.3 46.8 %collective-permute-start.11 = (f32[512,256]{1,0:T(8,128)}, f32[512,256]{1,0:T(8,128)S(1)}, u32[]{:S(2)}, u32[]{:S(2)}) collective-permute-start(f32[512,256]{1,0:T(8,128)} %get-tuple-element.194), channel_id=1, source_target_pairs={{0,24},{4,28},{8,0},{12,4},{16,8},{20,12},{24,16},{28,20},{1,25},{... | collective-permute-start | bytes 1572872 | tf_op jit(solution)/shard_map/ppermute | solution.py:466
  175.5 44.6 %collective-permute-start.9 = (f32[512,256]{1,0:T(8,128)}, f32[512,256]{1,0:T(8,128)S(1)}, u32[]{:S(2)}, u32[]{:S(2)}) collective-permute-start(f32[512,256]{1,0:T(8,128)} %get-tuple-element.192), channel_id=1, source_target_pairs={{0,8},{4,12},{8,16},{12,20},{16,24},{20,28},{24,0},{28,4},{1,9},{5... | collective-permute-start | bytes 1572872 | tf_op jit(solution)/shard_map/ppermute | solution.py:466
  220.1 0.8 copy-start.12
  220.1 1.0 copy-start.14
  220.1 1.1 copy-start.16
  224.3 58.3 %collective-permute-start.16 = (f32[4,512,256]{2,1,0:T(8,128)}, f32[4,512,256]{2,1,0:T(8,128)S(1)}, u32[]{:S(2)}, u32[]{:S(2)}) collective-permute-start(f32[4,512,256]{2,1,0:T(8,128)} %get-tuple-element.215.refs_0_), channel_id=1, source_target_pairs={{0,4},{4,0},{8,12},{12,8},{16,20},{20,16},{24,28},{28,24},{1,5},{5... | collective-permute-start | bytes 6291464 | tf_op jit(solution)/shard_map/ppermute | solution.py:477
  225.2 35.1 %collective-permute-start.13 = (f32[512,256]{1,0:T(8,128)}, f32[512,256]{1,0:T(8,128)S(1)}, u32[]{:S(2)}, u32[]{:S(2)}) collective-permute-start(f32[512,256]{1,0:T(8,128)} %get-tuple-element.207), channel_id=1, source_target_pairs={{0,8},{4,12},{8,16},{12,20},{16,24},{20,28},{24,0},{28,4},{1,9},{5... | collective-permute-start | bytes 1572872 | tf_op jit(solution)/shard_map/ppermute | solution.py:466
  227.2 34.4 %collective-permute-start.14 = (f32[512,256]{1,0:T(8,128)}, f32[512,256]{1,0:T(8,128)S(1)}, u32[]{:S(2)}, u32[]{:S(2)}) collective-permute-start(f32[512,256]{1,0:T(8,128)} %get-tuple-element.208), channel_id=1, source_target_pairs={{0,16},{4,20},{8,24},{12,28},{16,0},{20,4},{24,8},{28,12},{1,17},{... | collective-permute-start | bytes 1572872 | tf_op jit(solution)/shard_map/ppermute | solution.py:466
  229.0 32.5 %collective-permute-start.15 = (f32[512,256]{1,0:T(8,128)}, f32[512,256]{1,0:T(8,128)S(1)}, u32[]{:S(2)}, u32[]{:S(2)}) collective-permute-start(f32[512,256]{1,0:T(8,128)} %get-tuple-element.209), channel_id=1, source_target_pairs={{0,24},{4,28},{8,0},{12,4},{16,8},{20,12},{24,16},{28,20},{1,25},{... | collective-permute-start | bytes 1572872 | tf_op jit(solution)/shard_map/ppermute | solution.py:466
  260.3 1.3 copy-start.18
  261.6 0.8 copy-start.19
  261.6 1.0 copy-start.20
  265.7 40.3 %collective-permute-start.17 = (f32[512,256]{1,0:T(8,128)}, f32[512,256]{1,0:T(8,128)S(1)}, u32[]{:S(2)}, u32[]{:S(2)}) collective-permute-start(f32[512,256]{1,0:T(8,128)} %get-tuple-element.222), channel_id=1, source_target_pairs={{0,8},{4,12},{8,16},{12,20},{16,24},{20,28},{24,0},{28,4},{1,9},{5... | collective-permute-start | bytes 1572872 | tf_op jit(solution)/shard_map/ppermute | solution.py:466
  277.3 32.9 %collective-permute-start.18 = (f32[512,256]{1,0:T(8,128)}, f32[512,256]{1,0:T(8,128)S(1)}, u32[]{:S(2)}, u32[]{:S(2)}) collective-permute-start(f32[512,256]{1,0:T(8,128)} %get-tuple-element.223), channel_id=1, source_target_pairs={{0,16},{4,20},{8,24},{12,28},{16,0},{20,4},{24,8},{28,12},{1,17},{... | collective-permute-start | bytes 1572872 | tf_op jit(solution)/shard_map/ppermute | solution.py:466
  279.1 32.4 %collective-permute-start.19 = (f32[512,256]{1,0:T(8,128)}, f32[512,256]{1,0:T(8,128)S(1)}, u32[]{:S(2)}, u32[]{:S(2)}) collective-permute-start(f32[512,256]{1,0:T(8,128)} %get-tuple-element.224), channel_id=1, source_target_pairs={{0,24},{4,28},{8,0},{12,4},{16,8},{20,12},{24,16},{28,20},{1,25},{... | collective-permute-start | bytes 1572872 | tf_op jit(solution)/shard_map/ppermute | solution.py:466
  279.7 53.2 %collective-permute-start.24 = (f32[4,512,256]{2,1,0:T(8,128)}, f32[4,512,256]{2,1,0:T(8,128)}, u32[]{:S(2)}, u32[]{:S(2)}) collective-permute-start(f32[4,512,256]{2,1,0:T(8,128)} %get-tuple-element.231.refs_0_), channel_id=1, source_target_pairs={{0,2},{1,3},{2,0},{3,1},{4,6},{5,7},{6,4},{7,5},{8,10},{9,11},{10,... | collective-permute-start | bytes 6291464 | tf_op jit(solution)/shard_map/ppermute | solution.py:484
  282.7 1.3 copy-start.7
  306.0 5.5 %copy-start.13 = (f32[512,256]{1,0:T(8,128)}, f32[512,256]{1,0:T(8,128)S(1)}, u32[]{:S(2)}) copy-start(f32[512,256]{1,0:T(8,128)S(1)} %collective-permute-done.17.refs_9_) | copy-start | bytes 1572868
  310.2 1.3 copy-start.15
  311.5 0.8 copy-start.17
  312.3 19.7 %copy-start.26 = (f32[512]{0:T(512)S(1)}, f32[512]{0:T(512)}, u32[]{:S(2)}) copy-start(f32[512]{0:T(512)} %param.13) | copy-start | bytes 6148
  315.5 71.2 %collective-permute-start.20 = (f32[4,512,256]{2,1,0:T(8,128)}, f32[4,512,256]{2,1,0:T(8,128)}, u32[]{:S(2)}, u32[]{:S(2)}) collective-permute-start(f32[4,512,256]{2,1,0:T(8,128)} %get-tuple-element.226.refs_0_), channel_id=1, source_target_pairs={{0,2},{1,3},{2,0},{3,1},{4,6},{5,7},{6,4},{7,5},{8,10},{9,11},{10,... | collective-permute-start | bytes 6291464 | tf_op jit(solution)/shard_map/ppermute | solution.py:484
  317.0 36.4 %collective-permute-start.21 = (f32[512,256]{1,0:T(8,128)}, f32[512,256]{1,0:T(8,128)S(1)}, u32[]{:S(2)}, u32[]{:S(2)}) collective-permute-start(f32[512,256]{1,0:T(8,128)} %get-tuple-element.228), channel_id=1, source_target_pairs={{0,8},{4,12},{8,16},{12,20},{16,24},{20,28},{24,0},{28,4},{1,9},{5... | collective-permute-start | bytes 1572872 | tf_op jit(solution)/shard_map/ppermute | solution.py:466
  328.7 36.8 %collective-permute-start.22 = (f32[512,256]{1,0:T(8,128)}, f32[512,256]{1,0:T(8,128)S(1)}, u32[]{:S(2)}, u32[]{:S(2)}) collective-permute-start(f32[512,256]{1,0:T(8,128)} %get-tuple-element.229), channel_id=1, source_target_pairs={{0,16},{4,20},{8,24},{12,28},{16,0},{20,4},{24,8},{28,12},{1,17},{... | collective-permute-start | bytes 1572872 | tf_op jit(solution)/shard_map/ppermute | solution.py:466
  332.0 33.6 %collective-permute-start.23 = (f32[512,256]{1,0:T(8,128)}, f32[512,256]{1,0:T(8,128)S(1)}, u32[]{:S(2)}, u32[]{:S(2)}) collective-permute-start(f32[512,256]{1,0:T(8,128)} %get-tuple-element.230), channel_id=1, source_target_pairs={{0,24},{4,28},{8,0},{12,4},{16,8},{20,12},{24,16},{28,20},{1,25},{... | collective-permute-start | bytes 1572872 | tf_op jit(solution)/shard_map/ppermute | solution.py:466
  353.4 12.1 %copy-start.4 = (f32[512,256]{1,0:T(8,128)}, f32[512,256]{1,0:T(8,128)S(1)}, u32[]{:S(2)}) copy-start(f32[512,256]{1,0:T(8,128)S(1)} %collective-permute-done.21.refs_1_) | copy-start | bytes 1572868
  365.5 0.8 copy-start.5
  365.6 1.0 copy-start.6
  367.2 20.1 %collective-permute-start.25 = (f32[4,512,256]{2,1,0:T(8,128)}, f32[4,512,256]{2,1,0:T(8,128)S(1)}, u32[]{:S(2)}, u32[]{:S(2)}) collective-permute-start(f32[4,512,256]{2,1,0:T(8,128)} %get-tuple-element.248), channel_id=1, source_target_pairs={{0,1},{1,0},{2,3},{3,2},{4,5},{5,4},{6,7},{7,6},{8,9},{9,8},{10,11... | collective-permute-start | bytes 6291464 | tf_op jit(solution)/shard_map/ppermute | solution.py:489
  367.3 52.9 %collective-permute-start.27 = (f32[512,256]{1,0:T(8,128)}, f32[512,256]{1,0:T(8,128)S(1)}, u32[]{:S(2)}, u32[]{:S(2)}) collective-permute-start(f32[512,256]{1,0:T(8,128)} %get-tuple-element.254), channel_id=1, source_target_pairs={{0,8},{4,12},{8,16},{12,20},{16,24},{20,28},{24,0},{28,4},{1,9},{5... | collective-permute-start | bytes 1572872 | tf_op jit(solution)/shard_map/ppermute | solution.py:466
  378.9 41.4 %collective-permute-start.28 = (f32[512,256]{1,0:T(8,128)}, f32[512,256]{1,0:T(8,128)S(1)}, u32[]{:S(2)}, u32[]{:S(2)}) collective-permute-start(f32[512,256]{1,0:T(8,128)} %get-tuple-element.255), channel_id=1, source_target_pairs={{0,16},{4,20},{8,24},{12,28},{16,0},{20,4},{24,8},{28,12},{1,17},{... | collective-permute-start | bytes 1572872 | tf_op jit(solution)/shard_map/ppermute | solution.py:466
  378.9 41.4 %collective-permute-start.29 = (f32[512,256]{1,0:T(8,128)}, f32[512,256]{1,0:T(8,128)S(1)}, u32[]{:S(2)}, u32[]{:S(2)}) collective-permute-start(f32[512,256]{1,0:T(8,128)} %get-tuple-element.256), channel_id=1, source_target_pairs={{0,24},{4,28},{8,0},{12,4},{16,8},{20,12},{24,16},{28,20},{1,25},{... | collective-permute-start | bytes 1572872 | tf_op jit(solution)/shard_map/ppermute | solution.py:466
  387.3 1.3 copy-start.3
  388.7 6.1 %copy-start.24 = (f32[8,128]{1,0:T(8,128)S(1)}, f32[8,128]{1,0:T(8,128)}, u32[]{:S(2)}) copy-start(f32[8,128]{1,0:T(8,128)} %get-tuple-element.262) | copy-start | bytes 12292
  396.2 37.2 %all-to-all-start.3 = ((f32[32,16,128]{2,1,0:T(8,128)}), f32[32,16,128]{2,1,0:T(8,128)}, u32[]{:S(2)}, u32[]{:S(2)}) async-start(f32[32,16,128]{2,1,0:T(8,128)} %broadcast_in_dim.8), calls=%async_computation.3 | async-start | bytes 524288 | tf_op jit(solution)/shard_map/all_to_all | solution.py:494
  420.3 6.5 %collective-permute-start.26 = (f32[4,512,256]{2,1,0:T(8,128)}, f32[4,512,256]{2,1,0:T(8,128)}, u32[]{:S(2)}, u32[]{:S(2)}) collective-permute-start(f32[4,512,256]{2,1,0:T(8,128)} %get-tuple-element.252), channel_id=1, source_target_pairs={{0,1},{1,0},{2,3},{3,2},{4,5},{5,4},{6,7},{7,6},{8,9},{9,8},{10,11... | collective-permute-start | bytes 6291464 | tf_op jit(solution)/shard_map/ppermute | solution.py:489
  420.3 0.8 copy-start.9
  420.3 1.0 copy-start.10
  420.3 1.1 copy-start.11
  426.7 6.0 %copy-start.25 = (f32[8,128]{1,0:T(8,128)S(1)}, f32[8,128]{1,0:T(8,128)}, u32[]{:S(2)}) copy-start(f32[8,128]{1,0:T(8,128)} %get-tuple-element.260) | copy-start | bytes 12292
  434.1 25.0 %all-to-all-start.2 = ((f32[32,16,128]{2,1,0:T(8,128)}), f32[32,16,128]{2,1,0:T(8,128)S(1)}, u32[]{:S(2)}, u32[]{:S(2)}) async-start(f32[32,16,128]{2,1,0:T(8,128)} %broadcast_in_dim.7), calls=%async_computation.2 | async-start | bytes 524288 | tf_op jit(solution)/shard_map/all_to_all | solution.py:494
  459.1 0.7 copy-start.8
